TPU v7x, 32 devices: a whole 2x2x4 slice. The times are simulated.
32 devices in a mesh: slab: 4 (over y, x), chan: 8 (over z, core).
Axes of the slice: x: 2, y: 2, z: 4, core: 2. Of those that a mesh axis runs over, the one named last changes fastest.
Arguments:
- voltages: bfloat16 [64, 2, 188, 6144], P('chan', None, None, 'slab'), may hold values from -120 to 120
- steering: float32 [64, 2, 64, 188], P('chan'), may hold values from -0.6 to 0.6
- beam_index: int32 [36], replicated, may hold values from 0 to 63
- channel_flags: int32 [64], replicated, may hold values 0 or 1
Outputs:
- beam_output: bfloat16 [64, 2, 36, 6144], P('chan', None, None, 'slab')
All inputs are finite; a program needn't handle non-finite values.
Results may differ from a plain program's by a relative error of at most 0.0065.
Values may be sent and summed in bfloat16 or wider, within the bound.
No kernel may reach another device: no remote copies, remote signals or barrier semaphores. Data moves between devices by JAX's collectives and lax.ppermute only.
A program may use at most 128 MiB of HBM per device.

v0:
```python
import functools

import jax
import jax.numpy as jnp
from jax import lax
from jax.experimental import pallas as pl
from jax.experimental.pallas import tpu as pltpu
from jax.sharding import PartitionSpec as P

HW = 8


LOADING = 0.1

LANES = 128
VMEM_LIMIT = 48 * 1024 * 1024
SQUARINGS = 8


def round_up(value, multiple):
    return -(-value // multiple) * multiple


def dot_nn(left, right):
    return lax.dot_general(
        left, right, (((1,), (0,)), ((), ())), preferred_element_type=jnp.float32
    )


def dot_nt(left, right):
    return lax.dot_general(
        left, right, (((1,), (1,)), ((), ())), preferred_element_type=jnp.float32
    )


def iotas(rows, cols):
    return (
        lax.broadcasted_iota(jnp.int32, (rows, cols), 0),
        lax.broadcasted_iota(jnp.int32, (rows, cols), 1),
    )


def fold(square):
    half = square.shape[0] // 2
    rest = square[:, LANES:]
    return jnp.concatenate(
        [square[:, :LANES], jnp.concatenate([rest[:half], rest[half:]], axis=1)], axis=0
    )


def unfold(folded):
    size = folded.shape[0] * 2 // 3
    width = size - LANES
    rest = jnp.concatenate([folded[size:, :width], folded[size:, width:]], axis=0)
    return jnp.concatenate([folded[:size], rest], axis=1)


def split(x):
    high = x.astype(jnp.bfloat16)
    return high, (x - high.astype(jnp.float32)).astype(jnp.bfloat16)


def covariance_kernel(first_ref, flags_ref, volt_ref, up_ref, down_ref, own_ref, kept):
    step = pl.program_id(0)
    channels, size = kept.shape[0], kept.shape[1] * 2 // 3
    volt = volt_ref[0].astype(jnp.float32)
    blank = jnp.zeros((size - volt.shape[0], volt.shape[2]), jnp.float32)
    v_real = jnp.concatenate([volt[:, 0, :], blank], 0).astype(jnp.bfloat16)
    v_imag = jnp.concatenate([volt[:, 1, :], blank], 0).astype(jnp.bfloat16)
    real_part = dot_nt(v_real, v_real) + dot_nt(v_imag, v_imag)
    cross = dot_nt(v_imag, v_real)
    row, col = iotas(size, size)
    kept[step] = fold(jnp.where(row >= col, real_part, cross - cross.T))

    @pl.when(step == pl.num_programs(0) - 1)
    def _():
        flags = [flags_ref[first_ref[0] + c].astype(jnp.float32) for c in range(channels)]
        for start in range(0, kept.shape[1], 16):
            part = slice(start, start + 16)
            plain = [kept[c, part] for c in range(channels)]
            masked = [plain[c] * flags[c] for c in range(channels)]
            total = masked[0]
            down_ref[0, part] = total.astype(down_ref.dtype)
            for c in range(1, channels):
                total = total + masked[c]
                down_ref[c, part] = total.astype(down_ref.dtype)
            for c in range(channels):
                own_ref[c, part] = total + (1.0 - flags[c]) * plain[c]
            total = masked[-1]
            up_ref[channels - 1, part] = total.astype(up_ref.dtype)
            for c in range(channels - 2, -1, -1):
                total = total + masked[c]
                up_ref[c, part] = total.astype(up_ref.dtype)


def covariances(first, flags, voltages, size):
    channels, _, ports, samples = voltages.shape
    folded = (channels, size + size // 2, LANES)
    whole = pl.BlockSpec(folded, lambda i, *_: (0, 0, 0))
    return pl.pallas_call(
        covariance_kernel,
        grid_spec=pltpu.PrefetchScalarGridSpec(
            num_scalar_prefetch=2,
            grid=(channels,),
            in_specs=[pl.BlockSpec((1, ports, 2, samples), lambda i, *_: (i, 0, 0, 0))],
            out_specs=[whole, whole, whole],
            scratch_shapes=[pltpu.VMEM(folded, jnp.float32)],
        ),
        out_shape=[
            jax.ShapeDtypeStruct(folded, jnp.bfloat16),
            jax.ShapeDtypeStruct(folded, jnp.bfloat16),
            jax.ShapeDtypeStruct(folded, jnp.float32),
        ],
        compiler_params=pltpu.CompilerParams(vmem_limit_bytes=VMEM_LIMIT),
    )(first, flags, jnp.transpose(voltages, (0, 2, 1, 3)))


def window_kernel(slab_ref, own_ref, before_ref, after_ref, mine_ref, *sent_refs):
    share = mine_ref.shape[0]

    def window(slab):
        rows = pl.ds(slab * share, share)
        ends = before_ref[rows].astype(jnp.float32) + after_ref[rows].astype(jnp.float32)
        return own_ref[rows] + ends

    mine_ref[...] = window(slab_ref[0])
    for turn, sent_ref in enumerate(sent_refs, 1):
        sent_ref[...] = window(slab_ref[0] ^ turn).astype(sent_ref.dtype)


def windows(slab, own, before, after, slabs):
    shape = (own.shape[0] // slabs,) + own.shape[1:]
    return pl.pallas_call(
        window_kernel,
        in_specs=[pl.BlockSpec(memory_space=pltpu.SMEM)]
        + [pl.BlockSpec(own.shape, lambda: (0, 0, 0))] * 3,
        out_specs=[pl.BlockSpec(shape, lambda: (0, 0, 0))] * slabs,
        out_shape=[jax.ShapeDtypeStruct(shape, jnp.float32)]
        + [jax.ShapeDtypeStruct(shape, jnp.bfloat16)] * (slabs - 1),
        compiler_params=pltpu.CompilerParams(vmem_limit_bytes=VMEM_LIMIT),
    )(slab, own, before, after)


def choose_kernel(slab_ref, index_ref, steer_ref, out_ref):
    beams, half = index_ref.shape[0], out_ref.shape[1] // 2
    ports = steer_ref.shape[3]
    out_ref[...] = jnp.zeros_like(out_ref)
    for channel in range(out_ref.shape[0]):
        for part in range(2):
            for beam in range(beams):
                row = steer_ref[channel, part, pl.ds(index_ref[beam], 1), :]
                out_ref[channel, pl.ds(part * half + beam, 1), pl.ds(0, ports)] = row


def chosen_vectors(slab, beam_index, steering, share, half, size):
    directions, ports = steering.shape[2:]
    return pl.pallas_call(
        choose_kernel,
        grid_spec=pltpu.PrefetchScalarGridSpec(
            num_scalar_prefetch=2,
            grid=(1,),
            in_specs=[
                pl.BlockSpec((share, 2, directions, ports), lambda i, slab, _: (slab[0], 0, 0, 0))
            ],
            out_specs=pl.BlockSpec((share, 2 * half, size), lambda i, *_: (0, 0, 0)),
        ),
        out_shape=jax.ShapeDtypeStruct((share, 2 * half, size), jnp.float32),
        compiler_params=pltpu.CompilerParams(vmem_limit_bytes=VMEM_LIMIT),
    )(slab, beam_index, steering)


def gains(bound, steps):
    spread, out = (bound - 1.0) / (bound + 1.0), []
    for _ in range(steps):
        centre = spread * spread / 2
        out.append(1.0 / (1.0 - centre))
        spread = centre / (1.0 - centre)
    return out


def solve_kernel(ports, beams, first_ref, flags_ref, *refs):
    own_ref, *got_refs, chosen_ref, weight_ref = refs
    share, half, size = weight_ref.shape[0], chosen_ref.shape[1] // 2, chosen_ref.shape[2]
    bound = ports / LOADING + 1.0
    row, col = iotas(size, size)
    diagonal = row == col
    channels = range(share)
    state = []
    for c in channels:
        folded = own_ref[c]
        for got_ref in got_refs:
            folded = folded + got_ref[c].astype(jnp.float32)
        packed = unfold(folded)
        turned = packed.T
        on_diagonal = jnp.where(diagonal, packed, 0.0)
        trace = jnp.sum(jnp.sum(on_diagonal, axis=0, keepdims=True), axis=1, keepdims=True)
        loading = trace * (LOADING / ports)
        scale = 2.0 / (loading * (1.0 + bound))
        real_part = jnp.where(row >= col, packed, turned)
        real_part = real_part + jnp.where(diagonal & (row < ports), loading, 0.0)
        imag_part = jnp.where(diagonal, 0.0, jnp.where(row < col, packed, -turned))
        state.append((real_part * scale, imag_part * scale, chosen_ref[c] * scale))
    steps = gains(bound, SQUARINGS)
    for number, gain in enumerate(steps):
        squares = number + 1 < len(steps)
        for c in channels:
            real, imag, y = state[c]
            (rh, rl), (ih, il), (yh, yl) = split(real), split(imag), split(y)
            stack = functools.partial(jnp.concatenate, axis=0)
            if squares:
                by_rh = dot_nn(stack([yh, yl, rh, rl]), rh)
                by_rl = dot_nn(stack([yh, rh]), rl)
                by_ih = dot_nn(stack([yh, yl, ih, il, rh, rl]), ih)
                by_il = dot_nn(stack([yh, ih, rh]), il)
            else:
                by_rh, by_rl = dot_nn(stack([yh, yl]), rh), dot_nn(yh, rl)
                by_ih, by_il = dot_nn(stack([yh, yl]), ih), dot_nn(yh, il)
            n = 2 * half
            with_real = by_rh[:n] + by_rh[n : 2 * n] + by_rl[:n]
            with_imag = by_ih[:n] + by_ih[n : 2 * n] + by_il[:n]
            product = stack(
                [with_real[:half] + with_imag[half:], with_real[half:] - with_imag[:half]]
            )
            y = gain * (2.0 * y - product)
            if squares:
                m = size
                rr = by_rh[2 * n : 2 * n + m] + by_rh[2 * n + m :] + by_rl[n:]
                ii = by_ih[2 * n : 2 * n + m] + by_ih[2 * n + m : 2 * n + 2 * m] + by_il[n : n + m]
                ri = by_ih[2 * n + 2 * m : 2 * n + 3 * m] + by_ih[2 * n + 3 * m :] + by_il[n + m :]
                real = gain * (2.0 * real - (rr - ii))
                imag = gain * (2.0 * imag - (ri - ri.T))
            state[c] = real, imag, y
    beam = lax.broadcasted_iota(jnp.int32, (half, 1), 0)
    for c in channels:
        y = state[c][2]
        sums = jnp.sum(y * chosen_ref[c], axis=1, keepdims=True)
        denominator = jnp.where(beam < beams, sums[:half] + sums[half:], 1.0)
        flag = flags_ref[first_ref[0] + c].astype(jnp.float32)
        factor = jnp.where(beam < beams, flag / denominator, 0.0)
        weights = y * jnp.concatenate([factor, factor], axis=0)
        low = weights[:, :LANES]
        high = weights[:, LANES:]
        weight_ref[c, : 2 * half] = low.astype(jnp.bfloat16)
        weight_ref[c, 2 * half :] = jnp.concatenate([high[:half], high[half:]], axis=1).astype(
            jnp.bfloat16
        )


def solved_weights(first, flags, own, got, chosen, ports, beams):
    share, rows, _ = chosen.shape
    smem = pl.BlockSpec(memory_space=pltpu.SMEM)
    whole = [pl.BlockSpec(a.shape, lambda: (0, 0, 0)) for a in (own, *got, chosen)]
    shape = (share, rows + rows // 2, LANES)
    return pl.pallas_call(
        functools.partial(solve_kernel, ports, beams),
        in_specs=[smem, smem] + whole,
        out_specs=pl.BlockSpec(shape, lambda: (0, 0, 0)),
        out_shape=jax.ShapeDtypeStruct(shape, jnp.bfloat16),
        compiler_params=pltpu.CompilerParams(vmem_limit_bytes=VMEM_LIMIT),
    )(first, flags, own, *got, chosen)


def one_hot(rows, cols, hits):
    row, col = iotas(rows, cols)
    table = jnp.zeros((rows, cols), jnp.float32)
    for parity, target, sign in hits:
        hit = (row % 2 == parity) & (col == row // 2 + target)
        table = jnp.where(hit, sign, table)
    return table.astype(jnp.bfloat16)


def beam_kernel(slab_ref, volt_ref, *refs):
    *weight_refs, out_ref = refs
    share, rows, _ = weight_refs[0].shape
    half = rows // 3
    ports, samples = volt_ref.shape[1], volt_ref.shape[3]
    beams = out_ref.shape[1]
    step = pl.program_id(0)
    turn, place = step // share, step % share
    folded = weight_refs[0][place].astype(jnp.float32)
    for number, weight_ref in enumerate(weight_refs[1:], 1):
        folded = jnp.where(turn == number, weight_ref[place].astype(jnp.float32), folded)
    width = (ports - LANES + 63) // 64 * 64
    rest = folded[2 * half :]
    rest = jnp.concatenate([rest[:, :width], rest[:, width : 2 * width]], axis=0)
    weights = jnp.concatenate([folded[: 2 * half], rest], axis=1).astype(jnp.bfloat16)
    size = weights.shape[1]
    to_even = one_hot(2 * beams, 2 * half, [(0, 0, 1.0), (1, half, -1.0)])
    to_odd = one_hot(2 * beams, 2 * half, [(0, half, 1.0), (1, 0, 1.0)])
    even = dot_nn(to_even, weights).astype(jnp.bfloat16)
    odd = dot_nn(to_odd, weights).astype(jnp.bfloat16)
    row, col = iotas(size, 2 * ports)
    spread_even = (col == 2 * row).astype(jnp.float32).astype(jnp.bfloat16)
    spread_odd = (col == 2 * row + 1).astype(jnp.float32).astype(jnp.bfloat16)
    mixed = (dot_nn(even, spread_even) + dot_nn(odd, spread_odd)).astype(jnp.bfloat16)
    formed = dot_nn(mixed, volt_ref[0].reshape(2 * ports, samples))
    out_ref[0] = formed.astype(jnp.bfloat16).reshape(beams, 2, samples)


def formed_beams(slab, voltages, weights, beams):
    channels, _, ports, samples = voltages.shape
    share = weights[0].shape[0]

    def place(i, slab):
        return ((slab[0] ^ (i // share)) * share + i % share, 0, 0, 0)

    out = pl.pallas_call(
        beam_kernel,
        grid_spec=pltpu.PrefetchScalarGridSpec(
            num_scalar_prefetch=1,
            grid=(channels,),
            in_specs=[pl.BlockSpec((1, ports, 2, samples), place)]
            + [pl.BlockSpec(w.shape, lambda i, _: (0, 0, 0)) for w in weights],
            out_specs=pl.BlockSpec((1, beams, 2, samples), place),
        ),
        out_shape=jax.ShapeDtypeStruct((channels, beams, 2, samples), jnp.bfloat16),
        compiler_params=pltpu.CompilerParams(vmem_limit_bytes=VMEM_LIMIT),
    )(slab, jnp.transpose(voltages, (0, 2, 1, 3)), *weights)
    return jnp.transpose(out, (0, 2, 1, 3))


def body(voltages, steering, beam_index, channel_flags):
    channel_count, _, port_count, _ = voltages.shape
    beam_count = beam_index.shape[0]
    slabs, blocks = lax.axis_size("slab"), lax.axis_size("chan")
    if channel_count != HW or slabs & (slabs - 1):
        raise ValueError("unsupported mesh")
    share = channel_count // slabs
    size = round_up(port_count, 64)
    half = round_up(beam_count, 8)
    slab = lax.axis_index("slab").astype(jnp.int32).reshape(1)
    first_channel = (lax.axis_index("chan") * channel_count).astype(jnp.int32).reshape(1)
    chosen = chosen_vectors(slab, beam_index, steering, share, half, size)
    from_here, up_to_here, own = covariances(first_channel, channel_flags, voltages, size)
    upward = [(i, i + 1) for i in range(blocks - 1)]
    before = lax.ppermute(from_here, "chan", upward)
    after = lax.ppermute(up_to_here, "chan", [(j, i) for i, j in upward])
    mine, *sent = windows(slab, own, before, after, slabs)

    def swap(arrays):
        return [
            lax.ppermute(array, "slab", [(i, i ^ turn) for i in range(slabs)])
            for turn, array in enumerate(arrays, 1)
        ]

    got = swap(sent)
    first_share = first_channel + slab * share
    weights = solved_weights(first_share, channel_flags, mine, got, chosen, port_count, beam_count)
    others = swap([weights] * (slabs - 1))
    return formed_beams(slab, voltages, [weights, *others], beam_count)


def solution(mesh):
    return jax.shard_map(
        body,
        mesh=mesh,
        in_specs=(P("chan", None, None, "slab"), P("chan", None, None, None), P(), P()),
        out_specs=P("chan", None, None, "slab"),
        check_vma=False,
    )
```

profile of v0, /device:TPU:16, one launch (start us, length us, event | category | flops | bytes accessed | tf_op | source)
XLA Modules:
  0.0 61.7 jit_solution(6914683970103172047)
XLA Ops:
  0.0 0.0 copy-start.1
  0.0 0.7 %copy-done.1 = s32[64]{0:T(128)S(1)} copy-done((s32[64]{0:T(128)S(1)}, s32[64]{0:T(128)}, u32[]{:S(2)}) %copy-start.1) | copy-done | bytes 280
  0.7 13.0 %shard_map.46 = (bf16[8,288,128]{2,1,0:T(8,128)(2,1)}, bf16[8,288,128]{2,1,0:T(8,128)(2,1)}, f32[8,288,128]{2,1,0:T(8,128)S(1)}) custom-call(s32[1]{0:T(128)} %bitcast.2.first_ref, s32[64]{0:T(128)S(1)} %copy-done.1, bf16[8,188,2,1536]{3,2,1,0:T(2,128)(2,1)} %bitcast.4), custom_call_target="tpu_custom_call" | custom-call | tf_op jit(solution)/shard_map/pallas_call | solution.py:100
  13.6 0.0 copy-start
  13.6 0.0 copy-start.3
  13.6 2.0 %collective-permute-start = (bf16[8,288,128]{2,1,0:T(8,128)(2,1)}, bf16[8,288,128]{2,1,0:T(8,128)(2,1)S(1)}, u32[]{:S(2)}, u32[]{:S(2)}) collective-permute-start(bf16[8,288,128]{2,1,0:T(8,128)(2,1)} %get-tuple-element.13), channel_id=1, source_target_pairs={{0,1},{1,2},{2,3},{3,4},{4,5},{5,6},{6,7},{8,9},{9,10},{10,11},{11... | collective-permute-start | bytes 1769480 | tf_op jit(solution)/shard_map/ppermute | solution.py:336
  15.7 3.6 %collective-permute-start.1 = (bf16[8,288,128]{2,1,0:T(8,128)(2,1)}, bf16[8,288,128]{2,1,0:T(8,128)(2,1)S(1)}, u32[]{:S(2)}, u32[]{:S(2)}) collective-permute-start(bf16[8,288,128]{2,1,0:T(8,128)(2,1)} %get-tuple-element.14), channel_id=1, source_target_pairs={{1,0},{2,1},{3,2},{4,3},{5,4},{6,5},{7,6},{9,8},{10,9},{11,10},{12... | collective-permute-start | bytes 1769480 | tf_op jit(solution)/shard_map/ppermute | solution.py:337
  19.3 5.8 %collective-permute-done.before_ref = bf16[8,288,128]{2,1,0:T(8,128)(2,1)S(1)} collective-permute-done((bf16[8,288,128]{2,1,0:T(8,128)(2,1)}, bf16[8,288,128]{2,1,0:T(8,128)(2,1)S(1)}, u32[]{:S(2)}, u32[]{:S(2)}) %collective-permute-start) | collective-permute-done | bytes 589856 | tf_op jit(solution)/shard_map/ppermute | solution.py:336
  25.2 1.9 %collective-permute-done.1.after_ref = bf16[8,288,128]{2,1,0:T(8,128)(2,1)S(1)} collective-permute-done((bf16[8,288,128]{2,1,0:T(8,128)(2,1)}, bf16[8,288,128]{2,1,0:T(8,128)(2,1)S(1)}, u32[]{:S(2)}, u32[]{:S(2)}) %collective-permute-start.1) | collective-permute-done | bytes 589856 | tf_op jit(solution)/shard_map/ppermute | solution.py:337
  27.0 0.0 copy-start.2
  27.0 0.2 shard_map.47
  27.2 1.6 %collective-permute-start.2 = (bf16[2,288,128]{2,1,0:T(8,128)(2,1)S(1)}, bf16[2,288,128]{2,1,0:T(8,128)(2,1)S(1)}, u32[]{:S(2)}, u32[]{:S(2)}) collective-permute-start(bf16[2,288,128]{2,1,0:T(8,128)(2,1)S(1)} %get-tuple-element.16), channel_id=1, source_target_pairs={{0,8},{8,0},{16,24},{24,16},{1,9},{9,1},{17,25},{25,17},{2,10},{10... | collective-permute-start | bytes 442376 | tf_op jit(solution)/shard_map/ppermute | solution.py:342
  28.8 1.5 %collective-permute-start.3 = (bf16[2,288,128]{2,1,0:T(8,128)(2,1)S(1)}, bf16[2,288,128]{2,1,0:T(8,128)(2,1)S(1)}, u32[]{:S(2)}, u32[]{:S(2)}) collective-permute-start(bf16[2,288,128]{2,1,0:T(8,128)(2,1)S(1)} %get-tuple-element.17), channel_id=1, source_target_pairs={{0,16},{8,24},{16,0},{24,8},{1,17},{9,25},{17,1},{25,9},{2,18},{10... | collective-permute-start | bytes 442376 | tf_op jit(solution)/shard_map/ppermute | solution.py:342
  30.3 0.5 collective-permute-start.4
  30.7 0.0 copy-done
  30.8 0.0 copy-done.3
  30.8 0.7 %shard_map.48.refs_4_ = f32[2,80,192]{2,1,0:T(8,128)S(1)} custom-call(s32[1]{0:T(128)} %bitcast.slab_ref, s32[36]{0:T(128)S(1)} %copy-done.3, f32[8,2,64,188]{3,2,1,0:T(8,128)S(1)} %copy-done), custom_call_target="tpu_custom_call" | custom-call | tf_op jit(solution)/shard_map/pallas_call | solution.py:157
  31.4 1.8 %collective-permute-done.2.refs_1_ = bf16[2,288,128]{2,1,0:T(8,128)(2,1)S(1)} collective-permute-done((bf16[2,288,128]{2,1,0:T(8,128)(2,1)S(1)}, bf16[2,288,128]{2,1,0:T(8,128)(2,1)S(1)}, u32[]{:S(2)}, u32[]{:S(2)}) %collective-permute-start.2) | collective-permute-done | bytes 147488 | tf_op jit(solution)/shard_map/ppermute | solution.py:342
  33.2 5.0 %collective-permute-done.3.refs_2_ = bf16[2,288,128]{2,1,0:T(8,128)(2,1)S(1)} collective-permute-done((bf16[2,288,128]{2,1,0:T(8,128)(2,1)S(1)}, bf16[2,288,128]{2,1,0:T(8,128)(2,1)S(1)}, u32[]{:S(2)}, u32[]{:S(2)}) %collective-permute-start.3) | collective-permute-done | bytes 147488 | tf_op jit(solution)/shard_map/ppermute | solution.py:342
  38.2 0.0 collective-permute-done.4.refs_3_
  38.2 0.0 copy-done.2
  38.2 6.5 %shard_map.49.refs_0_ = bf16[2,120,128]{2,1,0:T(8,128)(2,1)S(1)} custom-call(s32[1]{0:T(128)S(6)} %add.3.first_ref, s32[64]{0:T(128)S(1)} %copy-done.2, f32[2,288,128]{2,1,0:T(8,128)S(1)} %get-tuple-element.15.refs_0_, bf16[2,288,128]{2,1,0:T(8,128)(2,1)S(1)} %collective-permute-done.2.refs_1_, bf16[2,288,128]{2,1,0:T(8,128)(2,1)S(1)} %collective-permute-done.3.refs_2_, ...), custom_call_target="tpu_custom_call" | custom-call | tf_op jit(solution)/shard_map/pallas_call | solution.py:254
  44.8 0.7 %collective-permute-start.5 = (bf16[2,120,128]{2,1,0:T(8,128)(2,1)S(1)}, bf16[2,120,128]{2,1,0:T(8,128)(2,1)S(1)}, u32[]{:S(2)}, u32[]{:S(2)}) collective-permute-start(bf16[2,120,128]{2,1,0:T(8,128)(2,1)S(1)} %shard_map.49.refs_0_), channel_id=1, source_target_pairs={{0,8},{8,0},{16,24},{24,16},{1,9},{9,1},{17,25},{25,17},{2,10},{10... | collective-permute-start | bytes 184328 | tf_op jit(solution)/shard_map/ppermute | solution.py:342
  45.4 1.4 %collective-permute-start.6 = (bf16[2,120,128]{2,1,0:T(8,128)(2,1)S(1)}, bf16[2,120,128]{2,1,0:T(8,128)(2,1)S(1)}, u32[]{:S(2)}, u32[]{:S(2)}) collective-permute-start(bf16[2,120,128]{2,1,0:T(8,128)(2,1)S(1)} %shard_map.49.refs_0_), channel_id=1, source_target_pairs={{0,16},{8,24},{16,0},{24,8},{1,17},{9,25},{17,1},{25,9},{2,18},{10... | collective-permute-start | bytes 184328 | tf_op jit(solution)/shard_map/ppermute | solution.py:342
  46.8 1.4 %collective-permute-start.7 = (bf16[2,120,128]{2,1,0:T(8,128)(2,1)S(1)}, bf16[2,120,128]{2,1,0:T(8,128)(2,1)S(1)}, u32[]{:S(2)}, u32[]{:S(2)}) collective-permute-start(bf16[2,120,128]{2,1,0:T(8,128)(2,1)S(1)} %shard_map.49.refs_0_), channel_id=1, source_target_pairs={{0,24},{8,16},{16,8},{24,0},{1,25},{9,17},{17,9},{25,1},{2,26},{10... | collective-permute-start | bytes 184328 | tf_op jit(solution)/shard_map/ppermute | solution.py:342
  48.3 0.7 %collective-permute-done.5.refs_1_ = bf16[2,120,128]{2,1,0:T(8,128)(2,1)S(1)} collective-permute-done((bf16[2,120,128]{2,1,0:T(8,128)(2,1)S(1)}, bf16[2,120,128]{2,1,0:T(8,128)(2,1)S(1)}, u32[]{:S(2)}, u32[]{:S(2)}) %collective-permute-start.5) | collective-permute-done | bytes 61472 | tf_op jit(solution)/shard_map/ppermute | solution.py:342
  49.0 0.6 %collective-permute-done.6.refs_2_ = bf16[2,120,128]{2,1,0:T(8,128)(2,1)S(1)} collective-permute-done((bf16[2,120,128]{2,1,0:T(8,128)(2,1)S(1)}, bf16[2,120,128]{2,1,0:T(8,128)(2,1)S(1)}, u32[]{:S(2)}, u32[]{:S(2)}) %collective-permute-start.6) | collective-permute-done | bytes 61472 | tf_op jit(solution)/shard_map/ppermute | solution.py:342
  49.6 2.3 %collective-permute-done.7.refs_3_ = bf16[2,120,128]{2,1,0:T(8,128)(2,1)S(1)} collective-permute-done((bf16[2,120,128]{2,1,0:T(8,128)(2,1)S(1)}, bf16[2,120,128]{2,1,0:T(8,128)(2,1)S(1)}, u32[]{:S(2)}, u32[]{:S(2)}) %collective-permute-start.7) | collective-permute-done | bytes 61472 | tf_op jit(solution)/shard_map/ppermute | solution.py:342
  52.0 9.7 %shard_map.50 = bf16[8,36,2,1536]{3,2,1,0:T(2,128)(2,1)} custom-call(s32[1]{0:T(128)} %bitcast.slab_ref, bf16[8,188,2,1536]{3,2,1,0:T(2,128)(2,1)} %bitcast.5, bf16[2,120,128]{2,1,0:T(8,128)(2,1)S(1)} %shard_map.49.refs_0_, bf16[2,120,128]{2,1,0:T(8,128)(2,1)S(1)} %collective-permute-done.5.refs_1_, bf16[2,120,128]{2,1,0:T(8,128)(2,1)S(1)} %collective-permute-done.6.refs_2_, ...), custom_call_target="tpu_custom_call" | custom-call | tf_op jit(solution)/shard_map/pallas_call | solution.py:307
Async XLA Ops:
  0.0 0.7 %copy-start.1 = (s32[64]{0:T(128)S(1)}, s32[64]{0:T(128)}, u32[]{:S(2)}) copy-start(s32[64]{0:T(128)} %flags_ref.3) | copy-start | bytes 772
  13.6 17.1 %copy-start = (f32[8,2,64,188]{3,2,1,0:T(8,128)S(1)}, f32[8,2,64,188]{3,2,1,0:T(8,128)}, u32[]{:S(2)}) copy-start(f32[8,2,64,188]{3,2,1,0:T(8,128)} %steer_ref.1) | copy-start | bytes 2310148
  13.6 17.1 %copy-start.3 = (s32[36]{0:T(128)S(1)}, s32[36]{0:T(128)}, u32[]{:S(2)}) copy-start(s32[36]{0:T(128)} %index_ref.1) | copy-start | bytes 436
  13.6 11.5 %collective-permute-start = (bf16[8,288,128]{2,1,0:T(8,128)(2,1)}, bf16[8,288,128]{2,1,0:T(8,128)(2,1)S(1)}, u32[]{:S(2)}, u32[]{:S(2)}) collective-permute-start(bf16[8,288,128]{2,1,0:T(8,128)(2,1)} %get-tuple-element.13), channel_id=1, source_target_pairs={{0,1},{1,2},{2,3},{3,4},{4,5},{5,6},{6,7},{8,9},{9,10},{10,11},{11... | collective-permute-start | bytes 1769480 | tf_op jit(solution)/shard_map/ppermute | solution.py:336
  15.7 11.3 %collective-permute-start.1 = (bf16[8,288,128]{2,1,0:T(8,128)(2,1)}, bf16[8,288,128]{2,1,0:T(8,128)(2,1)S(1)}, u32[]{:S(2)}, u32[]{:S(2)}) collective-permute-start(bf16[8,288,128]{2,1,0:T(8,128)(2,1)} %get-tuple-element.14), channel_id=1, source_target_pairs={{1,0},{2,1},{3,2},{4,3},{5,4},{6,5},{7,6},{9,8},{10,9},{11,10},{12... | collective-permute-start | bytes 1769480 | tf_op jit(solution)/shard_map/ppermute | solution.py:337
  27.0 11.2 %copy-start.2 = (s32[64]{0:T(128)S(1)}, s32[64]{0:T(128)}, u32[]{:S(2)}) copy-start(s32[64]{0:T(128)} %flags_ref.3) | copy-start | bytes 772
  27.2 6.0 %collective-permute-start.2 = (bf16[2,288,128]{2,1,0:T(8,128)(2,1)S(1)}, bf16[2,288,128]{2,1,0:T(8,128)(2,1)S(1)}, u32[]{:S(2)}, u32[]{:S(2)}) collective-permute-start(bf16[2,288,128]{2,1,0:T(8,128)(2,1)S(1)} %get-tuple-element.16), channel_id=1, source_target_pairs={{0,8},{8,0},{16,24},{24,16},{1,9},{9,1},{17,25},{25,17},{2,10},{10... | collective-permute-start | bytes 442376 | tf_op jit(solution)/shard_map/ppermute | solution.py:342
  28.8 9.5 %collective-permute-start.3 = (bf16[2,288,128]{2,1,0:T(8,128)(2,1)S(1)}, bf16[2,288,128]{2,1,0:T(8,128)(2,1)S(1)}, u32[]{:S(2)}, u32[]{:S(2)}) collective-permute-start(bf16[2,288,128]{2,1,0:T(8,128)(2,1)S(1)} %get-tuple-element.17), channel_id=1, source_target_pairs={{0,16},{8,24},{16,0},{24,8},{1,17},{9,25},{17,1},{25,9},{2,18},{10... | collective-permute-start | bytes 442376 | tf_op jit(solution)/shard_map/ppermute | solution.py:342
  30.3 7.9 %collective-permute-start.4 = (bf16[2,288,128]{2,1,0:T(8,128)(2,1)S(1)}, bf16[2,288,128]{2,1,0:T(8,128)(2,1)S(1)}, u32[]{:S(2)}, u32[]{:S(2)}) collective-permute-start(bf16[2,288,128]{2,1,0:T(8,128)(2,1)S(1)} %get-tuple-element.18), channel_id=1, source_target_pairs={{0,24},{8,16},{16,8},{24,0},{1,25},{9,17},{17,9},{25,1},{2,26},{10... | collective-permute-start | bytes 442376 | tf_op jit(solution)/shard_map/ppermute | solution.py:342
  44.8 4.3 %collective-permute-start.5 = (bf16[2,120,128]{2,1,0:T(8,128)(2,1)S(1)}, bf16[2,120,128]{2,1,0:T(8,128)(2,1)S(1)}, u32[]{:S(2)}, u32[]{:S(2)}) collective-permute-start(bf16[2,120,128]{2,1,0:T(8,128)(2,1)S(1)} %shard_map.49.refs_0_), channel_id=1, source_target_pairs={{0,8},{8,0},{16,24},{24,16},{1,9},{9,1},{17,25},{25,17},{2,10},{10... | collective-permute-start | bytes 184328 | tf_op jit(solution)/shard_map/ppermute | solution.py:342
  45.4 4.2 %collective-permute-start.6 = (bf16[2,120,128]{2,1,0:T(8,128)(2,1)S(1)}, bf16[2,120,128]{2,1,0:T(8,128)(2,1)S(1)}, u32[]{:S(2)}, u32[]{:S(2)}) collective-permute-start(bf16[2,120,128]{2,1,0:T(8,128)(2,1)S(1)} %shard_map.49.refs_0_), channel_id=1, source_target_pairs={{0,16},{8,24},{16,0},{24,8},{1,17},{9,25},{17,1},{25,9},{2,18},{10... | collective-permute-start | bytes 184328 | tf_op jit(solution)/shard_map/ppermute | solution.py:342
  46.8 5.1 %collective-permute-start.7 = (bf16[2,120,128]{2,1,0:T(8,128)(2,1)S(1)}, bf16[2,120,128]{2,1,0:T(8,128)(2,1)S(1)}, u32[]{:S(2)}, u32[]{:S(2)}) collective-permute-start(bf16[2,120,128]{2,1,0:T(8,128)(2,1)S(1)} %shard_map.49.refs_0_), channel_id=1, source_target_pairs={{0,24},{8,16},{16,8},{24,0},{1,25},{9,17},{17,9},{25,1},{2,26},{10... | collective-permute-start | bytes 184328 | tf_op jit(solution)/shard_map/ppermute | solution.py:342
where the time goes:
time: 62.2 us; the launch traced here: 61.7 us
  Pallas kernels  30.1 us (48%)
  waiting for transfers between devices  18.1 us (29%)
  starting transfers between devices  12.8 us (21%)
  local copies, waits for them, and re-layouts  0.67 us (1%)
    pallas_call x1, Pallas kernels, covariances(): pl.pallas_call(covariance_kernel, grid_spec=pltpu.PrefetchScalarGridSpec(...  13 us
    ppermute x6, waiting for transfers between devices, swap(): lax.ppermute(array, 'slab', [(i, i ^ turn) for i in range(slabs)])  10.4 us
    pallas_call x1, Pallas kernels, formed_beams(): pl.pallas_call(beam_kernel, grid_spec=pltpu.PrefetchScalarGridSpec(num_sc...  9.74 us
    ppermute x6, starting transfers between devices, swap(): lax.ppermute(array, 'slab', [(i, i ^ turn) for i in range(slabs)])  7.08 us
    pallas_call x1, Pallas kernels, solved_weights(): pl.pallas_call(functools.partial(solve_kernel, ports, beams), in_specs=[s...  6.55 us
    ppermute x1, waiting for transfers between devices, body(): before = lax.ppermute(from_here, 'chan', upward)  5.83 us
    ppermute x1, starting transfers between devices, body(): after = lax.ppermute(up_to_here, 'chan', [(j, i) for i, j in upward])  3.64 us
    ppermute x1, starting transfers between devices, body(): before = lax.ppermute(from_here, 'chan', upward)  2.04 us
  transfers between devices with their start and end apart: 8, of which 7 were waited for; matrix products, arithmetic and copies ran while one was open for 0% of the time, Pallas kernels for 1%

commit v1 on v0

v1 whole, which is shorter than its diff:
```python
import functools

import jax
import jax.numpy as jnp
from jax import lax
from jax.experimental import pallas as pl
from jax.experimental.pallas import tpu as pltpu
from jax.sharding import PartitionSpec as P

HW = 8


LOADING = 0.1

LANES = 128
VMEM_LIMIT = 24 * 1024 * 1024
SQUARINGS = 8


def round_up(value, multiple):
    return -(-value // multiple) * multiple


def dot_nn(left, right):
    return lax.dot_general(
        left, right, (((1,), (0,)), ((), ())), preferred_element_type=jnp.float32
    )


def dot_nt(left, right):
    return lax.dot_general(
        left, right, (((1,), (1,)), ((), ())), preferred_element_type=jnp.float32
    )


def iotas(rows, cols):
    return (
        lax.broadcasted_iota(jnp.int32, (rows, cols), 0),
        lax.broadcasted_iota(jnp.int32, (rows, cols), 1),
    )


def unfold(folded):
    size = folded.shape[0] * 2 // 3
    width = LANES // 2
    rest = jnp.concatenate([folded[size:, :width], folded[size:, width:]], axis=0)
    return jnp.concatenate([folded[:size], rest], axis=1)


def split(x):
    high = x.astype(jnp.bfloat16)
    return high, (x - high.astype(jnp.float32)).astype(jnp.bfloat16)


def combine(even_rows, odd_rows):
    lane = lax.broadcasted_iota(jnp.int32, even_rows.shape, 1)
    real = even_rows + pltpu.roll(odd_rows, LANES - 1, 1)
    return jnp.where(lane % 2 == 0, real, pltpu.roll(odd_rows, 1, 1) - even_rows)


def gram(volt, left_ref, right_ref):
    lead = left_ref.shape[1] // 2
    rest = volt.shape[0] - lead
    left, right = dot_nt(volt, volt[:lead]), dot_nt(volt[lead:], volt[lead:])
    left_ref[0, : volt.shape[0]] = left[:, :LANES]
    left_ref[1, : volt.shape[0], : lead - LANES] = left[:, LANES:]
    right_ref[0, :rest] = right[:, :LANES]
    right_ref[1, :rest, : rest - LANES] = right[:, LANES:]


def pack(left_ref, right_ref, out_ref):
    half = left_ref.shape[1] // 4

    def rows(ref, lanes, first, parity):
        return ref[lanes, pl.ds(2 * first + parity, half, stride=2), :]

    top = []
    for lanes in range(2):
        row, lane = iotas(half, LANES)
        gap = lane + lanes * LANES - 2 * row
        first = [rows(left_ref, lanes, 0, parity) for parity in range(2)]
        second = [rows(right_ref, lanes, 0, parity) for parity in range(2)]
        even = jnp.where(gap <= 0, first[0], jnp.where(gap == 1, -second[1], second[0]))
        odd = jnp.where(gap == 0, second[0], jnp.where(gap <= 1, first[1], second[1]))
        top.append((even, odd))
    low = [[rows(left_ref, lanes, half, parity) for parity in range(2)] for lanes in range(2)]
    width = LANES // 2
    side = [
        jnp.concatenate([above[:, :width], below[:, :width]], axis=1)
        for above, below in zip(top[1], low[1])
    ]
    for place, pair in enumerate((top[0], low[0], side)):
        out_ref[place * half : (place + 1) * half] = combine(*pair)


def covariance_kernel(
    first_ref, flags_ref, volt_hbm, across_ref, inside_ref, own_ref, volts, lefts, rights, kept, sems
):
    channels, ports, _, samples = volts.shape
    copies = [
        pltpu.make_async_copy(volt_hbm.at[c], volts.at[c], sems.at[c]) for c in range(channels)
    ]
    groups = [range(c, c + 2) for c in range(0, channels, 2)]
    for group in groups[:2]:
        for c in group:
            copies[c].start()
    lefts[...] = jnp.zeros_like(lefts)
    rights[...] = jnp.zeros_like(rights)
    for number, group in enumerate(groups):
        for c in group:
            copies[c].wait()
        for later in groups[number + 2 : number + 3]:
            for c in later:
                copies[c].start()
        for c in group:
            gram(volts[c].reshape(2 * ports, samples), lefts.at[c], rights.at[c])
        for c in groups[number - 1] if number else ():
            pack(lefts.at[c], rights.at[c], kept.at[c])
    for c in groups[-1]:
        pack(lefts.at[c], rights.at[c], kept.at[c])
    flags = [flags_ref[first_ref[0] + c].astype(jnp.float32) for c in range(channels)]
    odd_block = (first_ref[0] // channels) % 2 == 1
    for start in range(0, kept.shape[1], 16):
        part = slice(start, start + 16)
        plain = [kept[c, part] for c in range(channels)]
        masked = [plain[c] * flags[c] for c in range(channels)]
        up_to, onward = [masked[0]], [masked[-1]]
        for c in range(1, channels):
            up_to.append(up_to[-1] + masked[c])
            onward.append(onward[-1] + masked[channels - 1 - c])
        for c in range(channels):
            up, down = onward[channels - 1 - c], up_to[c]
            across_ref[c, part] = jnp.where(odd_block, up, down).astype(across_ref.dtype)
            inside_ref[c, part] = jnp.where(odd_block, down, up).astype(inside_ref.dtype)
            own_ref[c, part] = up_to[-1] + (1.0 - flags[c]) * plain[c]


def covariances(first, flags, voltages, size):
    channels, _, ports, samples = voltages.shape
    folded = (channels, size + size // 2, LANES)
    smem = pl.BlockSpec(memory_space=pltpu.SMEM)
    vmem = pl.BlockSpec(memory_space=pltpu.VMEM)
    return pl.pallas_call(
        covariance_kernel,
        in_specs=[smem, smem, pl.BlockSpec(memory_space=pltpu.HBM)],
        out_specs=[vmem] * 3,
        scratch_shapes=[
            pltpu.VMEM((channels, ports, 2, samples), voltages.dtype),
            pltpu.VMEM((channels, 2, 2 * size, LANES), jnp.float32),
            pltpu.VMEM((channels, 2, size, LANES), jnp.float32),
            pltpu.VMEM(folded, jnp.float32),
            pltpu.SemaphoreType.DMA((channels,)),
        ],
        out_shape=[
            jax.ShapeDtypeStruct(folded, jnp.bfloat16),
            jax.ShapeDtypeStruct(folded, jnp.bfloat16),
            jax.ShapeDtypeStruct(folded, jnp.float32),
        ],
        compiler_params=pltpu.CompilerParams(vmem_limit_bytes=56 * 1024 * 1024),
    )(first, flags, jnp.transpose(voltages, (0, 2, 1, 3)))


def window_kernel(slab_ref, own_ref, inside_ref, across_ref, mine_ref, *sent_refs):
    share = mine_ref.shape[0]

    def window(slab):
        rows = pl.ds(slab * share, share)
        ends = inside_ref[rows].astype(jnp.float32) + across_ref[rows].astype(jnp.float32)
        return own_ref[rows] + ends

    mine_ref[...] = window(slab_ref[0])
    for turn, sent_ref in enumerate(sent_refs, 1):
        sent_ref[...] = window(slab_ref[0] ^ turn).astype(sent_ref.dtype)


def windows(slab, own, inside, across, slabs):
    shape = (own.shape[0] // slabs,) + own.shape[1:]
    return pl.pallas_call(
        window_kernel,
        in_specs=[pl.BlockSpec(memory_space=pltpu.SMEM)]
        + [pl.BlockSpec(own.shape, lambda: (0, 0, 0))] * 3,
        out_specs=[pl.BlockSpec(shape, lambda: (0, 0, 0))] * slabs,
        out_shape=[jax.ShapeDtypeStruct(shape, jnp.float32)]
        + [jax.ShapeDtypeStruct(shape, jnp.bfloat16)] * (slabs - 1),
        compiler_params=pltpu.CompilerParams(vmem_limit_bytes=VMEM_LIMIT),
    )(slab, own, inside, across)


def choose_kernel(slab_ref, index_ref, steer_ref, out_ref):
    beams, half = index_ref.shape[0], out_ref.shape[1] // 2
    ports = steer_ref.shape[3]
    out_ref[...] = jnp.zeros_like(out_ref)
    for channel in range(out_ref.shape[0]):
        for part in range(2):
            for beam in range(beams):
                row = steer_ref[channel, part, pl.ds(index_ref[beam], 1), :]
                out_ref[channel, pl.ds(part * half + beam, 1), pl.ds(0, ports)] = row


def chosen_vectors(slab, beam_index, steering, share, half, size):
    directions, ports = steering.shape[2:]
    return pl.pallas_call(
        choose_kernel,
        grid_spec=pltpu.PrefetchScalarGridSpec(
            num_scalar_prefetch=2,
            grid=(1,),
            in_specs=[
                pl.BlockSpec((share, 2, directions, ports), lambda i, slab, _: (slab[0], 0, 0, 0))
            ],
            out_specs=pl.BlockSpec((share, 2 * half, size), lambda i, *_: (0, 0, 0)),
        ),
        out_shape=jax.ShapeDtypeStruct((share, 2 * half, size), jnp.float32),
        compiler_params=pltpu.CompilerParams(vmem_limit_bytes=VMEM_LIMIT),
    )(slab, beam_index, steering)


def unpack(folded):
    packed = unfold(folded)
    size = packed.shape[0]
    half = size // 2
    row, col = iotas(size, 2 * LANES)
    spread = (row == jnp.where(col < LANES, 2 * col, 2 * (col - LANES) + 1)) & (col % LANES < half)
    spread = spread.astype(jnp.float32).astype(jnp.bfloat16)
    high, rest = split(packed)
    lowest = packed - high.astype(jnp.float32) - rest.astype(jnp.float32)
    parts = dot_nn(jnp.concatenate([high, rest, lowest.astype(jnp.bfloat16)], axis=0), spread)
    parts = parts[:size] + (parts[size : 2 * size] + parts[2 * size :])
    real, imag = parts[:, :half], parts[:, LANES : LANES + half]
    row, col = iotas(half, half)
    turned_real, turned_imag = real[:half].T, imag[:half].T
    first_real = jnp.where(row >= col, real[:half], turned_real)
    first_imag = jnp.where(row > col, imag[:half], jnp.where(row < col, -turned_imag, 0.0))
    second_real = jnp.where(row < col, real[:half], jnp.where(row > col, turned_real, imag[:half]))
    second_imag = jnp.where(row < col, imag[:half], jnp.where(row > col, -turned_imag, 0.0))

    def blocks(first, second, low, high):
        return jnp.concatenate(
            [jnp.concatenate([first, high], axis=1), jnp.concatenate([low, second], axis=1)], axis=0
        )

    low_real, low_imag = real[half:], imag[half:]
    return (
        blocks(first_real, second_real, low_real, low_real.T),
        blocks(first_imag, second_imag, low_imag, -low_imag.T),
    )


def gains(bound, steps):
    spread, out = (bound - 1.0) / (bound + 1.0), []
    for _ in range(steps):
        centre = spread * spread / 2
        out.append((spread, 1.0 / (1.0 - centre)))
        spread = centre / (1.0 - centre)
    return out


def stack(*arrays):
    return jnp.concatenate(arrays, axis=0)


def apply(y, real, imag, passes):
    n = y.shape[0]
    half = n // 2
    if passes == 1:
        with_real = dot_nn(y.astype(jnp.bfloat16), real.astype(jnp.bfloat16))
        with_imag = dot_nn(y.astype(jnp.bfloat16), imag.astype(jnp.bfloat16))
    else:
        (rh, rl), (ih, il), (yh, yl) = split(real), split(imag), split(y)
        by_rh, by_ih = dot_nn(stack(yh, yl), rh), dot_nn(stack(yh, yl), ih)
        with_real = by_rh[:n] + by_rh[n:] + dot_nn(yh, rl)
        with_imag = by_ih[:n] + by_ih[n:] + dot_nn(yh, il)
    return stack(with_real[:half] + with_imag[half:], with_real[half:] - with_imag[:half])


def square(real, imag, passes):
    n = real.shape[0]
    if passes == 1:
        rh, ih = real.astype(jnp.bfloat16), imag.astype(jnp.bfloat16)
        by_ih = dot_nn(stack(ih, rh), ih)
        rr, ii, ri = dot_nn(rh, rh), by_ih[:n], by_ih[n:]
    else:
        (rh, rl), (ih, il) = split(real), split(imag)
        by_rh, by_rl = dot_nn(stack(rh, rl), rh), dot_nn(rh, rl)
        by_ih, by_il = dot_nn(stack(ih, il, rh, rl), ih), dot_nn(stack(ih, rh), il)
        rr = by_rh[:n] + by_rh[n:] + by_rl
        ii = by_ih[:n] + by_ih[n : 2 * n] + by_il[:n]
        ri = by_ih[2 * n : 3 * n] + by_ih[3 * n :] + by_il[n:]
    return rr - ii, ri - ri.T


def solve_kernel(ports, beams, first_ref, flags_ref, *refs):
    own_ref, *got_refs, chosen_ref, weight_ref = refs
    share, half, size = weight_ref.shape[0], chosen_ref.shape[1] // 2, chosen_ref.shape[2]
    bound = ports / LOADING + 1.0
    row, col = iotas(size, size)
    identity = jnp.where(row == col, 1.0, 0.0)
    channels = range(share)
    state = []
    for c in channels:
        folded = own_ref[c]
        for got_ref in got_refs:
            folded = folded + got_ref[c].astype(jnp.float32)
        real, imag = unpack(folded)
        trace = jnp.sum(jnp.sum(real * identity, axis=0, keepdims=True), axis=1, keepdims=True)
        loading = trace * (LOADING / ports)
        scale = 2.0 / (loading * (1.0 + bound))
        real = real + jnp.where((row == col) & (row < ports), loading, 0.0)
        state.append((real * scale, imag * scale, chosen_ref[c] * scale))
    steps = gains(bound, SQUARINGS)
    for number, (spread, gain) in enumerate(steps):
        squares = number + 1 < len(steps)
        for c in channels:
            real, imag, y = state[c]
            if number == len(steps) - 2:
                real, imag = identity - real, -imag
            if number < len(steps) - 2:
                new_y = gain * (2.0 * y - apply(y, real, imag, 3))
                real2, imag2 = square(real, imag, 3)
                real, imag = gain * (2.0 * real - real2), gain * (2.0 * imag - imag2)
            else:
                new_y = gain * (y + apply(y, real, imag, 3 if squares else 1))
                if squares:
                    real, imag = square(real, imag, 1)
                    real = gain * (real - identity * (spread * spread / 2))
                    imag = gain * imag
            state[c] = real, imag, new_y
    beam = lax.broadcasted_iota(jnp.int32, (half, 1), 0)
    row, col = iotas(2 * half, 2 * half)
    place = jnp.where(row % 2 == 0, row // 2, row // 2 + half)
    order = jnp.where(col == place, jnp.where(row % 2 == 0, 1.0, -1.0), 0.0).astype(jnp.bfloat16)
    for c in channels:
        y = state[c][2]
        sums = jnp.sum(y * chosen_ref[c], axis=1, keepdims=True)
        denominator = jnp.where(beam < beams, sums[:half] + sums[half:], 1.0)
        flag = flags_ref[first_ref[0] + c].astype(jnp.float32)
        factor = jnp.where(beam < beams, flag / denominator, 0.0)
        weights = dot_nn(order, (y * stack(factor, factor)).astype(jnp.bfloat16))
        high = weights[:, LANES:]
        weight_ref[c, : 2 * half] = weights[:, :LANES].astype(jnp.bfloat16)
        weight_ref[c, 2 * half :] = jnp.concatenate([high[:half], high[half:]], axis=1).astype(
            jnp.bfloat16
        )


def solved_weights(first, flags, own, got, chosen, ports, beams):
    share, rows, _ = chosen.shape
    smem = pl.BlockSpec(memory_space=pltpu.SMEM)
    whole = [pl.BlockSpec(a.shape, lambda: (0, 0, 0)) for a in (own, *got, chosen)]
    shape = (share, rows + rows // 2, LANES)
    return pl.pallas_call(
        functools.partial(solve_kernel, ports, beams),
        in_specs=[smem, smem] + whole,
        out_specs=pl.BlockSpec(shape, lambda: (0, 0, 0)),
        out_shape=jax.ShapeDtypeStruct(shape, jnp.bfloat16),
        compiler_params=pltpu.CompilerParams(vmem_limit_bytes=VMEM_LIMIT),
    )(first, flags, own, *got, chosen)


def beam_kernel(slab_ref, volt_ref, *refs):
    *weight_refs, out_ref, mixed = refs
    share, rows, _ = weight_refs[0].shape
    rows = rows * 2 // 3
    _, ports, _, samples = volt_ref.shape
    together, beams = out_ref.shape[:2]
    step = pl.program_id(0)

    @pl.when(step == 0)
    def _():
        folded = [ref[c].astype(jnp.float32) for ref in weight_refs for c in range(share)]
        real_rows = stack(*[unfold(f) for f in folded])
        count, size = real_rows.shape
        row, _ = iotas(count, size)
        below, above = pltpu.roll(real_rows, count - 1, 0), pltpu.roll(real_rows, 1, 0)
        imag_rows = jnp.where(row % 2 == 0, -below, above)
        row, col = iotas(size, 2 * ports)
        to_even = (col == 2 * row).astype(jnp.float32).astype(jnp.bfloat16)
        to_odd = (col == 2 * row + 1).astype(jnp.float32).astype(jnp.bfloat16)
        placed = dot_nn(real_rows.astype(jnp.bfloat16), to_even)
        placed = (placed + dot_nn(imag_rows.astype(jnp.bfloat16), to_odd)).astype(jnp.bfloat16)
        for turn in range(len(weight_refs)):
            first = (slab_ref[0] ^ turn) * share
            for c in range(share):
                at = (turn * share + c) * rows
                mixed[first + c] = placed[at : at + rows]

    for c in range(together):
        channel = step * together + c
        formed = dot_nn(mixed[channel], volt_ref[channel].reshape(2 * ports, samples))
        out_ref[c] = formed[: 2 * beams].astype(jnp.bfloat16).reshape(beams, 2, samples)


def formed_beams(slab, voltages, weights, beams):
    channels, _, ports, samples = voltages.shape
    rows = weights[0].shape[1] * 2 // 3
    together = 2
    whole = pl.BlockSpec(weights[0].shape, lambda i: (0, 0, 0))
    out = pl.pallas_call(
        beam_kernel,
        grid=(channels // together,),
        in_specs=[pl.BlockSpec(memory_space=pltpu.SMEM), pl.BlockSpec(memory_space=pltpu.VMEM)]
        + [whole] * len(weights),
        out_specs=pl.BlockSpec((together, beams, 2, samples), lambda i: (i, 0, 0, 0)),
        scratch_shapes=[pltpu.VMEM((channels, rows, 2 * ports), jnp.bfloat16)],
        out_shape=jax.ShapeDtypeStruct((channels, beams, 2, samples), jnp.bfloat16),
        compiler_params=pltpu.CompilerParams(vmem_limit_bytes=VMEM_LIMIT),
    )(slab, jnp.transpose(voltages, (0, 2, 1, 3)), *weights)
    return jnp.transpose(out, (0, 2, 1, 3))


def body(voltages, steering, beam_index, channel_flags):
    channel_count, _, port_count, _ = voltages.shape
    beam_count = beam_index.shape[0]
    slabs, blocks = lax.axis_size("slab"), lax.axis_size("chan")
    if channel_count != HW or slabs & (slabs - 1) or not LANES < port_count <= LANES * 3 // 2:
        raise ValueError("unsupported mesh")
    share = channel_count // slabs
    size = LANES + LANES // 2
    half = round_up(beam_count, 8)
    slab = lax.axis_index("slab").astype(jnp.int32).reshape(1)
    first_channel = (lax.axis_index("chan") * channel_count).astype(jnp.int32).reshape(1)
    chosen = chosen_vectors(slab, beam_index, steering, share, half, size)
    across, inside, own = covariances(first_channel, channel_flags, voltages, size)
    pairs = [[(i, i + 1) for i in range(start, blocks - 1, 2)] for start in range(2)]
    inside_pairs, across_pairs = [ahead + [(j, i) for i, j in ahead] for ahead in pairs]
    across = lax.ppermute(across, "chan", across_pairs)
    inside = lax.ppermute(inside, "chan", inside_pairs)
    mine, *sent = windows(slab, own, inside, across, slabs)

    def swap(arrays):
        return [
            lax.ppermute(array, "slab", [(i, i ^ turn) for i in range(slabs)])
            for turn, array in enumerate(arrays, 1)
        ]

    got = swap(sent)
    first_share = first_channel + slab * share
    weights = solved_weights(first_share, channel_flags, mine, got, chosen, port_count, beam_count)
    others = swap([weights] * (slabs - 1))
    return formed_beams(slab, voltages, [weights, *others], beam_count)


def solution(mesh):
    return jax.shard_map(
        body,
        mesh=mesh,
        in_specs=(P("chan", None, None, "slab"), P("chan", None, None, None), P(), P()),
        out_specs=P("chan", None, None, "slab"),
        check_vma=False,
    )
```

time: 62.2 us -> 54.2 us (0.87)
  Pallas kernels: 30.1 us -> 20.4 us
  local copies, waits for them, and re-layouts: 0.67 us -> 4.91 us
  starting transfers between devices: 12.8 us -> 9.77 us
  waiting for transfers between devices: 18.1 us -> 18.9 us
    pallas_call x2, Pallas kernels: 22.7 us -> 12.9 us  [the longest x1 8.83 us: covariances(): pl.pallas_call(covariance_kernel, in_specs=[smem, smem, pl.BlockSpec(memo...]
    unnamed x8 -> x10, local copies, waits for them, and re-layouts: 0.67 us -> 4.91 us
    ppermute x2, starting transfers between devices: 5.68 us -> 2.7 us  [the longest x1 2.63 us: body(): across = lax.ppermute(across, 'chan', across_pairs)]
    ppermute x2, waiting for transfers between devices: 7.69 us -> 8.76 us  [the longest x1 8.76 us: body(): across = lax.ppermute(across, 'chan', across_pairs)]
  transfers between devices with their start and end apart: 8 -> 8, of which waited for: 7 -> 6; matrix products, arithmetic and copies ran while one was open for 0% -> 0% of each run, Pallas kernels for 1% -> 1%
where the time goes in v1:
time: 54.2 us; the launch traced here: 54 us
  Pallas kernels  20.4 us (38%)
  waiting for transfers between devices  18.9 us (35%)
  starting transfers between devices  9.77 us (18%)
  local copies, waits for them, and re-layouts  4.91 us (9%)
    ppermute x6, waiting for transfers between devices, swap(): lax.ppermute(array, 'slab', [(i, i ^ turn) for i in range(slabs)])  10.1 us
    pallas_call x1, Pallas kernels, covariances(): pl.pallas_call(covariance_kernel, in_specs=[smem, smem, pl.BlockSpec(memo...  8.83 us
    ppermute x1, waiting for transfers between devices, body(): across = lax.ppermute(across, 'chan', across_pairs)  8.76 us
    ppermute x6, starting transfers between devices, swap(): lax.ppermute(array, 'slab', [(i, i ^ turn) for i in range(slabs)])  7.07 us
    pallas_call x1, Pallas kernels, solved_weights(): pl.pallas_call(functools.partial(solve_kernel, ports, beams), in_specs=[s...  6.64 us
    unnamed x10, local copies, waits for them, and re-layouts  4.91 us
    pallas_call x1, Pallas kernels, formed_beams(): pl.pallas_call(beam_kernel, grid=(channels // together,), in_specs=[pl.Bl...  4.05 us
    ppermute x1, starting transfers between devices, body(): across = lax.ppermute(across, 'chan', across_pairs)  2.63 us
  transfers between devices with their start and end apart: 8, of which 6 were waited for; matrix products, arithmetic and copies ran while one was open for 0% of the time, Pallas kernels for 1%

profile of v1, /device:TPU:16, one launch (start us, length us, event | category | flops | bytes accessed | tf_op | source)
XLA Modules:
  0.0 54.0 jit_solution(17404248178930177193)
XLA Ops:
  0.0 0.0 copy-start.2
  0.0 8.8 %shard_map.46 = (bf16[8,288,128]{2,1,0:T(8,128)(2,1)}, bf16[8,288,128]{2,1,0:T(8,128)(2,1)}, f32[8,288,128]{2,1,0:T(8,128)}) custom-call(s32[1]{0:T(128)} %bitcast.2.first_ref, s32[64]{0:T(128)} %flags_ref.3, bf16[8,188,2,1536]{3,2,1,0:T(2,128)(2,1)} %bitcast.4), custom_call_target="tpu_custom_call" | custom-call | tf_op jit(solution)/shard_map/pallas_call | solution.py:143
  8.8 0.0 copy-start.4
  8.8 0.1 collective-permute-start
  8.9 2.6 %collective-permute-start.1 = (bf16[8,288,128]{2,1,0:T(8,128)(2,1)}, bf16[8,288,128]{2,1,0:T(8,128)(2,1)S(1)}, u32[]{:S(2)}, u32[]{:S(2)}) collective-permute-start(bf16[8,288,128]{2,1,0:T(8,128)(2,1)} %get-tuple-element.14), channel_id=1, source_target_pairs={{1,2},{3,4},{5,6},{2,1},{4,3},{6,5},{9,10},{11,12},{13,14},{10,9},... | collective-permute-start | bytes 1769480 | tf_op jit(solution)/shard_map/ppermute | solution.py:425
  11.6 0.0 collective-permute-done.inside_ref
  11.6 8.8 %collective-permute-done.1.across_ref = bf16[8,288,128]{2,1,0:T(8,128)(2,1)S(1)} collective-permute-done((bf16[8,288,128]{2,1,0:T(8,128)(2,1)}, bf16[8,288,128]{2,1,0:T(8,128)(2,1)S(1)}, u32[]{:S(2)}, u32[]{:S(2)}) %collective-permute-start.1) | collective-permute-done | bytes 589856 | tf_op jit(solution)/shard_map/ppermute | solution.py:425
  20.3 0.0 copy-start.1
  20.3 1.3 %copy-done.1 = f32[8,288,128]{2,1,0:T(8,128)S(1)} copy-done((f32[8,288,128]{2,1,0:T(8,128)S(1)}, f32[8,288,128]{2,1,0:T(8,128)}, u32[]{:S(2)}) %copy-start.1) | copy-done | bytes 1179672
  21.6 0.0 copy-start.3
  21.6 0.2 shard_map.47
  21.8 1.6 %collective-permute-start.2 = (bf16[2,288,128]{2,1,0:T(8,128)(2,1)S(1)}, bf16[2,288,128]{2,1,0:T(8,128)(2,1)S(1)}, u32[]{:S(2)}, u32[]{:S(2)}) collective-permute-start(bf16[2,288,128]{2,1,0:T(8,128)(2,1)S(1)} %get-tuple-element.16), channel_id=1, source_target_pairs={{0,8},{8,0},{16,24},{24,16},{1,9},{9,1},{17,25},{25,17},{2,10},{10... | collective-permute-start | bytes 442376 | tf_op jit(solution)/shard_map/ppermute | solution.py:431
  23.3 1.5 %collective-permute-start.3 = (bf16[2,288,128]{2,1,0:T(8,128)(2,1)S(1)}, bf16[2,288,128]{2,1,0:T(8,128)(2,1)S(1)}, u32[]{:S(2)}, u32[]{:S(2)}) collective-permute-start(bf16[2,288,128]{2,1,0:T(8,128)(2,1)S(1)} %get-tuple-element.17), channel_id=1, source_target_pairs={{0,16},{8,24},{16,0},{24,8},{1,17},{9,25},{17,1},{25,9},{2,18},{10... | collective-permute-start | bytes 442376 | tf_op jit(solution)/shard_map/ppermute | solution.py:431
  24.9 0.5 collective-permute-start.4
  25.3 0.0 copy-done.2
  25.3 0.0 copy-done.4
  25.3 0.7 %shard_map.48.refs_4_ = f32[2,80,192]{2,1,0:T(8,128)S(1)} custom-call(s32[1]{0:T(128)} %bitcast.slab_ref, s32[36]{0:T(128)S(1)} %copy-done.4, f32[8,2,64,188]{3,2,1,0:T(8,128)S(1)} %copy-done.2), custom_call_target="tpu_custom_call" | custom-call | tf_op jit(solution)/shard_map/pallas_call | solution.py:202
  26.0 2.5 %collective-permute-done.2.refs_1_ = bf16[2,288,128]{2,1,0:T(8,128)(2,1)S(1)} collective-permute-done((bf16[2,288,128]{2,1,0:T(8,128)(2,1)S(1)}, bf16[2,288,128]{2,1,0:T(8,128)(2,1)S(1)}, u32[]{:S(2)}, u32[]{:S(2)}) %collective-permute-start.2) | collective-permute-done | bytes 147488 | tf_op jit(solution)/shard_map/ppermute | solution.py:431
  28.5 4.0 %collective-permute-done.3.refs_2_ = bf16[2,288,128]{2,1,0:T(8,128)(2,1)S(1)} collective-permute-done((bf16[2,288,128]{2,1,0:T(8,128)(2,1)S(1)}, bf16[2,288,128]{2,1,0:T(8,128)(2,1)S(1)}, u32[]{:S(2)}, u32[]{:S(2)}) %collective-permute-start.3) | collective-permute-done | bytes 147488 | tf_op jit(solution)/shard_map/ppermute | solution.py:431
  32.5 0.0 collective-permute-done.4.refs_3_
  32.5 0.0 copy-done.3
  32.5 6.6 %shard_map.49.refs_0_ = bf16[2,120,128]{2,1,0:T(8,128)(2,1)S(1)} custom-call(s32[1]{0:T(128)S(6)} %add.3.first_ref, s32[64]{0:T(128)S(1)} %copy-done.3, f32[2,288,128]{2,1,0:T(8,128)S(1)} %get-tuple-element.15.refs_0_, bf16[2,288,128]{2,1,0:T(8,128)(2,1)S(1)} %collective-permute-done.2.refs_1_, bf16[2,288,128]{2,1,0:T(8,128)(2,1)S(1)} %collective-permute-done.3.refs_2_, ...), custom_call_target="tpu_custom_call" | custom-call | tf_op jit(solution)/shard_map/pallas_call | solution.py:350
  39.1 1.3 %collective-permute-start.5 = (bf16[2,120,128]{2,1,0:T(8,128)(2,1)S(1)}, bf16[2,120,128]{2,1,0:T(8,128)(2,1)S(1)}, u32[]{:S(2)}, u32[]{:S(2)}) collective-permute-start(bf16[2,120,128]{2,1,0:T(8,128)(2,1)S(1)} %shard_map.49.refs_0_), channel_id=1, source_target_pairs={{0,8},{8,0},{16,24},{24,16},{1,9},{9,1},{17,25},{25,17},{2,10},{10... | collective-permute-start | bytes 184328 | tf_op jit(solution)/shard_map/ppermute | solution.py:431
  40.4 0.8 %collective-permute-start.6 = (bf16[2,120,128]{2,1,0:T(8,128)(2,1)S(1)}, bf16[2,120,128]{2,1,0:T(8,128)(2,1)S(1)}, u32[]{:S(2)}, u32[]{:S(2)}) collective-permute-start(bf16[2,120,128]{2,1,0:T(8,128)(2,1)S(1)} %shard_map.49.refs_0_), channel_id=1, source_target_pairs={{0,16},{8,24},{16,0},{24,8},{1,17},{9,25},{17,1},{25,9},{2,18},{10... | collective-permute-start | bytes 184328 | tf_op jit(solution)/shard_map/ppermute | solution.py:431
  41.2 1.4 %collective-permute-start.7 = (bf16[2,120,128]{2,1,0:T(8,128)(2,1)S(1)}, bf16[2,120,128]{2,1,0:T(8,128)(2,1)S(1)}, u32[]{:S(2)}, u32[]{:S(2)}) collective-permute-start(bf16[2,120,128]{2,1,0:T(8,128)(2,1)S(1)} %shard_map.49.refs_0_), channel_id=1, source_target_pairs={{0,24},{8,16},{16,8},{24,0},{1,25},{9,17},{17,9},{25,1},{2,26},{10... | collective-permute-start | bytes 184328 | tf_op jit(solution)/shard_map/ppermute | solution.py:431
  42.6 0.7 %collective-permute-done.5.refs_1_ = bf16[2,120,128]{2,1,0:T(8,128)(2,1)S(1)} collective-permute-done((bf16[2,120,128]{2,1,0:T(8,128)(2,1)S(1)}, bf16[2,120,128]{2,1,0:T(8,128)(2,1)S(1)}, u32[]{:S(2)}, u32[]{:S(2)}) %collective-permute-start.5) | collective-permute-done | bytes 61472 | tf_op jit(solution)/shard_map/ppermute | solution.py:431
  43.4 1.7 %collective-permute-done.6.refs_2_ = bf16[2,120,128]{2,1,0:T(8,128)(2,1)S(1)} collective-permute-done((bf16[2,120,128]{2,1,0:T(8,128)(2,1)S(1)}, bf16[2,120,128]{2,1,0:T(8,128)(2,1)S(1)}, u32[]{:S(2)}, u32[]{:S(2)}) %collective-permute-start.6) | collective-permute-done | bytes 61472 | tf_op jit(solution)/shard_map/ppermute | solution.py:431
  45.0 1.3 %collective-permute-done.7.refs_3_ = bf16[2,120,128]{2,1,0:T(8,128)(2,1)S(1)} collective-permute-done((bf16[2,120,128]{2,1,0:T(8,128)(2,1)S(1)}, bf16[2,120,128]{2,1,0:T(8,128)(2,1)S(1)}, u32[]{:S(2)}, u32[]{:S(2)}) %collective-permute-start.7) | collective-permute-done | bytes 61472 | tf_op jit(solution)/shard_map/ppermute | solution.py:431
  46.3 0.0 copy-start
  46.3 3.6 %copy-done = bf16[8,2,188,1536]{3,1,2,0:T(2,128)(2,1)S(1)} copy-done((bf16[8,2,188,1536]{3,1,2,0:T(2,128)(2,1)S(1)}, bf16[8,2,188,1536]{3,1,2,0:T(2,128)(2,1)}, u32[]{:S(2)}) %copy-start) | copy-done | bytes 9240600
  49.9 4.0 %shard_map.50 = bf16[8,36,2,1536]{3,2,1,0:T(2,128)(2,1)} custom-call(s32[1]{0:T(128)} %bitcast.slab_ref, bf16[8,188,2,1536]{3,2,1,0:T(2,128)(2,1)S(1)} %bitcast.5, bf16[2,120,128]{2,1,0:T(8,128)(2,1)S(1)} %shard_map.49.refs_0_, bf16[2,120,128]{2,1,0:T(8,128)(2,1)S(1)} %collective-permute-done.5.refs_1_, ...), custom_call_target="tpu_custom_call" | custom-call | tf_op jit(solution)/shard_map/pallas_call | solution.py:397
Async XLA Ops:
  0.0 25.3 %copy-start.2 = (f32[8,2,64,188]{3,2,1,0:T(8,128)S(1)}, f32[8,2,64,188]{3,2,1,0:T(8,128)}, u32[]{:S(2)}) copy-start(f32[8,2,64,188]{3,2,1,0:T(8,128)} %steer_ref.1) | copy-start | bytes 2310148
  8.8 16.5 %copy-start.4 = (s32[36]{0:T(128)S(1)}, s32[36]{0:T(128)}, u32[]{:S(2)}) copy-start(s32[36]{0:T(128)} %index_ref.1) | copy-start | bytes 436
  8.8 2.7 %collective-permute-start = (bf16[8,288,128]{2,1,0:T(8,128)(2,1)}, bf16[8,288,128]{2,1,0:T(8,128)(2,1)S(1)}, u32[]{:S(2)}, u32[]{:S(2)}) collective-permute-start(bf16[8,288,128]{2,1,0:T(8,128)(2,1)} %get-tuple-element.13), channel_id=1, source_target_pairs={{0,1},{2,3},{4,5},{6,7},{1,0},{3,2},{5,4},{7,6},{8,9},{10,11},{12,... | collective-permute-start | bytes 1769480 | tf_op jit(solution)/shard_map/ppermute | solution.py:426
  8.9 11.4 %collective-permute-start.1 = (bf16[8,288,128]{2,1,0:T(8,128)(2,1)}, bf16[8,288,128]{2,1,0:T(8,128)(2,1)S(1)}, u32[]{:S(2)}, u32[]{:S(2)}) collective-permute-start(bf16[8,288,128]{2,1,0:T(8,128)(2,1)} %get-tuple-element.14), channel_id=1, source_target_pairs={{1,2},{3,4},{5,6},{2,1},{4,3},{6,5},{9,10},{11,12},{13,14},{10,9},... | collective-permute-start | bytes 1769480 | tf_op jit(solution)/shard_map/ppermute | solution.py:425
  20.3 1.3 %copy-start.1 = (f32[8,288,128]{2,1,0:T(8,128)S(1)}, f32[8,288,128]{2,1,0:T(8,128)}, u32[]{:S(2)}) copy-start(f32[8,288,128]{2,1,0:T(8,128)} %get-tuple-element.12.own_ref) | copy-start | bytes 3538948
  21.6 10.9 %copy-start.3 = (s32[64]{0:T(128)S(1)}, s32[64]{0:T(128)}, u32[]{:S(2)}) copy-start(s32[64]{0:T(128)} %flags_ref.3) | copy-start | bytes 772
  21.8 6.7 %collective-permute-start.2 = (bf16[2,288,128]{2,1,0:T(8,128)(2,1)S(1)}, bf16[2,288,128]{2,1,0:T(8,128)(2,1)S(1)}, u32[]{:S(2)}, u32[]{:S(2)}) collective-permute-start(bf16[2,288,128]{2,1,0:T(8,128)(2,1)S(1)} %get-tuple-element.16), channel_id=1, source_target_pairs={{0,8},{8,0},{16,24},{24,16},{1,9},{9,1},{17,25},{25,17},{2,10},{10... | collective-permute-start | bytes 442376 | tf_op jit(solution)/shard_map/ppermute | solution.py:431
  23.3 9.1 %collective-permute-start.3 = (bf16[2,288,128]{2,1,0:T(8,128)(2,1)S(1)}, bf16[2,288,128]{2,1,0:T(8,128)(2,1)S(1)}, u32[]{:S(2)}, u32[]{:S(2)}) collective-permute-start(bf16[2,288,128]{2,1,0:T(8,128)(2,1)S(1)} %get-tuple-element.17), channel_id=1, source_target_pairs={{0,16},{8,24},{16,0},{24,8},{1,17},{9,25},{17,1},{25,9},{2,18},{10... | collective-permute-start | bytes 442376 | tf_op jit(solution)/shard_map/ppermute | solution.py:431
  24.9 7.6 %collective-permute-start.4 = (bf16[2,288,128]{2,1,0:T(8,128)(2,1)S(1)}, bf16[2,288,128]{2,1,0:T(8,128)(2,1)S(1)}, u32[]{:S(2)}, u32[]{:S(2)}) collective-permute-start(bf16[2,288,128]{2,1,0:T(8,128)(2,1)S(1)} %get-tuple-element.18), channel_id=1, source_target_pairs={{0,24},{8,16},{16,8},{24,0},{1,25},{9,17},{17,9},{25,1},{2,26},{10... | collective-permute-start | bytes 442376 | tf_op jit(solution)/shard_map/ppermute | solution.py:431
  39.1 4.3 %collective-permute-start.5 = (bf16[2,120,128]{2,1,0:T(8,128)(2,1)S(1)}, bf16[2,120,128]{2,1,0:T(8,128)(2,1)S(1)}, u32[]{:S(2)}, u32[]{:S(2)}) collective-permute-start(bf16[2,120,128]{2,1,0:T(8,128)(2,1)S(1)} %shard_map.49.refs_0_), channel_id=1, source_target_pairs={{0,8},{8,0},{16,24},{24,16},{1,9},{9,1},{17,25},{25,17},{2,10},{10... | collective-permute-start | bytes 184328 | tf_op jit(solution)/shard_map/ppermute | solution.py:431
  40.4 4.6 %collective-permute-start.6 = (bf16[2,120,128]{2,1,0:T(8,128)(2,1)S(1)}, bf16[2,120,128]{2,1,0:T(8,128)(2,1)S(1)}, u32[]{:S(2)}, u32[]{:S(2)}) collective-permute-start(bf16[2,120,128]{2,1,0:T(8,128)(2,1)S(1)} %shard_map.49.refs_0_), channel_id=1, source_target_pairs={{0,16},{8,24},{16,0},{24,8},{1,17},{9,25},{17,1},{25,9},{2,18},{10... | collective-permute-start | bytes 184328 | tf_op jit(solution)/shard_map/ppermute | solution.py:431
  41.2 5.1 %collective-permute-start.7 = (bf16[2,120,128]{2,1,0:T(8,128)(2,1)S(1)}, bf16[2,120,128]{2,1,0:T(8,128)(2,1)S(1)}, u32[]{:S(2)}, u32[]{:S(2)}) collective-permute-start(bf16[2,120,128]{2,1,0:T(8,128)(2,1)S(1)} %shard_map.49.refs_0_), channel_id=1, source_target_pairs={{0,24},{8,16},{16,8},{24,0},{1,25},{9,17},{17,9},{25,1},{2,26},{10... | collective-permute-start | bytes 184328 | tf_op jit(solution)/shard_map/ppermute | solution.py:431
  46.3 3.6 %copy-start = (bf16[8,2,188,1536]{3,1,2,0:T(2,128)(2,1)S(1)}, bf16[8,2,188,1536]{3,1,2,0:T(2,128)(2,1)}, u32[]{:S(2)}) copy-start(bf16[8,2,188,1536]{3,1,2,0:T(2,128)(2,1)} %param.4) | copy-start | bytes 27721732

commit v2 on v1

--- a/solution.py
+++ b/solution.py
@@ -94,12 +94,26 @@
 
 
 def covariance_kernel(
-    first_ref, flags_ref, volt_hbm, across_ref, inside_ref, own_ref, volts, lefts, rights, kept, sems
+    first_ref,
+    flags_hbm,
+    volt_hbm,
+    across_ref,
+    inside_ref,
+    own_ref,
+    volts,
+    lefts,
+    rights,
+    kept,
+    flags_ref,
+    sems,
+    flags_sem,
 ):
     channels, ports, _, samples = volts.shape
     copies = [
         pltpu.make_async_copy(volt_hbm.at[c], volts.at[c], sems.at[c]) for c in range(channels)
     ]
+    flags_copy = pltpu.make_async_copy(flags_hbm, flags_ref, flags_sem)
+    flags_copy.start()
     groups = [range(c, c + 2) for c in range(0, channels, 2)]
     for group in groups[:2]:
         for c in group:
@@ -113,11 +127,12 @@
             for c in later:
                 copies[c].start()
         for c in group:
-            gram(volts[c].reshape(2 * ports, samples), lefts.at[c], rights.at[c])
+            gram(volts[c].reshape(2 * ports, samples), lefts.at[c % 4], rights.at[c % 4])
         for c in groups[number - 1] if number else ():
-            pack(lefts.at[c], rights.at[c], kept.at[c])
+            pack(lefts.at[c % 4], rights.at[c % 4], kept.at[c])
     for c in groups[-1]:
-        pack(lefts.at[c], rights.at[c], kept.at[c])
+        pack(lefts.at[c % 4], rights.at[c % 4], kept.at[c])
+    flags_copy.wait()
     flags = [flags_ref[first_ref[0] + c].astype(jnp.float32) for c in range(channels)]
     odd_block = (first_ref[0] // channels) % 2 == 1
     for start in range(0, kept.shape[1], 16):
@@ -136,28 +151,30 @@
 
 
 def covariances(first, flags, voltages, size):
-    channels, _, ports, samples = voltages.shape
+    channels, ports, _, samples = voltages.shape
     folded = (channels, size + size // 2, LANES)
     smem = pl.BlockSpec(memory_space=pltpu.SMEM)
     vmem = pl.BlockSpec(memory_space=pltpu.VMEM)
     return pl.pallas_call(
         covariance_kernel,
-        in_specs=[smem, smem, pl.BlockSpec(memory_space=pltpu.HBM)],
-        out_specs=[vmem] * 3,
+        in_specs=[smem] + [pl.BlockSpec(memory_space=pltpu.HBM)] * 2,
+        out_specs=[vmem] * 4,
         scratch_shapes=[
-            pltpu.VMEM((channels, ports, 2, samples), voltages.dtype),
-            pltpu.VMEM((channels, 2, 2 * size, LANES), jnp.float32),
-            pltpu.VMEM((channels, 2, size, LANES), jnp.float32),
+            pltpu.VMEM((4, 2, 2 * size, LANES), jnp.float32),
+            pltpu.VMEM((4, 2, size, LANES), jnp.float32),
             pltpu.VMEM(folded, jnp.float32),
+            pltpu.SMEM(flags.shape, flags.dtype),
             pltpu.SemaphoreType.DMA((channels,)),
+            pltpu.SemaphoreType.DMA,
         ],
         out_shape=[
-            jax.ShapeDtypeStruct(folded, jnp.bfloat16),
-            jax.ShapeDtypeStruct(folded, jnp.bfloat16),
-            jax.ShapeDtypeStruct(folded, jnp.float32),
+            pltpu.VMEM(folded, jnp.bfloat16),
+            pltpu.VMEM(folded, jnp.bfloat16),
+            pltpu.VMEM(folded, jnp.float32),
+            pltpu.VMEM(voltages.shape, voltages.dtype),
         ],
-        compiler_params=pltpu.CompilerParams(vmem_limit_bytes=56 * 1024 * 1024),
-    )(first, flags, jnp.transpose(voltages, (0, 2, 1, 3)))
+        compiler_params=pltpu.CompilerParams(vmem_limit_bytes=VMEM_LIMIT),
+    )(first, *[pltpu.with_memory_space_constraint(a, pltpu.HBM) for a in (flags, voltages)])
 
 
 def window_kernel(slab_ref, own_ref, inside_ref, across_ref, mine_ref, *sent_refs):
@@ -258,34 +275,40 @@
     return jnp.concatenate(arrays, axis=0)
 
 
-def apply(y, real, imag, passes):
-    n = y.shape[0]
+def multiply(y, real, imag, squares=True):
+    n, m = y.shape[0], real.shape[0]
     half = n // 2
-    if passes == 1:
-        with_real = dot_nn(y.astype(jnp.bfloat16), real.astype(jnp.bfloat16))
-        with_imag = dot_nn(y.astype(jnp.bfloat16), imag.astype(jnp.bfloat16))
+    (rh, rl), (ih, il), (yh, yl) = split(real), split(imag), split(y)
+    if squares:
+        by_rh, by_rl = dot_nn(stack(yh, yl, rh, rl), rh), dot_nn(stack(yh, rh), rl)
+        by_ih, by_il = dot_nn(stack(yh, yl, ih, il), ih), dot_nn(stack(yh, ih, rh), il)
+        cross = dot_nn(stack(rh, rl), ih)
     else:
-        (rh, rl), (ih, il), (yh, yl) = split(real), split(imag), split(y)
-        by_rh, by_ih = dot_nn(stack(yh, yl), rh), dot_nn(stack(yh, yl), ih)
-        with_real = by_rh[:n] + by_rh[n:] + dot_nn(yh, rl)
-        with_imag = by_ih[:n] + by_ih[n:] + dot_nn(yh, il)
-    return stack(with_real[:half] + with_imag[half:], with_real[half:] - with_imag[:half])
-
-
-def square(real, imag, passes):
-    n = real.shape[0]
-    if passes == 1:
-        rh, ih = real.astype(jnp.bfloat16), imag.astype(jnp.bfloat16)
-        by_ih = dot_nn(stack(ih, rh), ih)
-        rr, ii, ri = dot_nn(rh, rh), by_ih[:n], by_ih[n:]
-    else:
-        (rh, rl), (ih, il) = split(real), split(imag)
-        by_rh, by_rl = dot_nn(stack(rh, rl), rh), dot_nn(rh, rl)
-        by_ih, by_il = dot_nn(stack(ih, il, rh, rl), ih), dot_nn(stack(ih, rh), il)
-        rr = by_rh[:n] + by_rh[n:] + by_rl
-        ii = by_ih[:n] + by_ih[n : 2 * n] + by_il[:n]
-        ri = by_ih[2 * n : 3 * n] + by_ih[3 * n :] + by_il[n:]
-    return rr - ii, ri - ri.T
+        by_rh, by_rl = dot_nn(stack(yh, yl), rh), dot_nn(yh, rl)
+        by_ih, by_il = dot_nn(stack(yh, yl), ih), dot_nn(yh, il)
+    with_real = by_rh[:n] + by_rh[n : 2 * n] + by_rl[:n]
+    with_imag = by_ih[:n] + by_ih[n : 2 * n] + by_il[:n]
+    product = stack(with_real[:half] + with_imag[half:], with_real[half:] - with_imag[:half])
+    if not squares:
+        return product, None, None
+    by_rh, by_rl, by_ih, by_il = by_rh[2 * n :], by_rl[n:], by_ih[2 * n :], by_il[n:]
+    rr = by_rh[:m] + by_rh[m:] + by_rl
+    ii = by_ih[:m] + by_ih[m:] + by_il[:m]
+    ri = cross[:m] + cross[m:] + by_il[m:]
+    return product, rr - ii, ri - ri.T
+
+
+def multiply_once(y, real, imag, squares):
+    n, m = y.shape[0], real.shape[0]
+    half = n // 2
+    rh, ih, yh = (a.astype(jnp.bfloat16) for a in (real, imag, y))
+    by_rh = dot_nn(stack(yh, rh) if squares else yh, rh)
+    by_ih = dot_nn(stack(yh, ih, rh) if squares else yh, ih)
+    product = stack(by_rh[:half] + by_ih[half:n], by_rh[half:n] - by_ih[:half])
+    if not squares:
+        return product, None, None
+    ri = by_ih[n + m :]
+    return product, by_rh[n:] - by_ih[n : n + m], ri - ri.T
 
 
 def solve_kernel(ports, beams, first_ref, flags_ref, *refs):
@@ -314,16 +337,17 @@
             if number == len(steps) - 2:
                 real, imag = identity - real, -imag
             if number < len(steps) - 2:
-                new_y = gain * (2.0 * y - apply(y, real, imag, 3))
-                real2, imag2 = square(real, imag, 3)
+                product, real2, imag2 = multiply(y, real, imag)
+                y = gain * (2.0 * y - product)
                 real, imag = gain * (2.0 * real - real2), gain * (2.0 * imag - imag2)
+            elif squares:
+                product, _, _ = multiply(y, real, imag, squares=False)
+                _, real, imag = multiply_once(y, real, imag, True)
+                y = gain * (y + product)
+                real, imag = gain * (real - identity * (spread * spread / 2)), gain * imag
             else:
-                new_y = gain * (y + apply(y, real, imag, 3 if squares else 1))
-                if squares:
-                    real, imag = square(real, imag, 1)
-                    real = gain * (real - identity * (spread * spread / 2))
-                    imag = gain * imag
-            state[c] = real, imag, new_y
+                y = gain * (y + multiply_once(y, real, imag, False)[0])
+            state[c] = real, imag, y
     beam = lax.broadcasted_iota(jnp.int32, (half, 1), 0)
     row, col = iotas(2 * half, 2 * half)
     place = jnp.where(row % 2 == 0, row // 2, row // 2 + half)
@@ -390,11 +414,11 @@
 
 
 def formed_beams(slab, voltages, weights, beams):
-    channels, _, ports, samples = voltages.shape
+    channels, ports, _, samples = voltages.shape
     rows = weights[0].shape[1] * 2 // 3
-    together = 2
+    together = 4
     whole = pl.BlockSpec(weights[0].shape, lambda i: (0, 0, 0))
-    out = pl.pallas_call(
+    return pl.pallas_call(
         beam_kernel,
         grid=(channels // together,),
         in_specs=[pl.BlockSpec(memory_space=pltpu.SMEM), pl.BlockSpec(memory_space=pltpu.VMEM)]
@@ -403,8 +427,7 @@
         scratch_shapes=[pltpu.VMEM((channels, rows, 2 * ports), jnp.bfloat16)],
         out_shape=jax.ShapeDtypeStruct((channels, beams, 2, samples), jnp.bfloat16),
         compiler_params=pltpu.CompilerParams(vmem_limit_bytes=VMEM_LIMIT),
-    )(slab, jnp.transpose(voltages, (0, 2, 1, 3)), *weights)
-    return jnp.transpose(out, (0, 2, 1, 3))
+    )(slab, voltages, *weights)
 
 
 def body(voltages, steering, beam_index, channel_flags):
@@ -419,7 +442,8 @@
     slab = lax.axis_index("slab").astype(jnp.int32).reshape(1)
     first_channel = (lax.axis_index("chan") * channel_count).astype(jnp.int32).reshape(1)
     chosen = chosen_vectors(slab, beam_index, steering, share, half, size)
-    across, inside, own = covariances(first_channel, channel_flags, voltages, size)
+    by_port = jnp.transpose(voltages, (0, 2, 1, 3))
+    across, inside, own, held = covariances(first_channel, channel_flags, by_port, size)
     pairs = [[(i, i + 1) for i in range(start, blocks - 1, 2)] for start in range(2)]
     inside_pairs, across_pairs = [ahead + [(j, i) for i, j in ahead] for ahead in pairs]
     across = lax.ppermute(across, "chan", across_pairs)
@@ -436,7 +460,8 @@
     first_share = first_channel + slab * share
     weights = solved_weights(first_share, channel_flags, mine, got, chosen, port_count, beam_count)
     others = swap([weights] * (slabs - 1))
-    return formed_beams(slab, voltages, [weights, *others], beam_count)
+    beams = formed_beams(slab, held, [weights, *others], beam_count)
+    return jnp.transpose(beams, (0, 2, 1, 3))
 
 
 def solution(mesh):

time: 54.2 us -> 55.1 us (1.017)
  local copies, waits for them, and re-layouts: 4.91 us -> 7.2 us
  Pallas kernels: 20.4 us -> 19.1 us
    unnamed x10, local copies, waits for them, and re-layouts: 4.91 us -> 7.2 us
    pallas_call x1, Pallas kernels: 8.83 us -> 7.89 us  [covariances(): pl.pallas_call(covariance_kernel, in_specs=[smem] + [pl.BlockSpec(memory_...]
where the time goes in v2:
time: 55.1 us; the launch traced here: 55 us
  Pallas kernels  19.1 us (35%)
  waiting for transfers between devices  18.9 us (34%)
  starting transfers between devices  9.72 us (18%)
  local copies, waits for them, and re-layouts  7.2 us (13%)
    ppermute x6, waiting for transfers between devices, swap(): lax.ppermute(array, 'slab', [(i, i ^ turn) for i in range(slabs)])  10.1 us
    ppermute x1, waiting for transfers between devices, body(): across = lax.ppermute(across, 'chan', across_pairs)  8.74 us
    pallas_call x1, Pallas kernels, covariances(): pl.pallas_call(covariance_kernel, in_specs=[smem] + [pl.BlockSpec(memory_...  7.89 us
    unnamed x10, local copies, waits for them, and re-layouts  7.2 us
    ppermute x6, starting transfers between devices, swap(): lax.ppermute(array, 'slab', [(i, i ^ turn) for i in range(slabs)])  7.08 us
    pallas_call x1, Pallas kernels, solved_weights(): pl.pallas_call(functools.partial(solve_kernel, ports, beams), in_specs=[s...  6.53 us
    pallas_call x1, Pallas kernels, formed_beams(): pl.pallas_call(beam_kernel, grid=(channels // together,), in_specs=[pl.Bl...  3.85 us
    ppermute x1, starting transfers between devices, body(): across = lax.ppermute(across, 'chan', across_pairs)  2.64 us
  transfers between devices with their start and end apart: 8, of which 6 were waited for; matrix products, arithmetic and copies ran while one was open for 0% of the time, Pallas kernels for 1%

profile of v2, /device:TPU:16, one launch (start us, length us, event | category | flops | bytes accessed | tf_op | source)
XLA Modules:
  0.0 55.0 jit_solution(13036299559606386375)
XLA Ops:
  0.0 0.0 copy-start.3
  0.0 0.0 copy-start.4
  0.0 0.0 copy-start.2
  0.0 7.9 %shard_map.46 = (bf16[8,288,128]{2,1,0:T(8,128)(2,1)}, bf16[8,288,128]{2,1,0:T(8,128)(2,1)}, f32[8,288,128]{2,1,0:T(8,128)S(1)}, bf16[8,188,2,1536]{3,2,1,0:T(2,128)(2,1)S(1)}) custom-call(s32[1]{0:T(128)} %bitcast.1.first_ref, s32[64]{0:T(128)} %flags_ref.1, bf16[8,188,2,1536]{3,2,1,0:T(2,128)(2,1)} %bitcast.4), custom_call_target="tpu_custom_call" | custom-call | tf_op jit(solution)/shard_map/pallas_call | solution.py:158
  7.9 0.0 copy-start
  7.9 3.6 %copy-done = bf16[8,188,2,1536]{3,2,1,0:T(2,128)(2,1)} copy-done((bf16[8,188,2,1536]{3,2,1,0:T(2,128)(2,1)}, bf16[8,188,2,1536]{3,2,1,0:T(2,128)(2,1)S(1)}, u32[]{:S(2)}) %copy-start) | copy-done | bytes 9240600
  11.5 0.0 collective-permute-start
  11.5 2.6 %collective-permute-start.1 = (bf16[8,288,128]{2,1,0:T(8,128)(2,1)}, bf16[8,288,128]{2,1,0:T(8,128)(2,1)S(1)}, u32[]{:S(2)}, u32[]{:S(2)}) collective-permute-start(bf16[8,288,128]{2,1,0:T(8,128)(2,1)} %get-tuple-element.16), channel_id=1, source_target_pairs={{1,2},{3,4},{5,6},{2,1},{4,3},{6,5},{9,10},{11,12},{13,14},{10,9},... | collective-permute-start | bytes 1769480 | tf_op jit(solution)/shard_map/ppermute | solution.py:449
  14.1 0.0 collective-permute-done.inside_ref
  14.1 8.7 %collective-permute-done.1.across_ref = bf16[8,288,128]{2,1,0:T(8,128)(2,1)S(1)} collective-permute-done((bf16[8,288,128]{2,1,0:T(8,128)(2,1)}, bf16[8,288,128]{2,1,0:T(8,128)(2,1)S(1)}, u32[]{:S(2)}, u32[]{:S(2)}) %collective-permute-start.1) | collective-permute-done | bytes 589856 | tf_op jit(solution)/shard_map/ppermute | solution.py:449
  22.9 0.2 shard_map.47
  23.1 1.5 %collective-permute-start.2 = (bf16[2,288,128]{2,1,0:T(8,128)(2,1)S(1)}, bf16[2,288,128]{2,1,0:T(8,128)(2,1)S(1)}, u32[]{:S(2)}, u32[]{:S(2)}) collective-permute-start(bf16[2,288,128]{2,1,0:T(8,128)(2,1)S(1)} %get-tuple-element.18), channel_id=1, source_target_pairs={{0,8},{8,0},{16,24},{24,16},{1,9},{9,1},{17,25},{25,17},{2,10},{10... | collective-permute-start | bytes 442376 | tf_op jit(solution)/shard_map/ppermute | solution.py:455
  24.6 1.5 %collective-permute-start.3 = (bf16[2,288,128]{2,1,0:T(8,128)(2,1)S(1)}, bf16[2,288,128]{2,1,0:T(8,128)(2,1)S(1)}, u32[]{:S(2)}, u32[]{:S(2)}) collective-permute-start(bf16[2,288,128]{2,1,0:T(8,128)(2,1)S(1)} %get-tuple-element.19), channel_id=1, source_target_pairs={{0,16},{8,24},{16,0},{24,8},{1,17},{9,25},{17,1},{25,9},{2,18},{10... | collective-permute-start | bytes 442376 | tf_op jit(solution)/shard_map/ppermute | solution.py:455
  26.1 0.5 collective-permute-start.4
  26.6 0.0 copy-done.4
  26.6 0.0 copy-done.2
  26.6 0.7 %shard_map.48.refs_4_ = f32[2,80,192]{2,1,0:T(8,128)S(1)} custom-call(s32[1]{0:T(128)} %bitcast.slab_ref, s32[36]{0:T(128)S(1)} %copy-done.4, f32[8,2,64,188]{3,2,1,0:T(8,128)S(1)} %copy-done.2), custom_call_target="tpu_custom_call" | custom-call | tf_op jit(solution)/shard_map/pallas_call | solution.py:219
  27.3 2.5 %collective-permute-done.2.refs_1_ = bf16[2,288,128]{2,1,0:T(8,128)(2,1)S(1)} collective-permute-done((bf16[2,288,128]{2,1,0:T(8,128)(2,1)S(1)}, bf16[2,288,128]{2,1,0:T(8,128)(2,1)S(1)}, u32[]{:S(2)}, u32[]{:S(2)}) %collective-permute-start.2) | collective-permute-done | bytes 147488 | tf_op jit(solution)/shard_map/ppermute | solution.py:455
  29.8 4.0 %collective-permute-done.3.refs_2_ = bf16[2,288,128]{2,1,0:T(8,128)(2,1)S(1)} collective-permute-done((bf16[2,288,128]{2,1,0:T(8,128)(2,1)S(1)}, bf16[2,288,128]{2,1,0:T(8,128)(2,1)S(1)}, u32[]{:S(2)}, u32[]{:S(2)}) %collective-permute-start.3) | collective-permute-done | bytes 147488 | tf_op jit(solution)/shard_map/ppermute | solution.py:455
  33.8 0.0 collective-permute-done.4.refs_3_
  33.8 0.0 copy-done.3
  33.8 6.5 %shard_map.49.refs_0_ = bf16[2,120,128]{2,1,0:T(8,128)(2,1)S(1)} custom-call(s32[1]{0:T(128)S(6)} %add.3.first_ref, s32[64]{0:T(128)S(1)} %copy-done.3, f32[2,288,128]{2,1,0:T(8,128)S(1)} %get-tuple-element.17.refs_0_, bf16[2,288,128]{2,1,0:T(8,128)(2,1)S(1)} %collective-permute-done.2.refs_1_, bf16[2,288,128]{2,1,0:T(8,128)(2,1)S(1)} %collective-permute-done.3.refs_2_, ...), custom_call_target="tpu_custom_call" | custom-call | tf_op jit(solution)/shard_map/pallas_call | solution.py:374
  40.3 1.3 %collective-permute-start.5 = (bf16[2,120,128]{2,1,0:T(8,128)(2,1)S(1)}, bf16[2,120,128]{2,1,0:T(8,128)(2,1)S(1)}, u32[]{:S(2)}, u32[]{:S(2)}) collective-permute-start(bf16[2,120,128]{2,1,0:T(8,128)(2,1)S(1)} %shard_map.49.refs_0_), channel_id=1, source_target_pairs={{0,8},{8,0},{16,24},{24,16},{1,9},{9,1},{17,25},{25,17},{2,10},{10... | collective-permute-start | bytes 184328 | tf_op jit(solution)/shard_map/ppermute | solution.py:455
  41.6 0.8 %collective-permute-start.6 = (bf16[2,120,128]{2,1,0:T(8,128)(2,1)S(1)}, bf16[2,120,128]{2,1,0:T(8,128)(2,1)S(1)}, u32[]{:S(2)}, u32[]{:S(2)}) collective-permute-start(bf16[2,120,128]{2,1,0:T(8,128)(2,1)S(1)} %shard_map.49.refs_0_), channel_id=1, source_target_pairs={{0,16},{8,24},{16,0},{24,8},{1,17},{9,25},{17,1},{25,9},{2,18},{10... | collective-permute-start | bytes 184328 | tf_op jit(solution)/shard_map/ppermute | solution.py:455
  42.4 1.4 %collective-permute-start.7 = (bf16[2,120,128]{2,1,0:T(8,128)(2,1)S(1)}, bf16[2,120,128]{2,1,0:T(8,128)(2,1)S(1)}, u32[]{:S(2)}, u32[]{:S(2)}) collective-permute-start(bf16[2,120,128]{2,1,0:T(8,128)(2,1)S(1)} %shard_map.49.refs_0_), channel_id=1, source_target_pairs={{0,24},{8,16},{16,8},{24,0},{1,25},{9,17},{17,9},{25,1},{2,26},{10... | collective-permute-start | bytes 184328 | tf_op jit(solution)/shard_map/ppermute | solution.py:455
  43.8 0.7 %collective-permute-done.5.refs_1_ = bf16[2,120,128]{2,1,0:T(8,128)(2,1)S(1)} collective-permute-done((bf16[2,120,128]{2,1,0:T(8,128)(2,1)S(1)}, bf16[2,120,128]{2,1,0:T(8,128)(2,1)S(1)}, u32[]{:S(2)}, u32[]{:S(2)}) %collective-permute-start.5) | collective-permute-done | bytes 61472 | tf_op jit(solution)/shard_map/ppermute | solution.py:455
  44.5 1.7 %collective-permute-done.6.refs_2_ = bf16[2,120,128]{2,1,0:T(8,128)(2,1)S(1)} collective-permute-done((bf16[2,120,128]{2,1,0:T(8,128)(2,1)S(1)}, bf16[2,120,128]{2,1,0:T(8,128)(2,1)S(1)}, u32[]{:S(2)}, u32[]{:S(2)}) %collective-permute-start.6) | collective-permute-done | bytes 61472 | tf_op jit(solution)/shard_map/ppermute | solution.py:455
  46.2 1.3 %collective-permute-done.7.refs_3_ = bf16[2,120,128]{2,1,0:T(8,128)(2,1)S(1)} collective-permute-done((bf16[2,120,128]{2,1,0:T(8,128)(2,1)S(1)}, bf16[2,120,128]{2,1,0:T(8,128)(2,1)S(1)}, u32[]{:S(2)}, u32[]{:S(2)}) %collective-permute-start.7) | collective-permute-done | bytes 61472 | tf_op jit(solution)/shard_map/ppermute | solution.py:455
  47.5 0.0 copy-start.1
  47.5 3.6 %copy-done.1 = bf16[8,188,2,1536]{3,2,1,0:T(2,128)(2,1)S(1)} copy-done((bf16[8,188,2,1536]{3,2,1,0:T(2,128)(2,1)S(1)}, bf16[8,188,2,1536]{3,2,1,0:T(2,128)(2,1)}, u32[]{:S(2)}) %copy-start.1) | copy-done | bytes 9240600
  51.1 3.9 %shard_map.50 = bf16[8,36,2,1536]{3,2,1,0:T(2,128)(2,1)} custom-call(s32[1]{0:T(128)} %bitcast.slab_ref, bf16[8,188,2,1536]{3,2,1,0:T(2,128)(2,1)S(1)} %copy-done.1, bf16[2,120,128]{2,1,0:T(8,128)(2,1)S(1)} %shard_map.49.refs_0_, bf16[2,120,128]{2,1,0:T(8,128)(2,1)S(1)} %collective-permute-done.5.refs_1_, ...), custom_call_target="tpu_custom_call" | custom-call | tf_op jit(solution)/shard_map/pallas_call | solution.py:421
Async XLA Ops:
  0.0 33.8 %copy-start.3 = (s32[64]{0:T(128)S(1)}, s32[64]{0:T(128)}, u32[]{:S(2)}) copy-start(s32[64]{0:T(128)} %flags_ref.1) | copy-start | bytes 772
  0.0 26.6 %copy-start.4 = (s32[36]{0:T(128)S(1)}, s32[36]{0:T(128)}, u32[]{:S(2)}) copy-start(s32[36]{0:T(128)} %index_ref.1) | copy-start | bytes 436
  0.0 26.6 %copy-start.2 = (f32[8,2,64,188]{3,2,1,0:T(8,128)S(1)}, f32[8,2,64,188]{3,2,1,0:T(8,128)}, u32[]{:S(2)}) copy-start(f32[8,2,64,188]{3,2,1,0:T(8,128)} %steer_ref.1) | copy-start | bytes 2310148
  7.9 3.6 %copy-start = (bf16[8,188,2,1536]{3,2,1,0:T(2,128)(2,1)}, bf16[8,188,2,1536]{3,2,1,0:T(2,128)(2,1)S(1)}, u32[]{:S(2)}) copy-start(bf16[8,188,2,1536]{3,2,1,0:T(2,128)(2,1)S(1)} %get-tuple-element.13.volt_ref) | copy-start | bytes 27721732
  11.5 2.7 %collective-permute-start = (bf16[8,288,128]{2,1,0:T(8,128)(2,1)}, bf16[8,288,128]{2,1,0:T(8,128)(2,1)S(1)}, u32[]{:S(2)}, u32[]{:S(2)}) collective-permute-start(bf16[8,288,128]{2,1,0:T(8,128)(2,1)} %get-tuple-element.15), channel_id=1, source_target_pairs={{0,1},{2,3},{4,5},{6,7},{1,0},{3,2},{5,4},{7,6},{8,9},{10,11},{12,... | collective-permute-start | bytes 1769480 | tf_op jit(solution)/shard_map/ppermute | solution.py:450
  11.5 11.4 %collective-permute-start.1 = (bf16[8,288,128]{2,1,0:T(8,128)(2,1)}, bf16[8,288,128]{2,1,0:T(8,128)(2,1)S(1)}, u32[]{:S(2)}, u32[]{:S(2)}) collective-permute-start(bf16[8,288,128]{2,1,0:T(8,128)(2,1)} %get-tuple-element.16), channel_id=1, source_target_pairs={{1,2},{3,4},{5,6},{2,1},{4,3},{6,5},{9,10},{11,12},{13,14},{10,9},... | collective-permute-start | bytes 1769480 | tf_op jit(solution)/shard_map/ppermute | solution.py:449
  23.1 6.7 %collective-permute-start.2 = (bf16[2,288,128]{2,1,0:T(8,128)(2,1)S(1)}, bf16[2,288,128]{2,1,0:T(8,128)(2,1)S(1)}, u32[]{:S(2)}, u32[]{:S(2)}) collective-permute-start(bf16[2,288,128]{2,1,0:T(8,128)(2,1)S(1)} %get-tuple-element.18), channel_id=1, source_target_pairs={{0,8},{8,0},{16,24},{24,16},{1,9},{9,1},{17,25},{25,17},{2,10},{10... | collective-permute-start | bytes 442376 | tf_op jit(solution)/shard_map/ppermute | solution.py:455
  24.6 9.1 %collective-permute-start.3 = (bf16[2,288,128]{2,1,0:T(8,128)(2,1)S(1)}, bf16[2,288,128]{2,1,0:T(8,128)(2,1)S(1)}, u32[]{:S(2)}, u32[]{:S(2)}) collective-permute-start(bf16[2,288,128]{2,1,0:T(8,128)(2,1)S(1)} %get-tuple-element.19), channel_id=1, source_target_pairs={{0,16},{8,24},{16,0},{24,8},{1,17},{9,25},{17,1},{25,9},{2,18},{10... | collective-permute-start | bytes 442376 | tf_op jit(solution)/shard_map/ppermute | solution.py:455
  26.1 7.6 %collective-permute-start.4 = (bf16[2,288,128]{2,1,0:T(8,128)(2,1)S(1)}, bf16[2,288,128]{2,1,0:T(8,128)(2,1)S(1)}, u32[]{:S(2)}, u32[]{:S(2)}) collective-permute-start(bf16[2,288,128]{2,1,0:T(8,128)(2,1)S(1)} %get-tuple-element.20), channel_id=1, source_target_pairs={{0,24},{8,16},{16,8},{24,0},{1,25},{9,17},{17,9},{25,1},{2,26},{10... | collective-permute-start | bytes 442376 | tf_op jit(solution)/shard_map/ppermute | solution.py:455
  40.3 4.3 %collective-permute-start.5 = (bf16[2,120,128]{2,1,0:T(8,128)(2,1)S(1)}, bf16[2,120,128]{2,1,0:T(8,128)(2,1)S(1)}, u32[]{:S(2)}, u32[]{:S(2)}) collective-permute-start(bf16[2,120,128]{2,1,0:T(8,128)(2,1)S(1)} %shard_map.49.refs_0_), channel_id=1, source_target_pairs={{0,8},{8,0},{16,24},{24,16},{1,9},{9,1},{17,25},{25,17},{2,10},{10... | collective-permute-start | bytes 184328 | tf_op jit(solution)/shard_map/ppermute | solution.py:455
  41.6 4.7 %collective-permute-start.6 = (bf16[2,120,128]{2,1,0:T(8,128)(2,1)S(1)}, bf16[2,120,128]{2,1,0:T(8,128)(2,1)S(1)}, u32[]{:S(2)}, u32[]{:S(2)}) collective-permute-start(bf16[2,120,128]{2,1,0:T(8,128)(2,1)S(1)} %shard_map.49.refs_0_), channel_id=1, source_target_pairs={{0,16},{8,24},{16,0},{24,8},{1,17},{9,25},{17,1},{25,9},{2,18},{10... | collective-permute-start | bytes 184328 | tf_op jit(solution)/shard_map/ppermute | solution.py:455
  42.4 5.1 %collective-permute-start.7 = (bf16[2,120,128]{2,1,0:T(8,128)(2,1)S(1)}, bf16[2,120,128]{2,1,0:T(8,128)(2,1)S(1)}, u32[]{:S(2)}, u32[]{:S(2)}) collective-permute-start(bf16[2,120,128]{2,1,0:T(8,128)(2,1)S(1)} %shard_map.49.refs_0_), channel_id=1, source_target_pairs={{0,24},{8,16},{16,8},{24,0},{1,25},{9,17},{17,9},{25,1},{2,26},{10... | collective-permute-start | bytes 184328 | tf_op jit(solution)/shard_map/ppermute | solution.py:455
  47.5 3.6 %copy-start.1 = (bf16[8,188,2,1536]{3,2,1,0:T(2,128)(2,1)S(1)}, bf16[8,188,2,1536]{3,2,1,0:T(2,128)(2,1)}, u32[]{:S(2)}) copy-start(bf16[8,188,2,1536]{3,2,1,0:T(2,128)(2,1)} %copy-done) | copy-start | bytes 27721732

commit v3 on v2

--- a/solution.py
+++ b/solution.py
@@ -158,8 +158,9 @@
     return pl.pallas_call(
         covariance_kernel,
         in_specs=[smem] + [pl.BlockSpec(memory_space=pltpu.HBM)] * 2,
-        out_specs=[vmem] * 4,
+        out_specs=[vmem] * 3,
         scratch_shapes=[
+            pltpu.VMEM(voltages.shape, voltages.dtype),
             pltpu.VMEM((4, 2, 2 * size, LANES), jnp.float32),
             pltpu.VMEM((4, 2, size, LANES), jnp.float32),
             pltpu.VMEM(folded, jnp.float32),
@@ -171,7 +172,6 @@
             pltpu.VMEM(folded, jnp.bfloat16),
             pltpu.VMEM(folded, jnp.bfloat16),
             pltpu.VMEM(folded, jnp.float32),
-            pltpu.VMEM(voltages.shape, voltages.dtype),
         ],
         compiler_params=pltpu.CompilerParams(vmem_limit_bytes=VMEM_LIMIT),
     )(first, *[pltpu.with_memory_space_constraint(a, pltpu.HBM) for a in (flags, voltages)])
@@ -311,7 +311,7 @@
     return product, by_rh[n:] - by_ih[n : n + m], ri - ri.T
 
 
-def solve_kernel(ports, beams, first_ref, flags_ref, *refs):
+def solve_kernel(ports, beams, first_ref, flags_ref, held_ref, *refs):
     own_ref, *got_refs, chosen_ref, weight_ref = refs
     share, half, size = weight_ref.shape[0], chosen_ref.shape[1] // 2, chosen_ref.shape[2]
     bound = ports / LOADING + 1.0
@@ -366,26 +366,48 @@
         )
 
 
-def solved_weights(first, flags, own, got, chosen, ports, beams):
+def solved_weights(first, flags, held, own, got, chosen, ports, beams):
     share, rows, _ = chosen.shape
     smem = pl.BlockSpec(memory_space=pltpu.SMEM)
     whole = [pl.BlockSpec(a.shape, lambda: (0, 0, 0)) for a in (own, *got, chosen)]
     shape = (share, rows + rows // 2, LANES)
     return pl.pallas_call(
         functools.partial(solve_kernel, ports, beams),
-        in_specs=[smem, smem] + whole,
+        in_specs=[smem, smem, pl.BlockSpec(memory_space=pl.ANY)] + whole,
         out_specs=pl.BlockSpec(shape, lambda: (0, 0, 0)),
         out_shape=jax.ShapeDtypeStruct(shape, jnp.bfloat16),
         compiler_params=pltpu.CompilerParams(vmem_limit_bytes=VMEM_LIMIT),
-    )(first, flags, own, *got, chosen)
-
-
-def beam_kernel(slab_ref, volt_ref, *refs):
-    *weight_refs, out_ref, mixed = refs
+    )(first, flags, held, own, *got, chosen)
+
+
+def hold_kernel(volt_hbm, weight_hbm, held_ref, sems):
+    copies = [
+        pltpu.make_async_copy(volt_hbm.at[c], held_ref.at[c], sems.at[c])
+        for c in range(held_ref.shape[0])
+    ]
+    for copy in copies:
+        copy.start()
+    for copy in copies:
+        copy.wait()
+
+
+def held_voltages(voltages, weights):
+    return pl.pallas_call(
+        hold_kernel,
+        in_specs=[pl.BlockSpec(memory_space=pltpu.HBM), pl.BlockSpec(memory_space=pl.ANY)],
+        out_specs=pl.BlockSpec(memory_space=pltpu.VMEM),
+        scratch_shapes=[pltpu.SemaphoreType.DMA((voltages.shape[0],))],
+        out_shape=pltpu.VMEM(voltages.shape, voltages.dtype),
+        compiler_params=pltpu.CompilerParams(vmem_limit_bytes=VMEM_LIMIT),
+    )(pltpu.with_memory_space_constraint(voltages, pltpu.HBM), weights)
+
+
+def beam_kernel(first_turn, slab_ref, volt_ref, *refs):
+    *weight_refs, out_ref, mixed = refs if first_turn == 0 else refs[1:]
     share, rows, _ = weight_refs[0].shape
     rows = rows * 2 // 3
     _, ports, _, samples = volt_ref.shape
-    together, beams = out_ref.shape[:2]
+    beams = out_ref.shape[1]
     step = pl.program_id(0)
 
     @pl.when(step == 0)
@@ -401,33 +423,41 @@
         to_odd = (col == 2 * row + 1).astype(jnp.float32).astype(jnp.bfloat16)
         placed = dot_nn(real_rows.astype(jnp.bfloat16), to_even)
         placed = (placed + dot_nn(imag_rows.astype(jnp.bfloat16), to_odd)).astype(jnp.bfloat16)
-        for turn in range(len(weight_refs)):
-            first = (slab_ref[0] ^ turn) * share
-            for c in range(share):
-                at = (turn * share + c) * rows
-                mixed[first + c] = placed[at : at + rows]
-
-    for c in range(together):
-        channel = step * together + c
-        formed = dot_nn(mixed[channel], volt_ref[channel].reshape(2 * ports, samples))
+        for number in range(len(folded)):
+            mixed[number] = placed[number * rows : (number + 1) * rows]
+
+    first = (slab_ref[0] ^ (step + first_turn)) * share
+    for c in range(share):
+        volt = volt_ref[first + c].reshape(2 * ports, samples)
+        formed = dot_nn(mixed[step * share + c], volt)
         out_ref[c] = formed[: 2 * beams].astype(jnp.bfloat16).reshape(beams, 2, samples)
 
 
-def formed_beams(slab, voltages, weights, beams):
+def formed_beams(slab, voltages, weights, beams, formed=None):
     channels, ports, _, samples = voltages.shape
-    rows = weights[0].shape[1] * 2 // 3
-    together = 4
-    whole = pl.BlockSpec(weights[0].shape, lambda i: (0, 0, 0))
+    share, rows, _ = weights[0].shape
+    first_turn = 0 if formed is None else 1
+    before = [] if formed is None else [formed]
+    whole = pl.BlockSpec(weights[0].shape, lambda i, _: (0, 0, 0))
     return pl.pallas_call(
-        beam_kernel,
-        grid=(channels // together,),
-        in_specs=[pl.BlockSpec(memory_space=pltpu.SMEM), pl.BlockSpec(memory_space=pltpu.VMEM)]
-        + [whole] * len(weights),
-        out_specs=pl.BlockSpec((together, beams, 2, samples), lambda i: (i, 0, 0, 0)),
-        scratch_shapes=[pltpu.VMEM((channels, rows, 2 * ports), jnp.bfloat16)],
+        functools.partial(beam_kernel, first_turn),
+        grid_spec=pltpu.PrefetchScalarGridSpec(
+            num_scalar_prefetch=1,
+            grid=(len(weights),),
+            in_specs=[pl.BlockSpec(memory_space=pltpu.VMEM)]
+            + [pl.BlockSpec(memory_space=pl.ANY)] * len(before)
+            + [whole] * len(weights),
+            out_specs=pl.BlockSpec(
+                (share, beams, 2, samples), lambda i, slab: (slab[0] ^ (i + first_turn), 0, 0, 0)
+            ),
+            scratch_shapes=[
+                pltpu.VMEM((len(weights) * share, rows * 2 // 3, 2 * ports), jnp.bfloat16)
+            ],
+        ),
         out_shape=jax.ShapeDtypeStruct((channels, beams, 2, samples), jnp.bfloat16),
+        input_output_aliases={} if formed is None else {2: 0},
         compiler_params=pltpu.CompilerParams(vmem_limit_bytes=VMEM_LIMIT),
-    )(slab, voltages, *weights)
+    )(slab, voltages, *before, *weights)
 
 
 def body(voltages, steering, beam_index, channel_flags):
@@ -443,7 +473,7 @@
     first_channel = (lax.axis_index("chan") * channel_count).astype(jnp.int32).reshape(1)
     chosen = chosen_vectors(slab, beam_index, steering, share, half, size)
     by_port = jnp.transpose(voltages, (0, 2, 1, 3))
-    across, inside, own, held = covariances(first_channel, channel_flags, by_port, size)
+    across, inside, own = covariances(first_channel, channel_flags, by_port, size)
     pairs = [[(i, i + 1) for i in range(start, blocks - 1, 2)] for start in range(2)]
     inside_pairs, across_pairs = [ahead + [(j, i) for i, j in ahead] for ahead in pairs]
     across = lax.ppermute(across, "chan", across_pairs)
@@ -457,10 +487,12 @@
         ]
 
     got = swap(sent)
+    held = held_voltages(by_port, mine)
     first_share = first_channel + slab * share
-    weights = solved_weights(first_share, channel_flags, mine, got, chosen, port_count, beam_count)
+    weights = solved_weights(first_share, channel_flags, held, mine, got, chosen, port_count, beam_count)
     others = swap([weights] * (slabs - 1))
-    beams = formed_beams(slab, held, [weights, *others], beam_count)
+    beams = formed_beams(slab, held, [weights], beam_count)
+    beams = formed_beams(slab, held, others, beam_count, beams)
     return jnp.transpose(beams, (0, 2, 1, 3))
 
 

time: 55.1 us -> 47 us (0.85)
  local copies, waits for them, and re-layouts: 7.2 us -> 0.02 us
  waiting for transfers between devices: 18.9 us -> 13.2 us
  Pallas kernels: 19.1 us -> 23.7 us
    unnamed x10 -> x6, local copies, waits for them, and re-layouts: 7.2 us -> 0.02 us
    ppermute x6, waiting for transfers between devices: 10.1 us -> 4.35 us  [swap(): lax.ppermute(array, 'slab', [(i, i ^ turn) for i in range(slabs)])]
    pallas_call x1 -> x3, Pallas kernels: 3.85 us -> 8.66 us  [the longest x2 4.93 us: formed_beams(): pl.pallas_call(functools.partial(beam_kernel, first_turn), grid_spec=pltp...]
  transfers between devices with their start and end apart: 8 -> 8, of which waited for: 6 -> 5; matrix products, arithmetic and copies ran while one was open for 0% -> 0% of each run, Pallas kernels for 1% -> 13%
where the time goes in v3:
time: 47 us; the launch traced here: 46.8 us
  Pallas kernels  23.7 us (50%)
  waiting for transfers between devices  13.2 us (28%)
  starting transfers between devices  9.78 us (21%)
    ppermute x1, waiting for transfers between devices, body(): across = lax.ppermute(across, 'chan', across_pairs)  8.89 us
    pallas_call x1, Pallas kernels, covariances(): pl.pallas_call(covariance_kernel, in_specs=[smem] + [pl.BlockSpec(memory_...  7.67 us
    ppermute x6, starting transfers between devices, swap(): lax.ppermute(array, 'slab', [(i, i ^ turn) for i in range(slabs)])  7.08 us
    pallas_call x1, Pallas kernels, solved_weights(): pl.pallas_call(functools.partial(solve_kernel, ports, beams), in_specs=[s...  6.52 us
    pallas_call x2, Pallas kernels, formed_beams(): pl.pallas_call(functools.partial(beam_kernel, first_turn), grid_spec=pltp...  4.93 us
    ppermute x6, waiting for transfers between devices, swap(): lax.ppermute(array, 'slab', [(i, i ^ turn) for i in range(slabs)])  4.35 us
    pallas_call x1, Pallas kernels, held_voltages(): pl.pallas_call(hold_kernel, in_specs=[pl.BlockSpec(memory_space=pltpu.HBM...  3.73 us
    ppermute x1, starting transfers between devices, body(): across = lax.ppermute(across, 'chan', across_pairs)  2.63 us
  transfers between devices with their start and end apart: 8, of which 5 were waited for; matrix products, arithmetic and copies ran while one was open for 0% of the time, Pallas kernels for 13%

profile of v3, /device:TPU:16, one launch (start us, length us, event | category | flops | bytes accessed | tf_op | source)
XLA Modules:
  0.0 46.8 jit_solution(12717672427802391968)
XLA Ops:
  0.0 7.7 %shard_map.46 = (bf16[8,288,128]{2,1,0:T(8,128)(2,1)}, bf16[8,288,128]{2,1,0:T(8,128)(2,1)}, f32[8,288,128]{2,1,0:T(8,128)S(1)}) custom-call(s32[1]{0:T(128)} %bitcast.2.first_ref, s32[64]{0:T(128)} %flags_ref.1, bf16[8,188,2,1536]{3,2,1,0:T(2,128)(2,1)} %bitcast.4), custom_call_target="tpu_custom_call" | custom-call | tf_op jit(solution)/shard_map/pallas_call | solution.py:158
  7.7 0.0 copy-start
  7.7 0.0 copy-start.2
  7.7 0.1 collective-permute-start
  7.8 2.6 %collective-permute-start.1 = (bf16[8,288,128]{2,1,0:T(8,128)(2,1)}, bf16[8,288,128]{2,1,0:T(8,128)(2,1)S(1)}, u32[]{:S(2)}, u32[]{:S(2)}) collective-permute-start(bf16[8,288,128]{2,1,0:T(8,128)(2,1)} %get-tuple-element.14), channel_id=1, source_target_pairs={{1,2},{3,4},{5,6},{2,1},{4,3},{6,5},{9,10},{11,12},{13,14},{10,9},... | collective-permute-start | bytes 1769480 | tf_op jit(solution)/shard_map/ppermute | solution.py:479
  10.4 0.0 collective-permute-done.inside_ref
  10.4 8.9 %collective-permute-done.1.across_ref = bf16[8,288,128]{2,1,0:T(8,128)(2,1)S(1)} collective-permute-done((bf16[8,288,128]{2,1,0:T(8,128)(2,1)}, bf16[8,288,128]{2,1,0:T(8,128)(2,1)S(1)}, u32[]{:S(2)}, u32[]{:S(2)}) %collective-permute-start.1) | collective-permute-done | bytes 589856 | tf_op jit(solution)/shard_map/ppermute | solution.py:479
  19.3 0.2 shard_map.47
  19.5 1.6 %collective-permute-start.2 = (bf16[2,288,128]{2,1,0:T(8,128)(2,1)S(1)}, bf16[2,288,128]{2,1,0:T(8,128)(2,1)S(1)}, u32[]{:S(2)}, u32[]{:S(2)}) collective-permute-start(bf16[2,288,128]{2,1,0:T(8,128)(2,1)S(1)} %get-tuple-element.16), channel_id=1, source_target_pairs={{0,8},{8,0},{16,24},{24,16},{1,9},{9,1},{17,25},{25,17},{2,10},{10... | collective-permute-start | bytes 442376 | tf_op jit(solution)/shard_map/ppermute | solution.py:485
  21.1 1.5 %collective-permute-start.3 = (bf16[2,288,128]{2,1,0:T(8,128)(2,1)S(1)}, bf16[2,288,128]{2,1,0:T(8,128)(2,1)S(1)}, u32[]{:S(2)}, u32[]{:S(2)}) collective-permute-start(bf16[2,288,128]{2,1,0:T(8,128)(2,1)S(1)} %get-tuple-element.17), channel_id=1, source_target_pairs={{0,16},{8,24},{16,0},{24,8},{1,17},{9,25},{17,1},{25,9},{2,18},{10... | collective-permute-start | bytes 442376 | tf_op jit(solution)/shard_map/ppermute | solution.py:485
  22.6 0.5 %collective-permute-start.4 = (bf16[2,288,128]{2,1,0:T(8,128)(2,1)S(1)}, bf16[2,288,128]{2,1,0:T(8,128)(2,1)S(1)}, u32[]{:S(2)}, u32[]{:S(2)}) collective-permute-start(bf16[2,288,128]{2,1,0:T(8,128)(2,1)S(1)} %get-tuple-element.18), channel_id=1, source_target_pairs={{0,24},{8,16},{16,8},{24,0},{1,25},{9,17},{17,9},{25,1},{2,26},{10... | collective-permute-start | bytes 442376 | tf_op jit(solution)/shard_map/ppermute | solution.py:485
  23.1 0.0 copy-done
  23.1 0.0 copy-done.2
  23.1 0.7 %shard_map.49.refs_4_ = f32[2,80,192]{2,1,0:T(8,128)S(1)} custom-call(s32[1]{0:T(128)} %bitcast.slab_ref, s32[36]{0:T(128)S(1)} %copy-done.2, f32[8,2,64,188]{3,2,1,0:T(8,128)S(1)} %copy-done), custom_call_target="tpu_custom_call" | custom-call | tf_op jit(solution)/shard_map/pallas_call | solution.py:219
  23.7 0.0 copy-start.1
  23.8 3.7 %shard_map.48.held_ref.volt_ref = bf16[8,188,2,1536]{3,2,1,0:T(2,128)(2,1)S(1)} custom-call(bf16[8,188,2,1536]{3,2,1,0:T(2,128)(2,1)} %bitcast.5, f32[2,288,128]{2,1,0:T(8,128)S(1)} %get-tuple-element.15.weight_hbm.refs_0_), custom_call_target="tpu_custom_call" | custom-call | tf_op jit(solution)/shard_map/pallas_call | solution.py:395
  27.5 0.0 collective-permute-done.2.refs_1_
  27.5 2.5 %collective-permute-done.3.refs_2_ = bf16[2,288,128]{2,1,0:T(8,128)(2,1)S(1)} collective-permute-done((bf16[2,288,128]{2,1,0:T(8,128)(2,1)S(1)}, bf16[2,288,128]{2,1,0:T(8,128)(2,1)S(1)}, u32[]{:S(2)}, u32[]{:S(2)}) %collective-permute-start.3) | collective-permute-done | bytes 147488 | tf_op jit(solution)/shard_map/ppermute | solution.py:485
  30.0 0.0 collective-permute-done.4.refs_3_
  30.1 0.0 copy-done.1
  30.1 6.5 %shard_map.50.refs_0_ = bf16[2,120,128]{2,1,0:T(8,128)(2,1)S(1)} custom-call(s32[1]{0:T(128)S(6)} %add.3.first_ref, s32[64]{0:T(128)S(1)} %copy-done.1, bf16[8,188,2,1536]{3,2,1,0:T(2,128)(2,1)S(1)} %shard_map.48.held_ref.volt_ref, f32[2,288,128]{2,1,0:T(8,128)S(1)} %get-tuple-element.15.weight_hbm.refs_0_, ...), custom_call_target="tpu_custom_call" | custom-call | tf_op jit(solution)/shard_map/pallas_call | solution.py:374
  36.6 1.5 %collective-permute-start.7 = (bf16[2,120,128]{2,1,0:T(8,128)(2,1)S(1)}, bf16[2,120,128]{2,1,0:T(8,128)(2,1)S(1)}, u32[]{:S(2)}, u32[]{:S(2)}) collective-permute-start(bf16[2,120,128]{2,1,0:T(8,128)(2,1)S(1)} %shard_map.50.refs_0_), channel_id=1, source_target_pairs={{0,24},{8,16},{16,8},{24,0},{1,25},{9,17},{17,9},{25,1},{2,26},{10... | collective-permute-start | bytes 184328 | tf_op jit(solution)/shard_map/ppermute | solution.py:485
  38.1 1.2 %collective-permute-start.6 = (bf16[2,120,128]{2,1,0:T(8,128)(2,1)S(1)}, bf16[2,120,128]{2,1,0:T(8,128)(2,1)S(1)}, u32[]{:S(2)}, u32[]{:S(2)}) collective-permute-start(bf16[2,120,128]{2,1,0:T(8,128)(2,1)S(1)} %shard_map.50.refs_0_), channel_id=1, source_target_pairs={{0,16},{8,24},{16,0},{24,8},{1,17},{9,25},{17,1},{25,9},{2,18},{10... | collective-permute-start | bytes 184328 | tf_op jit(solution)/shard_map/ppermute | solution.py:485
  39.3 0.8 %collective-permute-start.5 = (bf16[2,120,128]{2,1,0:T(8,128)(2,1)S(1)}, bf16[2,120,128]{2,1,0:T(8,128)(2,1)S(1)}, u32[]{:S(2)}, u32[]{:S(2)}) collective-permute-start(bf16[2,120,128]{2,1,0:T(8,128)(2,1)S(1)} %shard_map.50.refs_0_), channel_id=1, source_target_pairs={{0,8},{8,0},{16,24},{24,16},{1,9},{9,1},{17,25},{25,17},{2,10},{10... | collective-permute-start | bytes 184328 | tf_op jit(solution)/shard_map/ppermute | solution.py:485
  40.1 1.6 %shard_map.51.refs_0_ = bf16[8,36,2,1536]{3,2,1,0:T(2,128)(2,1)} custom-call(s32[1]{0:T(128)} %bitcast.slab_ref, bf16[8,188,2,1536]{3,2,1,0:T(2,128)(2,1)S(1)} %shard_map.48.held_ref.volt_ref, bf16[2,120,128]{2,1,0:T(8,128)(2,1)S(1)} %shard_map.50.refs_0_), custom_call_target="tpu_custom_call" | custom-call | tf_op jit(solution)/shard_map/pallas_call | solution.py:442
  41.7 0.6 %collective-permute-done.7.refs_3_ = bf16[2,120,128]{2,1,0:T(8,128)(2,1)S(1)} collective-permute-done((bf16[2,120,128]{2,1,0:T(8,128)(2,1)S(1)}, bf16[2,120,128]{2,1,0:T(8,128)(2,1)S(1)}, u32[]{:S(2)}, u32[]{:S(2)}) %collective-permute-start.7) | collective-permute-done | bytes 61472 | tf_op jit(solution)/shard_map/ppermute | solution.py:485
  42.3 0.4 collective-permute-done.6.refs_2_
  42.7 0.8 %collective-permute-done.5.refs_1_ = bf16[2,120,128]{2,1,0:T(8,128)(2,1)S(1)} collective-permute-done((bf16[2,120,128]{2,1,0:T(8,128)(2,1)S(1)}, bf16[2,120,128]{2,1,0:T(8,128)(2,1)S(1)}, u32[]{:S(2)}, u32[]{:S(2)}) %collective-permute-start.5) | collective-permute-done | bytes 61472 | tf_op jit(solution)/shard_map/ppermute | solution.py:485
  43.5 3.3 %shard_map.52 = bf16[8,36,2,1536]{3,2,1,0:T(2,128)(2,1)} custom-call(s32[1]{0:T(128)} %bitcast.slab_ref, bf16[8,188,2,1536]{3,2,1,0:T(2,128)(2,1)S(1)} %shard_map.48.held_ref.volt_ref, bf16[8,36,2,1536]{3,2,1,0:T(2,128)(2,1)} %shard_map.51.refs_0_, bf16[2,120,128]{2,1,0:T(8,128)(2,1)S(1)} %collective-permute-done.5.refs_1_, ...), custom_call_target="tpu_custom_call", output_to_operand_aliasing={{}: (2, {})} | custom-call | tf_op jit(solution)/shard_map/pallas_call | solution.py:442
Async XLA Ops:
  7.7 15.4 %copy-start = (f32[8,2,64,188]{3,2,1,0:T(8,128)S(1)}, f32[8,2,64,188]{3,2,1,0:T(8,128)}, u32[]{:S(2)}) copy-start(f32[8,2,64,188]{3,2,1,0:T(8,128)} %steer_ref.1) | copy-start | bytes 2310148
  7.7 15.4 %copy-start.2 = (s32[36]{0:T(128)S(1)}, s32[36]{0:T(128)}, u32[]{:S(2)}) copy-start(s32[36]{0:T(128)} %index_ref.1) | copy-start | bytes 436
  7.7 2.7 %collective-permute-start = (bf16[8,288,128]{2,1,0:T(8,128)(2,1)}, bf16[8,288,128]{2,1,0:T(8,128)(2,1)S(1)}, u32[]{:S(2)}, u32[]{:S(2)}) collective-permute-start(bf16[8,288,128]{2,1,0:T(8,128)(2,1)} %get-tuple-element.13), channel_id=1, source_target_pairs={{0,1},{2,3},{4,5},{6,7},{1,0},{3,2},{5,4},{7,6},{8,9},{10,11},{12,... | collective-permute-start | bytes 1769480 | tf_op jit(solution)/shard_map/ppermute | solution.py:480
  7.8 11.5 %collective-permute-start.1 = (bf16[8,288,128]{2,1,0:T(8,128)(2,1)}, bf16[8,288,128]{2,1,0:T(8,128)(2,1)S(1)}, u32[]{:S(2)}, u32[]{:S(2)}) collective-permute-start(bf16[8,288,128]{2,1,0:T(8,128)(2,1)} %get-tuple-element.14), channel_id=1, source_target_pairs={{1,2},{3,4},{5,6},{2,1},{4,3},{6,5},{9,10},{11,12},{13,14},{10,9},... | collective-permute-start | bytes 1769480 | tf_op jit(solution)/shard_map/ppermute | solution.py:479
  19.5 8.0 %collective-permute-start.2 = (bf16[2,288,128]{2,1,0:T(8,128)(2,1)S(1)}, bf16[2,288,128]{2,1,0:T(8,128)(2,1)S(1)}, u32[]{:S(2)}, u32[]{:S(2)}) collective-permute-start(bf16[2,288,128]{2,1,0:T(8,128)(2,1)S(1)} %get-tuple-element.16), channel_id=1, source_target_pairs={{0,8},{8,0},{16,24},{24,16},{1,9},{9,1},{17,25},{25,17},{2,10},{10... | collective-permute-start | bytes 442376 | tf_op jit(solution)/shard_map/ppermute | solution.py:485
  21.1 9.0 %collective-permute-start.3 = (bf16[2,288,128]{2,1,0:T(8,128)(2,1)S(1)}, bf16[2,288,128]{2,1,0:T(8,128)(2,1)S(1)}, u32[]{:S(2)}, u32[]{:S(2)}) collective-permute-start(bf16[2,288,128]{2,1,0:T(8,128)(2,1)S(1)} %get-tuple-element.17), channel_id=1, source_target_pairs={{0,16},{8,24},{16,0},{24,8},{1,17},{9,25},{17,1},{25,9},{2,18},{10... | collective-permute-start | bytes 442376 | tf_op jit(solution)/shard_map/ppermute | solution.py:485
  22.6 7.5 %collective-permute-start.4 = (bf16[2,288,128]{2,1,0:T(8,128)(2,1)S(1)}, bf16[2,288,128]{2,1,0:T(8,128)(2,1)S(1)}, u32[]{:S(2)}, u32[]{:S(2)}) collective-permute-start(bf16[2,288,128]{2,1,0:T(8,128)(2,1)S(1)} %get-tuple-element.18), channel_id=1, source_target_pairs={{0,24},{8,16},{16,8},{24,0},{1,25},{9,17},{17,9},{25,1},{2,26},{10... | collective-permute-start | bytes 442376 | tf_op jit(solution)/shard_map/ppermute | solution.py:485
  23.7 6.3 %copy-start.1 = (s32[64]{0:T(128)S(1)}, s32[64]{0:T(128)}, u32[]{:S(2)}) copy-start(s32[64]{0:T(128)} %flags_ref.1) | copy-start | bytes 772
  36.6 5.7 %collective-permute-start.7 = (bf16[2,120,128]{2,1,0:T(8,128)(2,1)S(1)}, bf16[2,120,128]{2,1,0:T(8,128)(2,1)S(1)}, u32[]{:S(2)}, u32[]{:S(2)}) collective-permute-start(bf16[2,120,128]{2,1,0:T(8,128)(2,1)S(1)} %shard_map.50.refs_0_), channel_id=1, source_target_pairs={{0,24},{8,16},{16,8},{24,0},{1,25},{9,17},{17,9},{25,1},{2,26},{10... | collective-permute-start | bytes 184328 | tf_op jit(solution)/shard_map/ppermute | solution.py:485
  38.1 4.6 %collective-permute-start.6 = (bf16[2,120,128]{2,1,0:T(8,128)(2,1)S(1)}, bf16[2,120,128]{2,1,0:T(8,128)(2,1)S(1)}, u32[]{:S(2)}, u32[]{:S(2)}) collective-permute-start(bf16[2,120,128]{2,1,0:T(8,128)(2,1)S(1)} %shard_map.50.refs_0_), channel_id=1, source_target_pairs={{0,16},{8,24},{16,0},{24,8},{1,17},{9,25},{17,1},{25,9},{2,18},{10... | collective-permute-start | bytes 184328 | tf_op jit(solution)/shard_map/ppermute | solution.py:485
  39.3 4.2 %collective-permute-start.5 = (bf16[2,120,128]{2,1,0:T(8,128)(2,1)S(1)}, bf16[2,120,128]{2,1,0:T(8,128)(2,1)S(1)}, u32[]{:S(2)}, u32[]{:S(2)}) collective-permute-start(bf16[2,120,128]{2,1,0:T(8,128)(2,1)S(1)} %shard_map.50.refs_0_), channel_id=1, source_target_pairs={{0,8},{8,0},{16,24},{24,16},{1,9},{9,1},{17,25},{25,17},{2,10},{10... | collective-permute-start | bytes 184328 | tf_op jit(solution)/shard_map/ppermute | solution.py:485

commit v4 on v3

--- a/solution.py
+++ b/solution.py
@@ -98,7 +98,8 @@
     flags_hbm,
     volt_hbm,
     across_ref,
-    inside_ref,
+    inside_lead_ref,
+    inside_rest_ref,
     own_ref,
     volts,
     lefts,
@@ -109,6 +110,7 @@
     flags_sem,
 ):
     channels, ports, _, samples = volts.shape
+    half = inside_lead_ref.shape[0]
     copies = [
         pltpu.make_async_copy(volt_hbm.at[c], volts.at[c], sems.at[c]) for c in range(channels)
     ]
@@ -146,19 +148,24 @@
         for c in range(channels):
             up, down = onward[channels - 1 - c], up_to[c]
             across_ref[c, part] = jnp.where(odd_block, up, down).astype(across_ref.dtype)
-            inside_ref[c, part] = jnp.where(odd_block, down, up).astype(inside_ref.dtype)
+            inside = jnp.where(odd_block, down, up).astype(across_ref.dtype)
+            if c < half:
+                inside_lead_ref[c, part] = inside
+            else:
+                inside_rest_ref[c - half, part] = inside
             own_ref[c, part] = up_to[-1] + (1.0 - flags[c]) * plain[c]
 
 
 def covariances(first, flags, voltages, size):
     channels, ports, _, samples = voltages.shape
     folded = (channels, size + size // 2, LANES)
+    half = channels // 2
     smem = pl.BlockSpec(memory_space=pltpu.SMEM)
     vmem = pl.BlockSpec(memory_space=pltpu.VMEM)
     return pl.pallas_call(
         covariance_kernel,
         in_specs=[smem] + [pl.BlockSpec(memory_space=pltpu.HBM)] * 2,
-        out_specs=[vmem] * 3,
+        out_specs=[vmem] * 4,
         scratch_shapes=[
             pltpu.VMEM(voltages.shape, voltages.dtype),
             pltpu.VMEM((4, 2, 2 * size, LANES), jnp.float32),
@@ -170,37 +177,44 @@
         ],
         out_shape=[
             pltpu.VMEM(folded, jnp.bfloat16),
-            pltpu.VMEM(folded, jnp.bfloat16),
+            pltpu.VMEM((half, *folded[1:]), jnp.bfloat16),
+            pltpu.VMEM((channels - half, *folded[1:]), jnp.bfloat16),
             pltpu.VMEM(folded, jnp.float32),
         ],
         compiler_params=pltpu.CompilerParams(vmem_limit_bytes=VMEM_LIMIT),
     )(first, *[pltpu.with_memory_space_constraint(a, pltpu.HBM) for a in (flags, voltages)])
 
 
-def window_kernel(slab_ref, own_ref, inside_ref, across_ref, mine_ref, *sent_refs):
+def window_kernel(slab_ref, own_ref, across_ref, inside_lead_ref, inside_rest_ref, *refs):
+    mine_ref, *sent_refs, sums = refs
     share = mine_ref.shape[0]
+    half = inside_lead_ref.shape[0]
+    for c in range(own_ref.shape[0]):
+        inside = inside_lead_ref[c] if c < half else inside_rest_ref[c - half]
+        ends = inside.astype(jnp.float32) + across_ref[c].astype(jnp.float32)
+        sums[c] = own_ref[c] + ends
 
     def window(slab):
-        rows = pl.ds(slab * share, share)
-        ends = inside_ref[rows].astype(jnp.float32) + across_ref[rows].astype(jnp.float32)
-        return own_ref[rows] + ends
+        return sums[pl.ds(slab * share, share)]
 
     mine_ref[...] = window(slab_ref[0])
     for turn, sent_ref in enumerate(sent_refs, 1):
         sent_ref[...] = window(slab_ref[0] ^ turn).astype(sent_ref.dtype)
 
 
-def windows(slab, own, inside, across, slabs):
+def windows(slab, own, across, inside_lead, inside_rest, slabs):
+    arrays = own, across, inside_lead, inside_rest
     shape = (own.shape[0] // slabs,) + own.shape[1:]
     return pl.pallas_call(
         window_kernel,
         in_specs=[pl.BlockSpec(memory_space=pltpu.SMEM)]
-        + [pl.BlockSpec(own.shape, lambda: (0, 0, 0))] * 3,
+        + [pl.BlockSpec(a.shape, lambda: (0, 0, 0)) for a in arrays],
         out_specs=[pl.BlockSpec(shape, lambda: (0, 0, 0))] * slabs,
         out_shape=[jax.ShapeDtypeStruct(shape, jnp.float32)]
         + [jax.ShapeDtypeStruct(shape, jnp.bfloat16)] * (slabs - 1),
+        scratch_shapes=[pltpu.VMEM(own.shape, jnp.float32)],
         compiler_params=pltpu.CompilerParams(vmem_limit_bytes=VMEM_LIMIT),
-    )(slab, own, inside, across)
+    )(slab, *arrays)
 
 
 def choose_kernel(slab_ref, index_ref, steer_ref, out_ref):
@@ -280,22 +294,21 @@
     half = n // 2
     (rh, rl), (ih, il), (yh, yl) = split(real), split(imag), split(y)
     if squares:
-        by_rh, by_rl = dot_nn(stack(yh, yl, rh, rl), rh), dot_nn(stack(yh, rh), rl)
-        by_ih, by_il = dot_nn(stack(yh, yl, ih, il), ih), dot_nn(stack(yh, ih, rh), il)
-        cross = dot_nn(stack(rh, rl), ih)
+        by_rh, by_rl = dot_nn(stack(yh, yl, rh), rh), dot_nn(stack(yh, rh), rl)
+        by_ih, by_il = dot_nn(stack(yh, yl, ih), ih), dot_nn(yh, il)
     else:
         by_rh, by_rl = dot_nn(stack(yh, yl), rh), dot_nn(yh, rl)
         by_ih, by_il = dot_nn(stack(yh, yl), ih), dot_nn(yh, il)
     with_real = by_rh[:n] + by_rh[n : 2 * n] + by_rl[:n]
-    with_imag = by_ih[:n] + by_ih[n : 2 * n] + by_il[:n]
+    with_imag = by_ih[:n] + by_ih[n : 2 * n] + by_il
     product = stack(with_real[:half] + with_imag[half:], with_real[half:] - with_imag[:half])
     if not squares:
         return product, None, None
-    by_rh, by_rl, by_ih, by_il = by_rh[2 * n :], by_rl[n:], by_ih[2 * n :], by_il[n:]
-    rr = by_rh[:m] + by_rh[m:] + by_rl
-    ii = by_ih[:m] + by_ih[m:] + by_il[:m]
-    ri = cross[:m] + cross[m:] + by_il[m:]
-    return product, rr - ii, ri - ri.T
+    cross = dot_nn(stack(rh, rl), ih)
+    mixed = by_rl[n:] - dot_nn(ih, il)
+    rr_less_ii = by_rh[2 * n :] - by_ih[2 * n :] + (mixed + mixed.T)
+    ri = cross[:m] + cross[m:] + dot_nn(rh, il)
+    return product, rr_less_ii, ri - ri.T
 
 
 def multiply_once(y, real, imag, squares):
@@ -473,12 +486,12 @@
     first_channel = (lax.axis_index("chan") * channel_count).astype(jnp.int32).reshape(1)
     chosen = chosen_vectors(slab, beam_index, steering, share, half, size)
     by_port = jnp.transpose(voltages, (0, 2, 1, 3))
-    across, inside, own = covariances(first_channel, channel_flags, by_port, size)
+    across, *inside, own = covariances(first_channel, channel_flags, by_port, size)
     pairs = [[(i, i + 1) for i in range(start, blocks - 1, 2)] for start in range(2)]
     inside_pairs, across_pairs = [ahead + [(j, i) for i, j in ahead] for ahead in pairs]
     across = lax.ppermute(across, "chan", across_pairs)
-    inside = lax.ppermute(inside, "chan", inside_pairs)
-    mine, *sent = windows(slab, own, inside, across, slabs)
+    inside = [lax.ppermute(part, "chan", inside_pairs) for part in inside]
+    mine, *sent = windows(slab, own, across, *inside, slabs)
 
     def swap(arrays):
         return [

time: 47 us -> 46 us (0.979)
  waiting for transfers between devices: 13.2 us -> 11.6 us
  starting transfers between devices: 9.78 us -> 11.1 us
  Pallas kernels: 23.7 us -> 23.1 us
    ppermute x1, waiting for transfers between devices: 8.89 us -> 5.71 us  [body(): across = lax.ppermute(across, 'chan', across_pairs)]
    ppermute x1 -> x2, waiting for transfers between devices: 0.01 us -> 1.76 us  [body(): inside = [lax.ppermute(part, 'chan', inside_pairs) for part in inside]]
    ppermute x1 -> x2, starting transfers between devices: 0.07 us -> 1.83 us  [body(): inside = [lax.ppermute(part, 'chan', inside_pairs) for part in inside]]
    pallas_call x1, Pallas kernels: 6.52 us -> 5.87 us  [solved_weights(): pl.pallas_call(functools.partial(solve_kernel, ports, beams), in_specs=[s...]
  transfers between devices with their start and end apart: 8 -> 9, of which waited for: 5 -> 7; matrix products, arithmetic and copies ran while one was open for 0% -> 0% of each run, Pallas kernels for 13% -> 13%
where the time goes in v4:
time: 46 us; the launch traced here: 45.9 us
  Pallas kernels  23.1 us (50%)
  waiting for transfers between devices  11.6 us (25%)
  starting transfers between devices  11.1 us (24%)
    pallas_call x1, Pallas kernels, covariances(): pl.pallas_call(covariance_kernel, in_specs=[smem] + [pl.BlockSpec(memory_...  7.6 us
    ppermute x6, starting transfers between devices, swap(): lax.ppermute(array, 'slab', [(i, i ^ turn) for i in range(slabs)])  7.08 us
    pallas_call x1, Pallas kernels, solved_weights(): pl.pallas_call(functools.partial(solve_kernel, ports, beams), in_specs=[s...  5.87 us
    ppermute x1, waiting for transfers between devices, body(): across = lax.ppermute(across, 'chan', across_pairs)  5.71 us
    pallas_call x2, Pallas kernels, formed_beams(): pl.pallas_call(functools.partial(beam_kernel, first_turn), grid_spec=pltp...  4.93 us
    ppermute x6, waiting for transfers between devices, swap(): lax.ppermute(array, 'slab', [(i, i ^ turn) for i in range(slabs)])  4.11 us
    pallas_call x1, Pallas kernels, held_voltages(): pl.pallas_call(hold_kernel, in_specs=[pl.BlockSpec(memory_space=pltpu.HBM...  3.73 us
    ppermute x1, starting transfers between devices, body(): across = lax.ppermute(across, 'chan', across_pairs)  2.23 us
  transfers between devices with their start and end apart: 9, of which 7 were waited for; matrix products, arithmetic and copies ran while one was open for 0% of the time, Pallas kernels for 13%

profile of v4, /device:TPU:16, one launch (start us, length us, event | category | flops | bytes accessed | tf_op | source)
XLA Modules:
  0.0 45.9 jit_solution(7101637496951131024)
XLA Ops:
  0.0 7.6 %shard_map.46 = (bf16[8,288,128]{2,1,0:T(8,128)(2,1)}, bf16[4,288,128]{2,1,0:T(8,128)(2,1)}, bf16[4,288,128]{2,1,0:T(8,128)(2,1)}, f32[8,288,128]{2,1,0:T(8,128)S(1)}) custom-call(s32[1]{0:T(128)} %bitcast.2.first_ref, s32[64]{0:T(128)} %flags_ref.1, bf16[8,188,2,1536]{3,2,1,0:T(2,128)(2,1)} %bitcast.4), custom_call_target="tpu_custom_call" | custom-call | tf_op jit(solution)/shard_map/pallas_call | solution.py:165
  7.6 0.0 copy-start
  7.6 0.0 copy-start.2
  7.6 2.2 %collective-permute-start = (bf16[8,288,128]{2,1,0:T(8,128)(2,1)}, bf16[8,288,128]{2,1,0:T(8,128)(2,1)S(1)}, u32[]{:S(2)}, u32[]{:S(2)}) collective-permute-start(bf16[8,288,128]{2,1,0:T(8,128)(2,1)} %get-tuple-element.14), channel_id=1, source_target_pairs={{1,2},{3,4},{5,6},{2,1},{4,3},{6,5},{9,10},{11,12},{13,14},{10,9},... | collective-permute-start | bytes 1769480 | tf_op jit(solution)/shard_map/ppermute | solution.py:492
  9.9 1.7 %collective-permute-start.1 = (bf16[4,288,128]{2,1,0:T(8,128)(2,1)}, bf16[4,288,128]{2,1,0:T(8,128)(2,1)S(1)}, u32[]{:S(2)}, u32[]{:S(2)}) collective-permute-start(bf16[4,288,128]{2,1,0:T(8,128)(2,1)} %get-tuple-element.15), channel_id=1, source_target_pairs={{0,1},{2,3},{4,5},{6,7},{1,0},{3,2},{5,4},{7,6},{8,9},{10,11},{12,... | collective-permute-start | bytes 884744 | tf_op jit(solution)/shard_map/ppermute | solution.py:493
  11.6 0.1 collective-permute-start.2
  11.7 1.3 %collective-permute-done.1.inside_lead_ref = bf16[4,288,128]{2,1,0:T(8,128)(2,1)S(1)} collective-permute-done((bf16[4,288,128]{2,1,0:T(8,128)(2,1)}, bf16[4,288,128]{2,1,0:T(8,128)(2,1)S(1)}, u32[]{:S(2)}, u32[]{:S(2)}) %collective-permute-start.1) | collective-permute-done | bytes 294944 | tf_op jit(solution)/shard_map/ppermute | solution.py:493
  13.0 0.4 collective-permute-done.2.inside_rest_ref
  13.5 5.7 %collective-permute-done.across_ref = bf16[8,288,128]{2,1,0:T(8,128)(2,1)S(1)} collective-permute-done((bf16[8,288,128]{2,1,0:T(8,128)(2,1)}, bf16[8,288,128]{2,1,0:T(8,128)(2,1)S(1)}, u32[]{:S(2)}, u32[]{:S(2)}) %collective-permute-start) | collective-permute-done | bytes 589856 | tf_op jit(solution)/shard_map/ppermute | solution.py:492
  19.2 0.3 shard_map.47
  19.4 1.6 %collective-permute-start.3 = (bf16[2,288,128]{2,1,0:T(8,128)(2,1)S(1)}, bf16[2,288,128]{2,1,0:T(8,128)(2,1)S(1)}, u32[]{:S(2)}, u32[]{:S(2)}) collective-permute-start(bf16[2,288,128]{2,1,0:T(8,128)(2,1)S(1)} %get-tuple-element.18), channel_id=1, source_target_pairs={{0,8},{8,0},{16,24},{24,16},{1,9},{9,1},{17,25},{25,17},{2,10},{10... | collective-permute-start | bytes 442376 | tf_op jit(solution)/shard_map/ppermute | solution.py:498
  21.0 1.5 %collective-permute-start.4 = (bf16[2,288,128]{2,1,0:T(8,128)(2,1)S(1)}, bf16[2,288,128]{2,1,0:T(8,128)(2,1)S(1)}, u32[]{:S(2)}, u32[]{:S(2)}) collective-permute-start(bf16[2,288,128]{2,1,0:T(8,128)(2,1)S(1)} %get-tuple-element.19), channel_id=1, source_target_pairs={{0,16},{8,24},{16,0},{24,8},{1,17},{9,25},{17,1},{25,9},{2,18},{10... | collective-permute-start | bytes 442376 | tf_op jit(solution)/shard_map/ppermute | solution.py:498
  22.5 0.5 %collective-permute-start.5 = (bf16[2,288,128]{2,1,0:T(8,128)(2,1)S(1)}, bf16[2,288,128]{2,1,0:T(8,128)(2,1)S(1)}, u32[]{:S(2)}, u32[]{:S(2)}) collective-permute-start(bf16[2,288,128]{2,1,0:T(8,128)(2,1)S(1)} %get-tuple-element.20), channel_id=1, source_target_pairs={{0,24},{8,16},{16,8},{24,0},{1,25},{9,17},{17,9},{25,1},{2,26},{10... | collective-permute-start | bytes 442376 | tf_op jit(solution)/shard_map/ppermute | solution.py:498
  23.0 0.0 copy-done
  23.0 0.0 copy-done.2
  23.0 0.7 %shard_map.49.refs_4_ = f32[2,80,192]{2,1,0:T(8,128)S(1)} custom-call(s32[1]{0:T(128)} %bitcast.slab_ref, s32[36]{0:T(128)S(1)} %copy-done.2, f32[8,2,64,188]{3,2,1,0:T(8,128)S(1)} %copy-done), custom_call_target="tpu_custom_call" | custom-call | tf_op jit(solution)/shard_map/pallas_call | solution.py:233
  23.7 0.0 copy-start.1
  23.7 3.7 %shard_map.48.held_ref.volt_ref = bf16[8,188,2,1536]{3,2,1,0:T(2,128)(2,1)S(1)} custom-call(bf16[8,188,2,1536]{3,2,1,0:T(2,128)(2,1)} %bitcast.5, f32[2,288,128]{2,1,0:T(8,128)S(1)} %get-tuple-element.17.weight_hbm.refs_0_), custom_call_target="tpu_custom_call" | custom-call | tf_op jit(solution)/shard_map/pallas_call | solution.py:408
  27.4 0.0 collective-permute-done.3.refs_1_
  27.5 2.3 %collective-permute-done.4.refs_2_ = bf16[2,288,128]{2,1,0:T(8,128)(2,1)S(1)} collective-permute-done((bf16[2,288,128]{2,1,0:T(8,128)(2,1)S(1)}, bf16[2,288,128]{2,1,0:T(8,128)(2,1)S(1)}, u32[]{:S(2)}, u32[]{:S(2)}) %collective-permute-start.4) | collective-permute-done | bytes 147488 | tf_op jit(solution)/shard_map/ppermute | solution.py:498
  29.8 0.0 collective-permute-done.5.refs_3_
  29.8 0.0 copy-done.1
  29.8 5.9 %shard_map.50.refs_0_ = bf16[2,120,128]{2,1,0:T(8,128)(2,1)S(1)} custom-call(s32[1]{0:T(128)S(6)} %add.3.first_ref, s32[64]{0:T(128)S(1)} %copy-done.1, bf16[8,188,2,1536]{3,2,1,0:T(2,128)(2,1)S(1)} %shard_map.48.held_ref.volt_ref, f32[2,288,128]{2,1,0:T(8,128)S(1)} %get-tuple-element.17.weight_hbm.refs_0_, ...), custom_call_target="tpu_custom_call" | custom-call | tf_op jit(solution)/shard_map/pallas_call | solution.py:387
  35.6 1.5 %collective-permute-start.8 = (bf16[2,120,128]{2,1,0:T(8,128)(2,1)S(1)}, bf16[2,120,128]{2,1,0:T(8,128)(2,1)S(1)}, u32[]{:S(2)}, u32[]{:S(2)}) collective-permute-start(bf16[2,120,128]{2,1,0:T(8,128)(2,1)S(1)} %shard_map.50.refs_0_), channel_id=1, source_target_pairs={{0,24},{8,16},{16,8},{24,0},{1,25},{9,17},{17,9},{25,1},{2,26},{10... | collective-permute-start | bytes 184328 | tf_op jit(solution)/shard_map/ppermute | solution.py:498
  37.2 1.2 %collective-permute-start.7 = (bf16[2,120,128]{2,1,0:T(8,128)(2,1)S(1)}, bf16[2,120,128]{2,1,0:T(8,128)(2,1)S(1)}, u32[]{:S(2)}, u32[]{:S(2)}) collective-permute-start(bf16[2,120,128]{2,1,0:T(8,128)(2,1)S(1)} %shard_map.50.refs_0_), channel_id=1, source_target_pairs={{0,16},{8,24},{16,0},{24,8},{1,17},{9,25},{17,1},{25,9},{2,18},{10... | collective-permute-start | bytes 184328 | tf_op jit(solution)/shard_map/ppermute | solution.py:498
  38.4 0.8 %collective-permute-start.6 = (bf16[2,120,128]{2,1,0:T(8,128)(2,1)S(1)}, bf16[2,120,128]{2,1,0:T(8,128)(2,1)S(1)}, u32[]{:S(2)}, u32[]{:S(2)}) collective-permute-start(bf16[2,120,128]{2,1,0:T(8,128)(2,1)S(1)} %shard_map.50.refs_0_), channel_id=1, source_target_pairs={{0,8},{8,0},{16,24},{24,16},{1,9},{9,1},{17,25},{25,17},{2,10},{10... | collective-permute-start | bytes 184328 | tf_op jit(solution)/shard_map/ppermute | solution.py:498
  39.2 1.6 %shard_map.51.refs_0_ = bf16[8,36,2,1536]{3,2,1,0:T(2,128)(2,1)} custom-call(s32[1]{0:T(128)} %bitcast.slab_ref, bf16[8,188,2,1536]{3,2,1,0:T(2,128)(2,1)S(1)} %shard_map.48.held_ref.volt_ref, bf16[2,120,128]{2,1,0:T(8,128)(2,1)S(1)} %shard_map.50.refs_0_), custom_call_target="tpu_custom_call" | custom-call | tf_op jit(solution)/shard_map/pallas_call | solution.py:455
  40.8 0.2 collective-permute-done.8.refs_3_
  41.0 0.6 %collective-permute-done.7.refs_2_ = bf16[2,120,128]{2,1,0:T(8,128)(2,1)S(1)} collective-permute-done((bf16[2,120,128]{2,1,0:T(8,128)(2,1)S(1)}, bf16[2,120,128]{2,1,0:T(8,128)(2,1)S(1)}, u32[]{:S(2)}, u32[]{:S(2)}) %collective-permute-start.7) | collective-permute-done | bytes 61472 | tf_op jit(solution)/shard_map/ppermute | solution.py:498
  41.6 0.9 %collective-permute-done.6.refs_1_ = bf16[2,120,128]{2,1,0:T(8,128)(2,1)S(1)} collective-permute-done((bf16[2,120,128]{2,1,0:T(8,128)(2,1)S(1)}, bf16[2,120,128]{2,1,0:T(8,128)(2,1)S(1)}, u32[]{:S(2)}, u32[]{:S(2)}) %collective-permute-start.6) | collective-permute-done | bytes 61472 | tf_op jit(solution)/shard_map/ppermute | solution.py:498
  42.6 3.3 %shard_map.52 = bf16[8,36,2,1536]{3,2,1,0:T(2,128)(2,1)} custom-call(s32[1]{0:T(128)} %bitcast.slab_ref, bf16[8,188,2,1536]{3,2,1,0:T(2,128)(2,1)S(1)} %shard_map.48.held_ref.volt_ref, bf16[8,36,2,1536]{3,2,1,0:T(2,128)(2,1)} %shard_map.51.refs_0_, bf16[2,120,128]{2,1,0:T(8,128)(2,1)S(1)} %collective-permute-done.6.refs_1_, ...), custom_call_target="tpu_custom_call", output_to_operand_aliasing={{}: (2, {})} | custom-call | tf_op jit(solution)/shard_map/pallas_call | solution.py:455
Async XLA Ops:
  7.6 15.4 %copy-start = (f32[8,2,64,188]{3,2,1,0:T(8,128)S(1)}, f32[8,2,64,188]{3,2,1,0:T(8,128)}, u32[]{:S(2)}) copy-start(f32[8,2,64,188]{3,2,1,0:T(8,128)} %steer_ref.1) | copy-start | bytes 2310148
  7.6 15.4 %copy-start.2 = (s32[36]{0:T(128)S(1)}, s32[36]{0:T(128)}, u32[]{:S(2)}) copy-start(s32[36]{0:T(128)} %index_ref.1) | copy-start | bytes 436
  7.6 11.5 %collective-permute-start = (bf16[8,288,128]{2,1,0:T(8,128)(2,1)}, bf16[8,288,128]{2,1,0:T(8,128)(2,1)S(1)}, u32[]{:S(2)}, u32[]{:S(2)}) collective-permute-start(bf16[8,288,128]{2,1,0:T(8,128)(2,1)} %get-tuple-element.14), channel_id=1, source_target_pairs={{1,2},{3,4},{5,6},{2,1},{4,3},{6,5},{9,10},{11,12},{13,14},{10,9},... | collective-permute-start | bytes 1769480 | tf_op jit(solution)/shard_map/ppermute | solution.py:492
  9.9 3.2 %collective-permute-start.1 = (bf16[4,288,128]{2,1,0:T(8,128)(2,1)}, bf16[4,288,128]{2,1,0:T(8,128)(2,1)S(1)}, u32[]{:S(2)}, u32[]{:S(2)}) collective-permute-start(bf16[4,288,128]{2,1,0:T(8,128)(2,1)} %get-tuple-element.15), channel_id=1, source_target_pairs={{0,1},{2,3},{4,5},{6,7},{1,0},{3,2},{5,4},{7,6},{8,9},{10,11},{12,... | collective-permute-start | bytes 884744 | tf_op jit(solution)/shard_map/ppermute | solution.py:493
  11.6 1.8 %collective-permute-start.2 = (bf16[4,288,128]{2,1,0:T(8,128)(2,1)}, bf16[4,288,128]{2,1,0:T(8,128)(2,1)S(1)}, u32[]{:S(2)}, u32[]{:S(2)}) collective-permute-start(bf16[4,288,128]{2,1,0:T(8,128)(2,1)} %get-tuple-element.16), channel_id=1, source_target_pairs={{0,1},{2,3},{4,5},{6,7},{1,0},{3,2},{5,4},{7,6},{8,9},{10,11},{12,... | collective-permute-start | bytes 884744 | tf_op jit(solution)/shard_map/ppermute | solution.py:493
  19.4 8.0 %collective-permute-start.3 = (bf16[2,288,128]{2,1,0:T(8,128)(2,1)S(1)}, bf16[2,288,128]{2,1,0:T(8,128)(2,1)S(1)}, u32[]{:S(2)}, u32[]{:S(2)}) collective-permute-start(bf16[2,288,128]{2,1,0:T(8,128)(2,1)S(1)} %get-tuple-element.18), channel_id=1, source_target_pairs={{0,8},{8,0},{16,24},{24,16},{1,9},{9,1},{17,25},{25,17},{2,10},{10... | collective-permute-start | bytes 442376 | tf_op jit(solution)/shard_map/ppermute | solution.py:498
  21.0 8.7 %collective-permute-start.4 = (bf16[2,288,128]{2,1,0:T(8,128)(2,1)S(1)}, bf16[2,288,128]{2,1,0:T(8,128)(2,1)S(1)}, u32[]{:S(2)}, u32[]{:S(2)}) collective-permute-start(bf16[2,288,128]{2,1,0:T(8,128)(2,1)S(1)} %get-tuple-element.19), channel_id=1, source_target_pairs={{0,16},{8,24},{16,0},{24,8},{1,17},{9,25},{17,1},{25,9},{2,18},{10... | collective-permute-start | bytes 442376 | tf_op jit(solution)/shard_map/ppermute | solution.py:498
  22.5 7.2 %collective-permute-start.5 = (bf16[2,288,128]{2,1,0:T(8,128)(2,1)S(1)}, bf16[2,288,128]{2,1,0:T(8,128)(2,1)S(1)}, u32[]{:S(2)}, u32[]{:S(2)}) collective-permute-start(bf16[2,288,128]{2,1,0:T(8,128)(2,1)S(1)} %get-tuple-element.20), channel_id=1, source_target_pairs={{0,24},{8,16},{16,8},{24,0},{1,25},{9,17},{17,9},{25,1},{2,26},{10... | collective-permute-start | bytes 442376 | tf_op jit(solution)/shard_map/ppermute | solution.py:498
  23.7 6.1 %copy-start.1 = (s32[64]{0:T(128)S(1)}, s32[64]{0:T(128)}, u32[]{:S(2)}) copy-start(s32[64]{0:T(128)} %flags_ref.1) | copy-start | bytes 772
  35.6 5.4 %collective-permute-start.8 = (bf16[2,120,128]{2,1,0:T(8,128)(2,1)S(1)}, bf16[2,120,128]{2,1,0:T(8,128)(2,1)S(1)}, u32[]{:S(2)}, u32[]{:S(2)}) collective-permute-start(bf16[2,120,128]{2,1,0:T(8,128)(2,1)S(1)} %shard_map.50.refs_0_), channel_id=1, source_target_pairs={{0,24},{8,16},{16,8},{24,0},{1,25},{9,17},{17,9},{25,1},{2,26},{10... | collective-permute-start | bytes 184328 | tf_op jit(solution)/shard_map/ppermute | solution.py:498
  37.2 4.5 %collective-permute-start.7 = (bf16[2,120,128]{2,1,0:T(8,128)(2,1)S(1)}, bf16[2,120,128]{2,1,0:T(8,128)(2,1)S(1)}, u32[]{:S(2)}, u32[]{:S(2)}) collective-permute-start(bf16[2,120,128]{2,1,0:T(8,128)(2,1)S(1)} %shard_map.50.refs_0_), channel_id=1, source_target_pairs={{0,16},{8,24},{16,0},{24,8},{1,17},{9,25},{17,1},{25,9},{2,18},{10... | collective-permute-start | bytes 184328 | tf_op jit(solution)/shard_map/ppermute | solution.py:498
  38.4 4.2 %collective-permute-start.6 = (bf16[2,120,128]{2,1,0:T(8,128)(2,1)S(1)}, bf16[2,120,128]{2,1,0:T(8,128)(2,1)S(1)}, u32[]{:S(2)}, u32[]{:S(2)}) collective-permute-start(bf16[2,120,128]{2,1,0:T(8,128)(2,1)S(1)} %shard_map.50.refs_0_), channel_id=1, source_target_pairs={{0,8},{8,0},{16,24},{24,16},{1,9},{9,1},{17,25},{25,17},{2,10},{10... | collective-permute-start | bytes 184328 | tf_op jit(solution)/shard_map/ppermute | solution.py:498

commit v5 on v4

--- a/solution.py
+++ b/solution.py
@@ -185,36 +185,30 @@
     )(first, *[pltpu.with_memory_space_constraint(a, pltpu.HBM) for a in (flags, voltages)])
 
 
-def window_kernel(slab_ref, own_ref, across_ref, inside_lead_ref, inside_rest_ref, *refs):
-    mine_ref, *sent_refs, sums = refs
+def window_kernel(slab_ref, own_ref, inside_ref, across_ref, mine_ref, *sent_refs):
     share = mine_ref.shape[0]
-    half = inside_lead_ref.shape[0]
-    for c in range(own_ref.shape[0]):
-        inside = inside_lead_ref[c] if c < half else inside_rest_ref[c - half]
-        ends = inside.astype(jnp.float32) + across_ref[c].astype(jnp.float32)
-        sums[c] = own_ref[c] + ends
 
     def window(slab):
-        return sums[pl.ds(slab * share, share)]
+        rows = pl.ds(slab * share, share)
+        ends = inside_ref[rows].astype(jnp.float32) + across_ref[rows].astype(jnp.float32)
+        return own_ref[rows] + ends
 
     mine_ref[...] = window(slab_ref[0])
     for turn, sent_ref in enumerate(sent_refs, 1):
         sent_ref[...] = window(slab_ref[0] ^ turn).astype(sent_ref.dtype)
 
 
-def windows(slab, own, across, inside_lead, inside_rest, slabs):
-    arrays = own, across, inside_lead, inside_rest
+def windows(slab, own, inside, across, slabs):
     shape = (own.shape[0] // slabs,) + own.shape[1:]
     return pl.pallas_call(
         window_kernel,
         in_specs=[pl.BlockSpec(memory_space=pltpu.SMEM)]
-        + [pl.BlockSpec(a.shape, lambda: (0, 0, 0)) for a in arrays],
+        + [pl.BlockSpec(own.shape, lambda: (0, 0, 0))] * 3,
         out_specs=[pl.BlockSpec(shape, lambda: (0, 0, 0))] * slabs,
         out_shape=[jax.ShapeDtypeStruct(shape, jnp.float32)]
         + [jax.ShapeDtypeStruct(shape, jnp.bfloat16)] * (slabs - 1),
-        scratch_shapes=[pltpu.VMEM(own.shape, jnp.float32)],
         compiler_params=pltpu.CompilerParams(vmem_limit_bytes=VMEM_LIMIT),
-    )(slab, *arrays)
+    )(slab, own, inside, across)
 
 
 def choose_kernel(slab_ref, index_ref, steer_ref, out_ref):
@@ -446,10 +440,9 @@
         out_ref[c] = formed[: 2 * beams].astype(jnp.bfloat16).reshape(beams, 2, samples)
 
 
-def formed_beams(slab, voltages, weights, beams, formed=None):
+def formed_beams(slab, voltages, weights, beams, first_turn=0, formed=None):
     channels, ports, _, samples = voltages.shape
     share, rows, _ = weights[0].shape
-    first_turn = 0 if formed is None else 1
     before = [] if formed is None else [formed]
     whole = pl.BlockSpec(weights[0].shape, lambda i, _: (0, 0, 0))
     return pl.pallas_call(
@@ -490,8 +483,8 @@
     pairs = [[(i, i + 1) for i in range(start, blocks - 1, 2)] for start in range(2)]
     inside_pairs, across_pairs = [ahead + [(j, i) for i, j in ahead] for ahead in pairs]
     across = lax.ppermute(across, "chan", across_pairs)
-    inside = [lax.ppermute(part, "chan", inside_pairs) for part in inside]
-    mine, *sent = windows(slab, own, across, *inside, slabs)
+    inside = jnp.concatenate([lax.ppermute(part, "chan", inside_pairs) for part in inside], axis=0)
+    mine, *sent = windows(slab, own, inside, across, slabs)
 
     def swap(arrays):
         return [
@@ -505,7 +498,8 @@
     weights = solved_weights(first_share, channel_flags, held, mine, got, chosen, port_count, beam_count)
     others = swap([weights] * (slabs - 1))
     beams = formed_beams(slab, held, [weights], beam_count)
-    beams = formed_beams(slab, held, others, beam_count, beams)
+    beams = formed_beams(slab, held, others[-1:], beam_count, slabs - 1, beams)
+    beams = formed_beams(slab, held, others[:-1], beam_count, 1, beams)
     return jnp.transpose(beams, (0, 2, 1, 3))
 
 

time: 46 us -> 44.2 us (0.961)
  waiting for transfers between devices: 11.6 us -> 9.99 us
    ppermute x6, waiting for transfers between devices: 4.11 us -> 2.78 us  [swap(): lax.ppermute(array, 'slab', [(i, i ^ turn) for i in range(slabs)])]
    pallas_call x1, Pallas kernels: 7.6 us -> 6.76 us  [covariances(): pl.pallas_call(covariance_kernel, in_specs=[smem] + [pl.BlockSpec(memory_...]
    pallas_call x2 -> x3, Pallas kernels: 4.93 us -> 5.7 us  [formed_beams(): pl.pallas_call(functools.partial(beam_kernel, first_turn), grid_spec=pltp...]
  transfers between devices with their start and end apart: 9 -> 9, of which waited for: 7 -> 6; matrix products, arithmetic and copies ran while one was open for 0% -> 0% of each run, Pallas kernels for 13% -> 17%
where the time goes in v5:
time: 44.2 us; the launch traced here: 44 us
  Pallas kernels  22.9 us (52%)
  starting transfers between devices  11 us (25%)
  waiting for transfers between devices  9.99 us (23%)
    ppermute x6, starting transfers between devices, swap(): lax.ppermute(array, 'slab', [(i, i ^ turn) for i in range(slabs)])  7.08 us
    pallas_call x1, Pallas kernels, covariances(): pl.pallas_call(covariance_kernel, in_specs=[smem] + [pl.BlockSpec(memory_...  6.76 us
    pallas_call x1, Pallas kernels, solved_weights(): pl.pallas_call(functools.partial(solve_kernel, ports, beams), in_specs=[s...  5.87 us
    pallas_call x3, Pallas kernels, formed_beams(): pl.pallas_call(functools.partial(beam_kernel, first_turn), grid_spec=pltp...  5.7 us
    ppermute x1, waiting for transfers between devices, body(): across = lax.ppermute(across, 'chan', across_pairs)  5.66 us
    pallas_call x1, Pallas kernels, held_voltages(): pl.pallas_call(hold_kernel, in_specs=[pl.BlockSpec(memory_space=pltpu.HBM...  3.73 us
    ppermute x6, waiting for transfers between devices, swap(): lax.ppermute(array, 'slab', [(i, i ^ turn) for i in range(slabs)])  2.78 us
    ppermute x1, starting transfers between devices, body(): across = lax.ppermute(across, 'chan', across_pairs)  2.1 us
  transfers between devices with their start and end apart: 9, of which 6 were waited for; matrix products, arithmetic and copies ran while one was open for 0% of the time, Pallas kernels for 17%

profile of v5, /device:TPU:16, one launch (start us, length us, event | category | flops | bytes accessed | tf_op | source)
XLA Modules:
  0.0 44.0 jit_solution(12446780976379520521)
XLA Ops:
  0.0 6.8 %shard_map.46 = (bf16[8,288,128]{2,1,0:T(8,128)(2,1)S(1)}, bf16[4,288,128]{2,1,0:T(8,128)(2,1)S(1)}, bf16[4,288,128]{2,1,0:T(8,128)(2,1)S(1)}, f32[8,288,128]{2,1,0:T(8,128)S(1)}) custom-call(s32[1]{0:T(128)} %bitcast.2.first_ref, s32[64]{0:T(128)} %flags_ref.1, bf16[8,188,2,1536]{3,2,1,0:T(2,128)(2,1)} %bitcast.4), custom_call_target="tpu_custom_call" | custom-call | tf_op jit(solution)/shard_map/pallas_call | solution.py:165
  6.8 2.1 %collective-permute-start.2 = (bf16[8,288,128]{2,1,0:T(8,128)(2,1)S(1)}, bf16[8,288,128]{2,1,0:T(8,128)(2,1)S(1)}, u32[]{:S(2)}, u32[]{:S(2)}) collective-permute-start(bf16[8,288,128]{2,1,0:T(8,128)(2,1)S(1)} %get-tuple-element.16), channel_id=1, source_target_pairs={{1,2},{3,4},{5,6},{2,1},{4,3},{6,5},{9,10},{11,12},{13,14},{10,9},... | collective-permute-start | bytes 1769480 | tf_op jit(solution)/shard_map/ppermute | solution.py:485
  8.9 1.7 %collective-permute-start = (bf16[4,288,128]{2,1,0:T(8,128)(2,1)S(1)}, bf16[4,288,128]{2,1,0:T(8,128)(2,1)S(1)}, u32[]{:S(2)}, u32[]{:S(2)}) collective-permute-start(bf16[4,288,128]{2,1,0:T(8,128)(2,1)S(1)} %get-tuple-element.14), channel_id=1, source_target_pairs={{0,1},{2,3},{4,5},{6,7},{1,0},{3,2},{5,4},{7,6},{8,9},{10,11},{12,... | collective-permute-start | bytes 884744 | tf_op jit(solution)/shard_map/ppermute | solution.py:486
  10.6 0.1 collective-permute-start.1
  10.7 0.0 copy-start
  10.7 0.0 copy-start.2
  10.7 1.1 %collective-permute-done = bf16[4,288,128]{2,1,0:T(8,128)(2,1)S(1)} collective-permute-done((bf16[4,288,128]{2,1,0:T(8,128)(2,1)S(1)}, bf16[4,288,128]{2,1,0:T(8,128)(2,1)S(1)}, u32[]{:S(2)}, u32[]{:S(2)}) %collective-permute-start) | collective-permute-done | bytes 294944 | tf_op jit(solution)/shard_map/ppermute | solution.py:486
  11.8 0.4 collective-permute-done.1
  12.3 0.1 pad_maximum_fusion.inside_ref
  12.3 5.7 %collective-permute-done.2.across_ref = bf16[8,288,128]{2,1,0:T(8,128)(2,1)S(1)} collective-permute-done((bf16[8,288,128]{2,1,0:T(8,128)(2,1)S(1)}, bf16[8,288,128]{2,1,0:T(8,128)(2,1)S(1)}, u32[]{:S(2)}, u32[]{:S(2)}) %collective-permute-start.2) | collective-permute-done | bytes 589856 | tf_op jit(solution)/shard_map/ppermute | solution.py:485
  18.0 0.2 shard_map.47
  18.1 1.6 %collective-permute-start.3 = (bf16[2,288,128]{2,1,0:T(8,128)(2,1)S(1)}, bf16[2,288,128]{2,1,0:T(8,128)(2,1)S(1)}, u32[]{:S(2)}, u32[]{:S(2)}) collective-permute-start(bf16[2,288,128]{2,1,0:T(8,128)(2,1)S(1)} %get-tuple-element.18), channel_id=1, source_target_pairs={{0,8},{8,0},{16,24},{24,16},{1,9},{9,1},{17,25},{25,17},{2,10},{10... | collective-permute-start | bytes 442376 | tf_op jit(solution)/shard_map/ppermute | solution.py:491
  19.7 1.5 %collective-permute-start.4 = (bf16[2,288,128]{2,1,0:T(8,128)(2,1)S(1)}, bf16[2,288,128]{2,1,0:T(8,128)(2,1)S(1)}, u32[]{:S(2)}, u32[]{:S(2)}) collective-permute-start(bf16[2,288,128]{2,1,0:T(8,128)(2,1)S(1)} %get-tuple-element.19), channel_id=1, source_target_pairs={{0,16},{8,24},{16,0},{24,8},{1,17},{9,25},{17,1},{25,9},{2,18},{10... | collective-permute-start | bytes 442376 | tf_op jit(solution)/shard_map/ppermute | solution.py:491
  21.2 0.5 %collective-permute-start.5 = (bf16[2,288,128]{2,1,0:T(8,128)(2,1)S(1)}, bf16[2,288,128]{2,1,0:T(8,128)(2,1)S(1)}, u32[]{:S(2)}, u32[]{:S(2)}) collective-permute-start(bf16[2,288,128]{2,1,0:T(8,128)(2,1)S(1)} %get-tuple-element.20), channel_id=1, source_target_pairs={{0,24},{8,16},{16,8},{24,0},{1,25},{9,17},{17,9},{25,1},{2,26},{10... | collective-permute-start | bytes 442376 | tf_op jit(solution)/shard_map/ppermute | solution.py:491
  21.7 0.0 copy-done
  21.7 0.0 copy-done.2
  21.7 0.7 %shard_map.49.refs_4_ = f32[2,80,192]{2,1,0:T(8,128)S(1)} custom-call(s32[1]{0:T(128)} %bitcast.slab_ref, s32[36]{0:T(128)S(1)} %copy-done.2, f32[8,2,64,188]{3,2,1,0:T(8,128)S(1)} %copy-done), custom_call_target="tpu_custom_call" | custom-call | tf_op jit(solution)/shard_map/pallas_call | solution.py:227
  22.4 0.0 copy-start.1
  22.4 3.7 %shard_map.48.held_ref.volt_ref = bf16[8,188,2,1536]{3,2,1,0:T(2,128)(2,1)S(1)} custom-call(bf16[8,188,2,1536]{3,2,1,0:T(2,128)(2,1)} %bitcast.5, f32[2,288,128]{2,1,0:T(8,128)S(1)} %get-tuple-element.17.weight_hbm.refs_0_), custom_call_target="tpu_custom_call" | custom-call | tf_op jit(solution)/shard_map/pallas_call | solution.py:402
  26.1 0.0 collective-permute-done.3.refs_1_
  26.2 2.3 %collective-permute-done.4.refs_2_ = bf16[2,288,128]{2,1,0:T(8,128)(2,1)S(1)} collective-permute-done((bf16[2,288,128]{2,1,0:T(8,128)(2,1)S(1)}, bf16[2,288,128]{2,1,0:T(8,128)(2,1)S(1)}, u32[]{:S(2)}, u32[]{:S(2)}) %collective-permute-start.4) | collective-permute-done | bytes 147488 | tf_op jit(solution)/shard_map/ppermute | solution.py:491
  28.5 0.0 collective-permute-done.5.refs_3_
  28.5 0.0 copy-done.1
  28.5 5.9 %shard_map.50.refs_0_ = bf16[2,120,128]{2,1,0:T(8,128)(2,1)S(1)} custom-call(s32[1]{0:T(128)S(6)} %add.3.first_ref, s32[64]{0:T(128)S(1)} %copy-done.1, bf16[8,188,2,1536]{3,2,1,0:T(2,128)(2,1)S(1)} %shard_map.48.held_ref.volt_ref, f32[2,288,128]{2,1,0:T(8,128)S(1)} %get-tuple-element.17.weight_hbm.refs_0_, ...), custom_call_target="tpu_custom_call" | custom-call | tf_op jit(solution)/shard_map/pallas_call | solution.py:381
  34.3 1.5 %collective-permute-start.6 = (bf16[2,120,128]{2,1,0:T(8,128)(2,1)S(1)}, bf16[2,120,128]{2,1,0:T(8,128)(2,1)S(1)}, u32[]{:S(2)}, u32[]{:S(2)}) collective-permute-start(bf16[2,120,128]{2,1,0:T(8,128)(2,1)S(1)} %shard_map.50.refs_0_), channel_id=1, source_target_pairs={{0,24},{8,16},{16,8},{24,0},{1,25},{9,17},{17,9},{25,1},{2,26},{10... | collective-permute-start | bytes 184328 | tf_op jit(solution)/shard_map/ppermute | solution.py:491
  35.9 1.5 %collective-permute-start.7 = (bf16[2,120,128]{2,1,0:T(8,128)(2,1)S(1)}, bf16[2,120,128]{2,1,0:T(8,128)(2,1)S(1)}, u32[]{:S(2)}, u32[]{:S(2)}) collective-permute-start(bf16[2,120,128]{2,1,0:T(8,128)(2,1)S(1)} %shard_map.50.refs_0_), channel_id=1, source_target_pairs={{0,8},{8,0},{16,24},{24,16},{1,9},{9,1},{17,25},{25,17},{2,10},{10... | collective-permute-start | bytes 184328 | tf_op jit(solution)/shard_map/ppermute | solution.py:491
  37.3 0.5 %collective-permute-start.8 = (bf16[2,120,128]{2,1,0:T(8,128)(2,1)S(1)}, bf16[2,120,128]{2,1,0:T(8,128)(2,1)S(1)}, u32[]{:S(2)}, u32[]{:S(2)}) collective-permute-start(bf16[2,120,128]{2,1,0:T(8,128)(2,1)S(1)} %shard_map.50.refs_0_), channel_id=1, source_target_pairs={{0,16},{8,24},{16,0},{24,8},{1,17},{9,25},{17,1},{25,9},{2,18},{10... | collective-permute-start | bytes 184328 | tf_op jit(solution)/shard_map/ppermute | solution.py:491
  37.9 1.6 %shard_map.51.refs_0_ = bf16[8,36,2,1536]{3,2,1,0:T(2,128)(2,1)} custom-call(s32[1]{0:T(128)} %bitcast.slab_ref, bf16[8,188,2,1536]{3,2,1,0:T(2,128)(2,1)S(1)} %shard_map.48.held_ref.volt_ref, bf16[2,120,128]{2,1,0:T(8,128)(2,1)S(1)} %shard_map.50.refs_0_), custom_call_target="tpu_custom_call" | custom-call | tf_op jit(solution)/shard_map/pallas_call | solution.py:448
  39.5 0.1 collective-permute-done.6.refs_1_
  39.6 1.6 %shard_map.52.refs_0_ = bf16[8,36,2,1536]{3,2,1,0:T(2,128)(2,1)} custom-call(s32[1]{0:T(128)} %bitcast.slab_ref, bf16[8,188,2,1536]{3,2,1,0:T(2,128)(2,1)S(1)} %shard_map.48.held_ref.volt_ref, bf16[8,36,2,1536]{3,2,1,0:T(2,128)(2,1)} %shard_map.51.refs_0_, bf16[2,120,128]{2,1,0:T(8,128)(2,1)S(1)} %collective-permute-done.6.refs_1_), custom_call_target="tpu_custom_call", output_to_operand_aliasing={{}: (2, {})} | custom-call | tf_op jit(solution)/shard_map/pallas_call | solution.py:448
  41.2 0.0 collective-permute-done.7.refs_1_
  41.2 0.4 collective-permute-done.8.refs_2_
  41.6 2.5 %shard_map.53 = bf16[8,36,2,1536]{3,2,1,0:T(2,128)(2,1)} custom-call(s32[1]{0:T(128)} %bitcast.slab_ref, bf16[8,188,2,1536]{3,2,1,0:T(2,128)(2,1)S(1)} %shard_map.48.held_ref.volt_ref, bf16[8,36,2,1536]{3,2,1,0:T(2,128)(2,1)} %shard_map.52.refs_0_, bf16[2,120,128]{2,1,0:T(8,128)(2,1)S(1)} %collective-permute-done.7.refs_1_, ...), custom_call_target="tpu_custom_call", output_to_operand_aliasing={{}: (2, {})} | custom-call | tf_op jit(solution)/shard_map/pallas_call | solution.py:448
Async XLA Ops:
  6.8 11.2 %collective-permute-start.2 = (bf16[8,288,128]{2,1,0:T(8,128)(2,1)S(1)}, bf16[8,288,128]{2,1,0:T(8,128)(2,1)S(1)}, u32[]{:S(2)}, u32[]{:S(2)}) collective-permute-start(bf16[8,288,128]{2,1,0:T(8,128)(2,1)S(1)} %get-tuple-element.16), channel_id=1, source_target_pairs={{1,2},{3,4},{5,6},{2,1},{4,3},{6,5},{9,10},{11,12},{13,14},{10,9},... | collective-permute-start | bytes 1769480 | tf_op jit(solution)/shard_map/ppermute | solution.py:485
  8.9 3.0 %collective-permute-start = (bf16[4,288,128]{2,1,0:T(8,128)(2,1)S(1)}, bf16[4,288,128]{2,1,0:T(8,128)(2,1)S(1)}, u32[]{:S(2)}, u32[]{:S(2)}) collective-permute-start(bf16[4,288,128]{2,1,0:T(8,128)(2,1)S(1)} %get-tuple-element.14), channel_id=1, source_target_pairs={{0,1},{2,3},{4,5},{6,7},{1,0},{3,2},{5,4},{7,6},{8,9},{10,11},{12,... | collective-permute-start | bytes 884744 | tf_op jit(solution)/shard_map/ppermute | solution.py:486
  10.6 1.6 %collective-permute-start.1 = (bf16[4,288,128]{2,1,0:T(8,128)(2,1)S(1)}, bf16[4,288,128]{2,1,0:T(8,128)(2,1)S(1)}, u32[]{:S(2)}, u32[]{:S(2)}) collective-permute-start(bf16[4,288,128]{2,1,0:T(8,128)(2,1)S(1)} %get-tuple-element.15), channel_id=1, source_target_pairs={{0,1},{2,3},{4,5},{6,7},{1,0},{3,2},{5,4},{7,6},{8,9},{10,11},{12,... | collective-permute-start | bytes 884744 | tf_op jit(solution)/shard_map/ppermute | solution.py:486
  10.7 11.0 %copy-start = (f32[8,2,64,188]{3,2,1,0:T(8,128)S(1)}, f32[8,2,64,188]{3,2,1,0:T(8,128)}, u32[]{:S(2)}) copy-start(f32[8,2,64,188]{3,2,1,0:T(8,128)} %steer_ref.1) | copy-start | bytes 2310148
  10.7 11.0 %copy-start.2 = (s32[36]{0:T(128)S(1)}, s32[36]{0:T(128)}, u32[]{:S(2)}) copy-start(s32[36]{0:T(128)} %index_ref.1) | copy-start | bytes 436
  18.1 8.0 %collective-permute-start.3 = (bf16[2,288,128]{2,1,0:T(8,128)(2,1)S(1)}, bf16[2,288,128]{2,1,0:T(8,128)(2,1)S(1)}, u32[]{:S(2)}, u32[]{:S(2)}) collective-permute-start(bf16[2,288,128]{2,1,0:T(8,128)(2,1)S(1)} %get-tuple-element.18), channel_id=1, source_target_pairs={{0,8},{8,0},{16,24},{24,16},{1,9},{9,1},{17,25},{25,17},{2,10},{10... | collective-permute-start | bytes 442376 | tf_op jit(solution)/shard_map/ppermute | solution.py:491
  19.7 8.7 %collective-permute-start.4 = (bf16[2,288,128]{2,1,0:T(8,128)(2,1)S(1)}, bf16[2,288,128]{2,1,0:T(8,128)(2,1)S(1)}, u32[]{:S(2)}, u32[]{:S(2)}) collective-permute-start(bf16[2,288,128]{2,1,0:T(8,128)(2,1)S(1)} %get-tuple-element.19), channel_id=1, source_target_pairs={{0,16},{8,24},{16,0},{24,8},{1,17},{9,25},{17,1},{25,9},{2,18},{10... | collective-permute-start | bytes 442376 | tf_op jit(solution)/shard_map/ppermute | solution.py:491
  21.2 7.2 %collective-permute-start.5 = (bf16[2,288,128]{2,1,0:T(8,128)(2,1)S(1)}, bf16[2,288,128]{2,1,0:T(8,128)(2,1)S(1)}, u32[]{:S(2)}, u32[]{:S(2)}) collective-permute-start(bf16[2,288,128]{2,1,0:T(8,128)(2,1)S(1)} %get-tuple-element.20), channel_id=1, source_target_pairs={{0,24},{8,16},{16,8},{24,0},{1,25},{9,17},{17,9},{25,1},{2,26},{10... | collective-permute-start | bytes 442376 | tf_op jit(solution)/shard_map/ppermute | solution.py:491
  22.4 6.1 %copy-start.1 = (s32[64]{0:T(128)S(1)}, s32[64]{0:T(128)}, u32[]{:S(2)}) copy-start(s32[64]{0:T(128)} %flags_ref.1) | copy-start | bytes 772
  34.3 5.3 %collective-permute-start.6 = (bf16[2,120,128]{2,1,0:T(8,128)(2,1)S(1)}, bf16[2,120,128]{2,1,0:T(8,128)(2,1)S(1)}, u32[]{:S(2)}, u32[]{:S(2)}) collective-permute-start(bf16[2,120,128]{2,1,0:T(8,128)(2,1)S(1)} %shard_map.50.refs_0_), channel_id=1, source_target_pairs={{0,24},{8,16},{16,8},{24,0},{1,25},{9,17},{17,9},{25,1},{2,26},{10... | collective-permute-start | bytes 184328 | tf_op jit(solution)/shard_map/ppermute | solution.py:491
  35.9 5.4 %collective-permute-start.7 = (bf16[2,120,128]{2,1,0:T(8,128)(2,1)S(1)}, bf16[2,120,128]{2,1,0:T(8,128)(2,1)S(1)}, u32[]{:S(2)}, u32[]{:S(2)}) collective-permute-start(bf16[2,120,128]{2,1,0:T(8,128)(2,1)S(1)} %shard_map.50.refs_0_), channel_id=1, source_target_pairs={{0,8},{8,0},{16,24},{24,16},{1,9},{9,1},{17,25},{25,17},{2,10},{10... | collective-permute-start | bytes 184328 | tf_op jit(solution)/shard_map/ppermute | solution.py:491
  37.3 4.2 %collective-permute-start.8 = (bf16[2,120,128]{2,1,0:T(8,128)(2,1)S(1)}, bf16[2,120,128]{2,1,0:T(8,128)(2,1)S(1)}, u32[]{:S(2)}, u32[]{:S(2)}) collective-permute-start(bf16[2,120,128]{2,1,0:T(8,128)(2,1)S(1)} %shard_map.50.refs_0_), channel_id=1, source_target_pairs={{0,16},{8,24},{16,0},{24,8},{1,17},{9,25},{17,1},{25,9},{2,18},{10... | collective-permute-start | bytes 184328 | tf_op jit(solution)/shard_map/ppermute | solution.py:491

commit v6 on v5

--- a/solution.py
+++ b/solution.py
@@ -40,10 +40,10 @@
     )
 
 
-def unfold(folded):
-    size = folded.shape[0] * 2 // 3
+def unfold(folded, size):
     width = LANES // 2
-    rest = jnp.concatenate([folded[size:, :width], folded[size:, width:]], axis=0)
+    rest = folded[size : size + size // 2]
+    rest = jnp.concatenate([rest[:, :width], rest[:, width:]], axis=0)
     return jnp.concatenate([folded[:size], rest], axis=1)
 
 
@@ -59,7 +59,7 @@
 
 
 def gram(volt, left_ref, right_ref):
-    lead = left_ref.shape[1] // 2
+    lead = round_up(volt.shape[0], 16) // 2
     rest = volt.shape[0] - lead
     left, right = dot_nt(volt, volt[:lead]), dot_nt(volt[lead:], volt[lead:])
     left_ref[0, : volt.shape[0]] = left[:, :LANES]
@@ -69,7 +69,7 @@
 
 
 def pack(left_ref, right_ref, out_ref):
-    half = left_ref.shape[1] // 4
+    half = out_ref.shape[0] // 3
 
     def rows(ref, lanes, first, parity):
         return ref[lanes, pl.ds(2 * first + parity, half, stride=2), :]
@@ -168,8 +168,8 @@
         out_specs=[vmem] * 4,
         scratch_shapes=[
             pltpu.VMEM(voltages.shape, voltages.dtype),
-            pltpu.VMEM((4, 2, 2 * size, LANES), jnp.float32),
-            pltpu.VMEM((4, 2, size, LANES), jnp.float32),
+            pltpu.VMEM((4, 2, 2 * size + 8, LANES), jnp.float32),
+            pltpu.VMEM((4, 2, size + 8, LANES), jnp.float32),
             pltpu.VMEM(folded, jnp.float32),
             pltpu.SMEM(flags.shape, flags.dtype),
             pltpu.SemaphoreType.DMA((channels,)),
@@ -240,8 +240,8 @@
 
 
 def unpack(folded):
-    packed = unfold(folded)
-    size = packed.shape[0]
+    size = folded.shape[0] * 2 // 3
+    packed = unfold(folded, size)
     half = size // 2
     row, col = iotas(size, 2 * LANES)
     spread = (row == jnp.where(col < LANES, 2 * col, 2 * (col - LANES) + 1)) & (col % LANES < half)
@@ -368,16 +368,18 @@
         weights = dot_nn(order, (y * stack(factor, factor)).astype(jnp.bfloat16))
         high = weights[:, LANES:]
         weight_ref[c, : 2 * half] = weights[:, :LANES].astype(jnp.bfloat16)
-        weight_ref[c, 2 * half :] = jnp.concatenate([high[:half], high[half:]], axis=1).astype(
-            jnp.bfloat16
-        )
+        high = jnp.concatenate([high[:half], high[half:]], axis=1)
+        spare = weight_ref.shape[1] - 3 * half
+        if spare:
+            high = stack(high, jnp.zeros((spare, LANES), jnp.float32))
+        weight_ref[c, 2 * half :] = high.astype(jnp.bfloat16)
 
 
 def solved_weights(first, flags, held, own, got, chosen, ports, beams):
     share, rows, _ = chosen.shape
     smem = pl.BlockSpec(memory_space=pltpu.SMEM)
     whole = [pl.BlockSpec(a.shape, lambda: (0, 0, 0)) for a in (own, *got, chosen)]
-    shape = (share, rows + rows // 2, LANES)
+    shape = (share, round_up(rows + rows // 2, 16), LANES)
     return pl.pallas_call(
         functools.partial(solve_kernel, ports, beams),
         in_specs=[smem, smem, pl.BlockSpec(memory_space=pl.ANY)] + whole,
@@ -411,16 +413,16 @@
 
 def beam_kernel(first_turn, slab_ref, volt_ref, *refs):
     *weight_refs, out_ref, mixed = refs if first_turn == 0 else refs[1:]
-    share, rows, _ = weight_refs[0].shape
-    rows = rows * 2 // 3
+    share = weight_refs[0].shape[0]
     _, ports, _, samples = volt_ref.shape
     beams = out_ref.shape[1]
+    rows = mixed.shape[1]
     step = pl.program_id(0)
 
     @pl.when(step == 0)
     def _():
         folded = [ref[c].astype(jnp.float32) for ref in weight_refs for c in range(share)]
-        real_rows = stack(*[unfold(f) for f in folded])
+        real_rows = stack(*[unfold(f, rows) for f in folded])
         count, size = real_rows.shape
         row, _ = iotas(count, size)
         below, above = pltpu.roll(real_rows, count - 1, 0), pltpu.roll(real_rows, 1, 0)
@@ -442,7 +444,7 @@
 
 def formed_beams(slab, voltages, weights, beams, first_turn=0, formed=None):
     channels, ports, _, samples = voltages.shape
-    share, rows, _ = weights[0].shape
+    share = weights[0].shape[0]
     before = [] if formed is None else [formed]
     whole = pl.BlockSpec(weights[0].shape, lambda i, _: (0, 0, 0))
     return pl.pallas_call(
@@ -457,7 +459,7 @@
                 (share, beams, 2, samples), lambda i, slab: (slab[0] ^ (i + first_turn), 0, 0, 0)
             ),
             scratch_shapes=[
-                pltpu.VMEM((len(weights) * share, rows * 2 // 3, 2 * ports), jnp.bfloat16)
+                pltpu.VMEM((len(weights) * share, 2 * round_up(beams, 8), 2 * ports), jnp.bfloat16)
             ],
         ),
         out_shape=jax.ShapeDtypeStruct((channels, beams, 2, samples), jnp.bfloat16),

time: 44.2 us -> 44.2 us (level)
  no operation moved by 1% of the time
where the time goes in v6:
time: 44.2 us; the launch traced here: 44.1 us
  Pallas kernels  22.9 us (52%)
  starting transfers between devices  11 us (25%)
  waiting for transfers between devices  10 us (23%)
    ppermute x6, starting transfers between devices, swap(): lax.ppermute(array, 'slab', [(i, i ^ turn) for i in range(slabs)])  7.08 us
    pallas_call x1, Pallas kernels, covariances(): pl.pallas_call(covariance_kernel, in_specs=[smem] + [pl.BlockSpec(memory_...  6.75 us
    pallas_call x1, Pallas kernels, solved_weights(): pl.pallas_call(functools.partial(solve_kernel, ports, beams), in_specs=[s...  5.87 us
    pallas_call x3, Pallas kernels, formed_beams(): pl.pallas_call(functools.partial(beam_kernel, first_turn), grid_spec=pltp...  5.7 us
    ppermute x1, waiting for transfers between devices, body(): across = lax.ppermute(across, 'chan', across_pairs)  5.66 us
    pallas_call x1, Pallas kernels, held_voltages(): pl.pallas_call(hold_kernel, in_specs=[pl.BlockSpec(memory_space=pltpu.HBM...  3.73 us
    ppermute x6, waiting for transfers between devices, swap(): lax.ppermute(array, 'slab', [(i, i ^ turn) for i in range(slabs)])  2.82 us
    ppermute x1, starting transfers between devices, body(): across = lax.ppermute(across, 'chan', across_pairs)  2.1 us
  transfers between devices with their start and end apart: 9, of which 6 were waited for; matrix products, arithmetic and copies ran while one was open for 0% of the time, Pallas kernels for 17%

profile of v6, /device:TPU:16, one launch (start us, length us, event | category | flops | bytes accessed | tf_op | source)
XLA Modules:
  0.0 44.1 jit_solution(9887386103353433262)
XLA Ops:
  0.0 6.8 %shard_map.46 = (bf16[8,288,128]{2,1,0:T(8,128)(2,1)S(1)}, bf16[4,288,128]{2,1,0:T(8,128)(2,1)S(1)}, bf16[4,288,128]{2,1,0:T(8,128)(2,1)S(1)}, f32[8,288,128]{2,1,0:T(8,128)S(1)}) custom-call(s32[1]{0:T(128)} %bitcast.2.first_ref, s32[64]{0:T(128)} %flags_ref.1, bf16[8,188,2,1536]{3,2,1,0:T(2,128)(2,1)} %bitcast.4), custom_call_target="tpu_custom_call" | custom-call | tf_op jit(solution)/shard_map/pallas_call | solution.py:165
  6.8 2.1 %collective-permute-start.2 = (bf16[8,288,128]{2,1,0:T(8,128)(2,1)S(1)}, bf16[8,288,128]{2,1,0:T(8,128)(2,1)S(1)}, u32[]{:S(2)}, u32[]{:S(2)}) collective-permute-start(bf16[8,288,128]{2,1,0:T(8,128)(2,1)S(1)} %get-tuple-element.16), channel_id=1, source_target_pairs={{1,2},{3,4},{5,6},{2,1},{4,3},{6,5},{9,10},{11,12},{13,14},{10,9},... | collective-permute-start | bytes 1769480 | tf_op jit(solution)/shard_map/ppermute | solution.py:487
  8.9 1.7 %collective-permute-start = (bf16[4,288,128]{2,1,0:T(8,128)(2,1)S(1)}, bf16[4,288,128]{2,1,0:T(8,128)(2,1)S(1)}, u32[]{:S(2)}, u32[]{:S(2)}) collective-permute-start(bf16[4,288,128]{2,1,0:T(8,128)(2,1)S(1)} %get-tuple-element.14), channel_id=1, source_target_pairs={{0,1},{2,3},{4,5},{6,7},{1,0},{3,2},{5,4},{7,6},{8,9},{10,11},{12,... | collective-permute-start | bytes 884744 | tf_op jit(solution)/shard_map/ppermute | solution.py:488
  10.6 0.1 collective-permute-start.1
  10.7 0.0 copy-start
  10.7 0.0 copy-start.2
  10.7 1.1 %collective-permute-done = bf16[4,288,128]{2,1,0:T(8,128)(2,1)S(1)} collective-permute-done((bf16[4,288,128]{2,1,0:T(8,128)(2,1)S(1)}, bf16[4,288,128]{2,1,0:T(8,128)(2,1)S(1)}, u32[]{:S(2)}, u32[]{:S(2)}) %collective-permute-start) | collective-permute-done | bytes 294944 | tf_op jit(solution)/shard_map/ppermute | solution.py:488
  11.8 0.4 collective-permute-done.1
  12.3 0.1 pad_maximum_fusion.inside_ref
  12.3 5.7 %collective-permute-done.2.across_ref = bf16[8,288,128]{2,1,0:T(8,128)(2,1)S(1)} collective-permute-done((bf16[8,288,128]{2,1,0:T(8,128)(2,1)S(1)}, bf16[8,288,128]{2,1,0:T(8,128)(2,1)S(1)}, u32[]{:S(2)}, u32[]{:S(2)}) %collective-permute-start.2) | collective-permute-done | bytes 589856 | tf_op jit(solution)/shard_map/ppermute | solution.py:487
  18.0 0.2 shard_map.47
  18.1 1.6 %collective-permute-start.3 = (bf16[2,288,128]{2,1,0:T(8,128)(2,1)S(1)}, bf16[2,288,128]{2,1,0:T(8,128)(2,1)S(1)}, u32[]{:S(2)}, u32[]{:S(2)}) collective-permute-start(bf16[2,288,128]{2,1,0:T(8,128)(2,1)S(1)} %get-tuple-element.18), channel_id=1, source_target_pairs={{0,8},{8,0},{16,24},{24,16},{1,9},{9,1},{17,25},{25,17},{2,10},{10... | collective-permute-start | bytes 442376 | tf_op jit(solution)/shard_map/ppermute | solution.py:493
  19.7 1.5 %collective-permute-start.4 = (bf16[2,288,128]{2,1,0:T(8,128)(2,1)S(1)}, bf16[2,288,128]{2,1,0:T(8,128)(2,1)S(1)}, u32[]{:S(2)}, u32[]{:S(2)}) collective-permute-start(bf16[2,288,128]{2,1,0:T(8,128)(2,1)S(1)} %get-tuple-element.19), channel_id=1, source_target_pairs={{0,16},{8,24},{16,0},{24,8},{1,17},{9,25},{17,1},{25,9},{2,18},{10... | collective-permute-start | bytes 442376 | tf_op jit(solution)/shard_map/ppermute | solution.py:493
  21.2 0.5 %collective-permute-start.5 = (bf16[2,288,128]{2,1,0:T(8,128)(2,1)S(1)}, bf16[2,288,128]{2,1,0:T(8,128)(2,1)S(1)}, u32[]{:S(2)}, u32[]{:S(2)}) collective-permute-start(bf16[2,288,128]{2,1,0:T(8,128)(2,1)S(1)} %get-tuple-element.20), channel_id=1, source_target_pairs={{0,24},{8,16},{16,8},{24,0},{1,25},{9,17},{17,9},{25,1},{2,26},{10... | collective-permute-start | bytes 442376 | tf_op jit(solution)/shard_map/ppermute | solution.py:493
  21.7 0.0 copy-done
  21.7 0.0 copy-done.2
  21.7 0.7 %shard_map.49.refs_4_ = f32[2,80,192]{2,1,0:T(8,128)S(1)} custom-call(s32[1]{0:T(128)} %bitcast.slab_ref, s32[36]{0:T(128)S(1)} %copy-done.2, f32[8,2,64,188]{3,2,1,0:T(8,128)S(1)} %copy-done), custom_call_target="tpu_custom_call" | custom-call | tf_op jit(solution)/shard_map/pallas_call | solution.py:227
  22.4 0.0 copy-start.1
  22.4 3.7 %shard_map.48.held_ref.volt_ref = bf16[8,188,2,1536]{3,2,1,0:T(2,128)(2,1)S(1)} custom-call(bf16[8,188,2,1536]{3,2,1,0:T(2,128)(2,1)} %bitcast.5, f32[2,288,128]{2,1,0:T(8,128)S(1)} %get-tuple-element.17.weight_hbm.refs_0_), custom_call_target="tpu_custom_call" | custom-call | tf_op jit(solution)/shard_map/pallas_call | solution.py:404
  26.1 0.0 collective-permute-done.3.refs_1_
  26.1 2.3 %collective-permute-done.4.refs_2_ = bf16[2,288,128]{2,1,0:T(8,128)(2,1)S(1)} collective-permute-done((bf16[2,288,128]{2,1,0:T(8,128)(2,1)S(1)}, bf16[2,288,128]{2,1,0:T(8,128)(2,1)S(1)}, u32[]{:S(2)}, u32[]{:S(2)}) %collective-permute-start.4) | collective-permute-done | bytes 147488 | tf_op jit(solution)/shard_map/ppermute | solution.py:493
  28.5 0.0 collective-permute-done.5.refs_3_
  28.5 0.0 copy-done.1
  28.5 5.9 %shard_map.50.refs_0_ = bf16[2,128,128]{2,1,0:T(8,128)(2,1)S(1)} custom-call(s32[1]{0:T(128)S(6)} %add.3.first_ref, s32[64]{0:T(128)S(1)} %copy-done.1, bf16[8,188,2,1536]{3,2,1,0:T(2,128)(2,1)S(1)} %shard_map.48.held_ref.volt_ref, f32[2,288,128]{2,1,0:T(8,128)S(1)} %get-tuple-element.17.weight_hbm.refs_0_, ...), custom_call_target="tpu_custom_call" | custom-call | tf_op jit(solution)/shard_map/pallas_call | solution.py:383
  34.3 1.5 %collective-permute-start.6 = (bf16[2,128,128]{2,1,0:T(8,128)(2,1)S(1)}, bf16[2,128,128]{2,1,0:T(8,128)(2,1)S(1)}, u32[]{:S(2)}, u32[]{:S(2)}) collective-permute-start(bf16[2,128,128]{2,1,0:T(8,128)(2,1)S(1)} %shard_map.50.refs_0_), channel_id=1, source_target_pairs={{0,24},{8,16},{16,8},{24,0},{1,25},{9,17},{17,9},{25,1},{2,26},{10... | collective-permute-start | bytes 196616 | tf_op jit(solution)/shard_map/ppermute | solution.py:493
  35.9 1.5 %collective-permute-start.7 = (bf16[2,128,128]{2,1,0:T(8,128)(2,1)S(1)}, bf16[2,128,128]{2,1,0:T(8,128)(2,1)S(1)}, u32[]{:S(2)}, u32[]{:S(2)}) collective-permute-start(bf16[2,128,128]{2,1,0:T(8,128)(2,1)S(1)} %shard_map.50.refs_0_), channel_id=1, source_target_pairs={{0,8},{8,0},{16,24},{24,16},{1,9},{9,1},{17,25},{25,17},{2,10},{10... | collective-permute-start | bytes 196616 | tf_op jit(solution)/shard_map/ppermute | solution.py:493
  37.3 0.5 %collective-permute-start.8 = (bf16[2,128,128]{2,1,0:T(8,128)(2,1)S(1)}, bf16[2,128,128]{2,1,0:T(8,128)(2,1)S(1)}, u32[]{:S(2)}, u32[]{:S(2)}) collective-permute-start(bf16[2,128,128]{2,1,0:T(8,128)(2,1)S(1)} %shard_map.50.refs_0_), channel_id=1, source_target_pairs={{0,16},{8,24},{16,0},{24,8},{1,17},{9,25},{17,1},{25,9},{2,18},{10... | collective-permute-start | bytes 196616 | tf_op jit(solution)/shard_map/ppermute | solution.py:493
  37.9 1.6 %shard_map.51.refs_0_ = bf16[8,36,2,1536]{3,2,1,0:T(2,128)(2,1)} custom-call(s32[1]{0:T(128)} %bitcast.slab_ref, bf16[8,188,2,1536]{3,2,1,0:T(2,128)(2,1)S(1)} %shard_map.48.held_ref.volt_ref, bf16[2,128,128]{2,1,0:T(8,128)(2,1)S(1)} %shard_map.50.refs_0_), custom_call_target="tpu_custom_call" | custom-call | tf_op jit(solution)/shard_map/pallas_call | solution.py:450
  39.5 0.2 collective-permute-done.6.refs_1_
  39.6 1.6 %shard_map.52.refs_0_ = bf16[8,36,2,1536]{3,2,1,0:T(2,128)(2,1)} custom-call(s32[1]{0:T(128)} %bitcast.slab_ref, bf16[8,188,2,1536]{3,2,1,0:T(2,128)(2,1)S(1)} %shard_map.48.held_ref.volt_ref, bf16[8,36,2,1536]{3,2,1,0:T(2,128)(2,1)} %shard_map.51.refs_0_, bf16[2,128,128]{2,1,0:T(8,128)(2,1)S(1)} %collective-permute-done.6.refs_1_), custom_call_target="tpu_custom_call", output_to_operand_aliasing={{}: (2, {})} | custom-call | tf_op jit(solution)/shard_map/pallas_call | solution.py:450
  41.3 0.0 collective-permute-done.7.refs_1_
  41.3 0.4 collective-permute-done.8.refs_2_
  41.6 2.5 %shard_map.53 = bf16[8,36,2,1536]{3,2,1,0:T(2,128)(2,1)} custom-call(s32[1]{0:T(128)} %bitcast.slab_ref, bf16[8,188,2,1536]{3,2,1,0:T(2,128)(2,1)S(1)} %shard_map.48.held_ref.volt_ref, bf16[8,36,2,1536]{3,2,1,0:T(2,128)(2,1)} %shard_map.52.refs_0_, bf16[2,128,128]{2,1,0:T(8,128)(2,1)S(1)} %collective-permute-done.7.refs_1_, ...), custom_call_target="tpu_custom_call", output_to_operand_aliasing={{}: (2, {})} | custom-call | tf_op jit(solution)/shard_map/pallas_call | solution.py:450
Async XLA Ops:
  6.8 11.2 %collective-permute-start.2 = (bf16[8,288,128]{2,1,0:T(8,128)(2,1)S(1)}, bf16[8,288,128]{2,1,0:T(8,128)(2,1)S(1)}, u32[]{:S(2)}, u32[]{:S(2)}) collective-permute-start(bf16[8,288,128]{2,1,0:T(8,128)(2,1)S(1)} %get-tuple-element.16), channel_id=1, source_target_pairs={{1,2},{3,4},{5,6},{2,1},{4,3},{6,5},{9,10},{11,12},{13,14},{10,9},... | collective-permute-start | bytes 1769480 | tf_op jit(solution)/shard_map/ppermute | solution.py:487
  8.9 3.0 %collective-permute-start = (bf16[4,288,128]{2,1,0:T(8,128)(2,1)S(1)}, bf16[4,288,128]{2,1,0:T(8,128)(2,1)S(1)}, u32[]{:S(2)}, u32[]{:S(2)}) collective-permute-start(bf16[4,288,128]{2,1,0:T(8,128)(2,1)S(1)} %get-tuple-element.14), channel_id=1, source_target_pairs={{0,1},{2,3},{4,5},{6,7},{1,0},{3,2},{5,4},{7,6},{8,9},{10,11},{12,... | collective-permute-start | bytes 884744 | tf_op jit(solution)/shard_map/ppermute | solution.py:488
  10.6 1.6 %collective-permute-start.1 = (bf16[4,288,128]{2,1,0:T(8,128)(2,1)S(1)}, bf16[4,288,128]{2,1,0:T(8,128)(2,1)S(1)}, u32[]{:S(2)}, u32[]{:S(2)}) collective-permute-start(bf16[4,288,128]{2,1,0:T(8,128)(2,1)S(1)} %get-tuple-element.15), channel_id=1, source_target_pairs={{0,1},{2,3},{4,5},{6,7},{1,0},{3,2},{5,4},{7,6},{8,9},{10,11},{12,... | collective-permute-start | bytes 884744 | tf_op jit(solution)/shard_map/ppermute | solution.py:488
  10.7 11.0 %copy-start = (f32[8,2,64,188]{3,2,1,0:T(8,128)S(1)}, f32[8,2,64,188]{3,2,1,0:T(8,128)}, u32[]{:S(2)}) copy-start(f32[8,2,64,188]{3,2,1,0:T(8,128)} %steer_ref.1) | copy-start | bytes 2310148
  10.7 11.0 %copy-start.2 = (s32[36]{0:T(128)S(1)}, s32[36]{0:T(128)}, u32[]{:S(2)}) copy-start(s32[36]{0:T(128)} %index_ref.1) | copy-start | bytes 436
  18.1 8.0 %collective-permute-start.3 = (bf16[2,288,128]{2,1,0:T(8,128)(2,1)S(1)}, bf16[2,288,128]{2,1,0:T(8,128)(2,1)S(1)}, u32[]{:S(2)}, u32[]{:S(2)}) collective-permute-start(bf16[2,288,128]{2,1,0:T(8,128)(2,1)S(1)} %get-tuple-element.18), channel_id=1, source_target_pairs={{0,8},{8,0},{16,24},{24,16},{1,9},{9,1},{17,25},{25,17},{2,10},{10... | collective-permute-start | bytes 442376 | tf_op jit(solution)/shard_map/ppermute | solution.py:493
  19.7 8.7 %collective-permute-start.4 = (bf16[2,288,128]{2,1,0:T(8,128)(2,1)S(1)}, bf16[2,288,128]{2,1,0:T(8,128)(2,1)S(1)}, u32[]{:S(2)}, u32[]{:S(2)}) collective-permute-start(bf16[2,288,128]{2,1,0:T(8,128)(2,1)S(1)} %get-tuple-element.19), channel_id=1, source_target_pairs={{0,16},{8,24},{16,0},{24,8},{1,17},{9,25},{17,1},{25,9},{2,18},{10... | collective-permute-start | bytes 442376 | tf_op jit(solution)/shard_map/ppermute | solution.py:493
  21.2 7.2 %collective-permute-start.5 = (bf16[2,288,128]{2,1,0:T(8,128)(2,1)S(1)}, bf16[2,288,128]{2,1,0:T(8,128)(2,1)S(1)}, u32[]{:S(2)}, u32[]{:S(2)}) collective-permute-start(bf16[2,288,128]{2,1,0:T(8,128)(2,1)S(1)} %get-tuple-element.20), channel_id=1, source_target_pairs={{0,24},{8,16},{16,8},{24,0},{1,25},{9,17},{17,9},{25,1},{2,26},{10... | collective-permute-start | bytes 442376 | tf_op jit(solution)/shard_map/ppermute | solution.py:493
  22.4 6.1 %copy-start.1 = (s32[64]{0:T(128)S(1)}, s32[64]{0:T(128)}, u32[]{:S(2)}) copy-start(s32[64]{0:T(128)} %flags_ref.1) | copy-start | bytes 772
  34.3 5.3 %collective-permute-start.6 = (bf16[2,128,128]{2,1,0:T(8,128)(2,1)S(1)}, bf16[2,128,128]{2,1,0:T(8,128)(2,1)S(1)}, u32[]{:S(2)}, u32[]{:S(2)}) collective-permute-start(bf16[2,128,128]{2,1,0:T(8,128)(2,1)S(1)} %shard_map.50.refs_0_), channel_id=1, source_target_pairs={{0,24},{8,16},{16,8},{24,0},{1,25},{9,17},{17,9},{25,1},{2,26},{10... | collective-permute-start | bytes 196616 | tf_op jit(solution)/shard_map/ppermute | solution.py:493
  35.9 5.4 %collective-permute-start.7 = (bf16[2,128,128]{2,1,0:T(8,128)(2,1)S(1)}, bf16[2,128,128]{2,1,0:T(8,128)(2,1)S(1)}, u32[]{:S(2)}, u32[]{:S(2)}) collective-permute-start(bf16[2,128,128]{2,1,0:T(8,128)(2,1)S(1)} %shard_map.50.refs_0_), channel_id=1, source_target_pairs={{0,8},{8,0},{16,24},{24,16},{1,9},{9,1},{17,25},{25,17},{2,10},{10... | collective-permute-start | bytes 196616 | tf_op jit(solution)/shard_map/ppermute | solution.py:493
  37.3 4.3 %collective-permute-start.8 = (bf16[2,128,128]{2,1,0:T(8,128)(2,1)S(1)}, bf16[2,128,128]{2,1,0:T(8,128)(2,1)S(1)}, u32[]{:S(2)}, u32[]{:S(2)}) collective-permute-start(bf16[2,128,128]{2,1,0:T(8,128)(2,1)S(1)} %shard_map.50.refs_0_), channel_id=1, source_target_pairs={{0,16},{8,24},{16,0},{24,8},{1,17},{9,25},{17,1},{25,9},{2,18},{10... | collective-permute-start | bytes 196616 | tf_op jit(solution)/shard_map/ppermute | solution.py:493
